TPU v7x, 32 devices: a whole 2x2x4 slice. The times are simulated.
32 devices in a mesh: gz: 2 (over y), xy: 16 (over z, x, core).
Axes of the slice: x: 2, y: 2, z: 4, core: 2. Of those that a mesh axis runs over, the one named last changes fastest.
Arguments:
- velocity_free: float32 [2, 16, 6, 512], P('gz', 'xy'), may hold values from -6 to 6
- inverse_mass: float32 [2, 16, 2, 512], P('gz', 'xy'), may hold values from 0.25 to 4
- jacobian: float32 [2, 16, 36, 2048], P('gz', 'xy'), may hold values from -1.75 to 1.75
- impulses: float32 [2, 16, 3, 2048], P('gz', 'xy'), may hold values from -6 to 6
- previous_impulses: float32 [2, 16, 3, 2048], P('gz', 'xy'), may hold values from -6 to 6
- compliance: float32 [2, 16, 2048], P('gz', 'xy'), may hold values from 0.05 to 0.5
- offset: float32 [2, 16, 2048], P('gz', 'xy'), may hold values from -6 to 6
- friction: float32 [2, 16, 2048], P('gz', 'xy'), may hold values from 0.2 to 0.8
- body_near: int32 [2, 16, 2048], P('gz', 'xy'), may hold values from 0 to 511
- body_far: int32 [2, 16, 2048], P('gz', 'xy'), may hold values from 0 to 1023
- block_counts: int32 [2, 16, 16], P('gz', 'xy'), may hold values from 0 to 128, as said below
- layer_send: int32 [2, 16, 128], P('gz', 'xy'), may hold values from 0 to 511
- side_send: int32 [2, 16, 2, 192], P('gz', 'xy'), may hold values from 0 to 639
Outputs:
- impulses_out: float32 [2, 16, 3, 2048], P('gz', 'xy')
- velocity_out: float32 [2, 16, 6, 512], P('gz', 'xy')
Inputs may be any that keep to these rules, and one draw needn't show every extreme that they name: `block_counts`: on each device the blocks that hold live contacts come first, every one of them but the last full; some device holds 2048 live contacts. `body_far`: entries of 512 or more name received rows: 512 + i is the row received as the i-th from the layer above, then 192 rows from the lower-side and 192 from the higher-side neighbour. `side_send`: entries of 512 or more name rows received from the layer above.
All inputs are finite; a program needn't handle non-finite values.
Results may differ from a plain program's by a relative error of at most 0.0003.
Values sent between devices are 32-bit elements; how exact they have to be, the bound alone decides.
No kernel may reach another device: no remote copies, remote signals or barrier semaphores. Data moves between devices by JAX's collectives and lax.ppermute only.
A program may use at most 64 MiB of HBM per device.

v0:
```python
import math

import jax
import jax.numpy as jnp
from jax import lax
from jax.experimental import pallas as pl
from jax.experimental.pallas import tpu as pltpu
from jax.sharding import PartitionSpec as P

ITERS = 2
EPSILON = 1e-06
THETA_START = 0.3
LANES = 128
WIDE = 256
F32 = jnp.float32
BF16 = jnp.bfloat16
I32 = jnp.int32


def theta_after(theta_value):
    return 0.5 * (
        -theta_value * theta_value + theta_value * math.sqrt(theta_value * theta_value + 4.0)
    )


def momentum_factors(iteration_count):
    thetas = [THETA_START]
    for iteration in range(iteration_count):
        thetas.append(theta_after(thetas[-1]))
    return [
        thetas[position]
        * (1.0 - thetas[position])
        / (thetas[position] * thetas[position] + thetas[position + 1])
        for position in range(iteration_count)
    ]


def pair_swaps(count, parity):
    target = list(range(count))
    for cell in range(parity, count - 1, 2):
        target[cell], target[cell + 1] = cell + 1, cell
    return list(enumerate(target))


class Sizes:
    def __init__(self, contacts, own, layer, side, slots, cells):
        self.contacts, self.own, self.layer, self.side = contacts, own, layer, side
        self.slots, self.cells = slots, cells
        self.blocks = contacts // LANES
        self.section = own + layer
        self.total = self.section + 2 * side
        self.window = -(-side // LANES) * LANES
        self.margin = self.window - side
        self.own_groups = own // LANES
        self.layer_groups = layer // LANES
        self.section_groups = self.section // LANES
        self.total_groups = self.total // LANES
        self.window_groups = self.window // LANES
        self.contact_rows = 48 * self.blocks
        self.layer_at = 2 * self.own_groups
        self.side_at = self.layer_at + self.layer_groups
        self.sphere_rows = 8 * (self.side_at + self.window_groups)
        self.sent = own + self.window
        assert contacts % LANES == own % LANES == layer % LANES == 2 * side % LANES == 0
        assert 8 >= 6 and self.blocks % 8 == 0


SPARE = [half * 8 + 16 * row + 6 + at for row in range(3) for half in range(2) for at in range(2)]
NEAR, FAR, ALIVE, FRICTION, SOFTNESS, OFFSET, CURRENT, GUESS = 0, 1, 2, 3, 4, 5, 6, 9


class Contacts:
    def __init__(self, ref, sizes):
        self.ref, self.sizes = ref, sizes

    def near_part(self, block, row):
        return self.ref[pl.ds(block * 48 + row * 16, 8), :]

    def far_part(self, block, row):
        return self.ref[pl.ds(block * 48 + row * 16 + 8, 8), :]

    def tile(self, which):
        return self.ref[pl.ds(SPARE[which], self.sizes.blocks, stride=48), :]


class Spheres:
    def __init__(self, ref, sizes):
        self.ref, self.sizes = ref, sizes

    def misc(self, group):
        return self.ref[pl.ds(group * 8, 8), :]

    def free(self, group):
        return self.misc(group)

    def weight(self, group):
        return self.misc(self.sizes.own_groups + group)

    def layer_list(self, group):
        return self.misc(self.sizes.layer_at + group)[0:1].astype(I32)

    def side_list(self, which, group):
        return self.misc(self.sizes.side_at + group)[which : which + 1].astype(I32)


def gather(groups, index):
    lane = jnp.broadcast_to(index & (LANES - 1), (8, LANES))
    which = jnp.broadcast_to(index >> 7, (8, LANES))
    out = jnp.zeros((8, LANES), groups[0].dtype)
    for number, group in enumerate(groups):
        picked = jnp.take_along_axis(group, lane, axis=1, mode="promise_in_bounds")
        out = jnp.where(which == number, picked, out)
    return out


def look_up(lists, index):
    groups = [jnp.broadcast_to(row, (8, LANES)) for row in lists]
    pieces = [gather(groups, index[at : at + 8]) for at in range(0, index.shape[0], 8)]
    return jnp.concatenate(pieces, axis=0) - 1


def spread_out(values, index, groups, at, spread_ref, hot_ref):
    lanes = pl.ds(at * LANES, LANES)
    upper = values.astype(BF16).astype(F32)
    both = jnp.concatenate([upper, values - upper], axis=0).astype(BF16)
    which = jnp.broadcast_to((index >> 7).astype(F32), (16, LANES)).astype(BF16)
    low = jnp.broadcast_to((index & (LANES - 1)).astype(F32), (16, LANES)).astype(BF16)
    for number in range(groups):
        part = jnp.where(which == jnp.asarray(number, BF16), both, jnp.zeros((16, LANES), BF16))
        spread_ref[pl.ds(number * 16, 16), lanes] = part
    row_number = lax.broadcasted_iota(I32, (LANES, LANES), 0).astype(F32).astype(BF16)
    for part in range(LANES // 16):
        rows = slice(part * 16, part * 16 + 16)
        hot = jnp.where(row_number[rows] == low, jnp.ones((16, LANES), BF16), jnp.zeros((16, LANES), BF16))
        hot_ref[pl.ds(part * 16, 16), lanes] = hot


def summed(groups, spread_ref, hot_ref):
    out = lax.dot_general(
        spread_ref[...], hot_ref[...], (((1,), (1,)), ((), ())), preferred_element_type=F32
    )
    return [out[g * 16 : g * 16 + 8] + out[g * 16 + 8 : g * 16 + 16] for g in range(groups)]


class Maps:
    def __init__(self, spheres, sizes, flags):
        self.spheres, self.sizes, self.flags = spheres, sizes, flags

    def upper(self, slot):
        above = self.spheres[(slot + 1) % self.sizes.slots]
        return [above.layer_list(group) for group in range(self.sizes.layer_groups)]

    def side(self, slot, which):
        picks = []
        for group in range(self.sizes.window_groups):
            to_lower = self.spheres[slot].side_list(0, group)
            to_higher = self.spheres[slot].side_list(1, group)
            higher = (self.flags[0] == 0) == (which == 1)
            picks.append(jnp.where(higher, to_higher, to_lower))
        return picks

    def window_index(self, far, which):
        sizes = self.sizes
        higher = (self.flags[0] == 0) == (which == 1)
        return far - jnp.where(higher, sizes.section, sizes.section + sizes.side - sizes.margin)

    def resolved(self, slot, which, far):
        sizes = self.sizes
        if which == 0:
            row = jnp.where(far < sizes.section, far, -1)
        else:
            row = look_up(self.side(slot, which), self.window_index(far, which))
            row = jnp.where(self.flags[which] != 0, row, -1)
        above = look_up(self.upper(slot), row - sizes.own) + sizes.own
        above = jnp.where(self.flags[3 + slot] != 0, above, -1)
        return jnp.where(row < sizes.own, row, above)


def collected(sets, values, maps, sizes, work):
    slots, own_groups = sizes.slots, sizes.own_groups
    spans = 2 * own_groups if slots > 1 else own_groups
    result = [[None] * own_groups for _ in range(slots)]

    def add(slot, group, value):
        held = result[slot][group]
        result[slot][group] = value if held is None else held + value

    for slot in range(slots):
        near_ref, near_hot, far_ref, far_hot = work[(slot % 2) * 4 : (slot % 2) * 4 + 4]
        for which in range(3):
            pack, value = sets[slot][which], values[slot][which]
            far = maps.resolved(slot, which, pack.tile(FAR).astype(I32))
            near = pack.tile(NEAR).astype(I32) if which == 0 else None
            for block in range(sizes.blocks):
                far_value = near_value = None
                for row in range(3):
                    line = value[row][block : block + 1]
                    term = pack.far_part(block, row) * line
                    far_value = term if far_value is None else far_value + term
                    if which == 0:
                        term = pack.near_part(block, row) * line
                        near_value = term if near_value is None else near_value + term
                at = which * sizes.blocks + block
                spread_out(far_value, far[block : block + 1], spans, at, far_ref, far_hot)
                if which == 0:
                    spread_out(near_value, near[block : block + 1], own_groups, block, near_ref, near_hot)
        for group, value in enumerate(summed(own_groups, near_ref, near_hot)):
            add(slot, group, value)
        for group, value in enumerate(summed(spans, far_ref, far_hot)):
            add((slot + group // own_groups) % slots, group % own_groups, value)
    return result


def rows_of(pack, own, table, index, sizes, rows_ref):
    near = pack.tile(NEAR).astype(I32)
    for block in range(sizes.blocks):
        near_value = gather(own, near[block : block + 1])
        far_value = gather(table, index[block : block + 1])
        for row in range(3):
            terms = pack.near_part(block, row) * near_value + pack.far_part(block, row) * far_value
            rows_ref[row, pl.ds(block, 1), :] = jnp.sum(terms, axis=0, keepdims=True)


def cone_project(impulse_value, cone_friction):
    normal, first, second = impulse_value
    slide_norm = jnp.sqrt(first * first + second * second)
    inside_cone = slide_norm <= cone_friction * normal
    polar_cone = cone_friction * slide_norm <= -normal
    outside_both = jnp.logical_not(jnp.logical_or(inside_cone, polar_cone))
    onto_normal = (cone_friction * slide_norm + normal) / (cone_friction * cone_friction + 1.0)
    tangent_scale = cone_friction * onto_normal / jnp.where(outside_both, slide_norm, 1.0)
    scale = jnp.where(inside_cone, 1.0, jnp.where(polar_cone, 0.0, tangent_scale))
    new_normal = jnp.where(inside_cone, normal, jnp.where(polar_cone, 0.0, onto_normal))
    return [new_normal, scale * first, scale * second]


def call(body, out_shape, operands, scratch=(), smem=1):
    specs = [pl.BlockSpec(memory_space=pltpu.SMEM)] * smem
    specs += [pl.BlockSpec(memory_space=pltpu.VMEM)] * (len(operands) - smem)
    return pl.pallas_call(
        body,
        out_shape=[jax.ShapeDtypeStruct(shape, F32) for shape in out_shape],
        in_specs=specs,
        out_specs=[pl.BlockSpec(memory_space=pltpu.VMEM)] * len(out_shape),
        scratch_shapes=list(scratch),
        compiler_params=pltpu.CompilerParams(vmem_limit_bytes=40 * 1024 * 1024),
    )(*operands)


def on_device(
    velocity_free,
    inverse_mass,
    jacobian,
    impulses,
    previous_impulses,
    compliance,
    offset,
    friction,
    body_near,
    body_far,
    block_counts,
    layer_send,
    side_send,
):
    slots, cells = lax.axis_size("gz"), lax.axis_size("xy")
    layer_at, cell_at = lax.axis_index("gz"), lax.axis_index("xy")
    sizes = Sizes(
        jacobian.shape[3], velocity_free.shape[3], layer_send.shape[2], side_send.shape[3], slots, cells
    )
    blocks, window = sizes.blocks, sizes.window
    factors = momentum_factors(ITERS)

    odd = cell_at % 2
    lower, higher = cell_at > 0, cell_at < cells - 1
    flags = jnp.stack(
        [odd, jnp.where(odd == 0, higher, lower), jnp.where(odd == 0, lower, higher)]
        + [(layer_at + slot) % slots != slots - 1 for slot in range(slots)]
    ).astype(I32)

    def tiles(array):
        return array.reshape(-1, blocks, LANES)

    def pack_body(
        counts, free_ref, mass_ref, jac_ref, imp_ref, prev_ref, soft_ref, off_ref, fric_ref, near_ref,
        far_ref, layer_ref, side_ref, out_ref, sphere_ref,
    ):
        lane = lax.broadcasted_iota(I32, (1, LANES), 1)
        for block in range(blocks):
            lanes = pl.ds(block * LANES, LANES)
            one = slice(block, block + 1)
            alive = jnp.where(lane < counts[block], 1.0, 0.0)
            spare = [
                near_ref[0, one].astype(F32), far_ref[0, one].astype(F32), alive,
                fric_ref[0, one], soft_ref[0, one], off_ref[0, one],
            ]
            current = [alive * imp_ref[row, one] for row in range(3)]
            earlier = [alive * prev_ref[row, one] for row in range(3)]
            spare += current
            spare += [alive * (c + factors[0] * (c - e)) for c, e in zip(current, earlier)]
            for part in range(6):
                rows = jac_ref[pl.ds(part * 6, 6), lanes]
                both = jnp.concatenate([rows, spare[2 * part], spare[2 * part + 1]], axis=0)
                out_ref[pl.ds(block * 48 + part * 8, 8), :] = both

        gap = jnp.zeros((2, LANES), F32)

        def misc(group, value):
            sphere_ref[pl.ds(group * 8, 8), :] = value

        for group in range(sizes.own_groups):
            lanes = pl.ds(group * LANES, LANES)
            misc(group, jnp.concatenate([free_ref[:, lanes], gap], axis=0))
            mass = mass_ref[:, lanes]
            linear = jnp.broadcast_to(mass[0:1], (3, LANES))
            angular = jnp.broadcast_to(mass[1:2], (3, LANES))
            misc(sizes.own_groups + group, jnp.concatenate([linear, angular, gap], axis=0))
        for group in range(sizes.layer_groups):
            lanes = pl.ds(group * LANES, LANES)
            rows = jnp.broadcast_to(layer_ref[:, lanes] + 1, (8, LANES))
            misc(sizes.layer_at + group, rows.astype(F32))
        for group in range(sizes.window_groups):
            lanes = pl.ds(group * LANES, LANES)
            rows = jnp.concatenate([side_ref[:, lanes] + 1] * 4, axis=0)
            misc(sizes.side_at + group, rows.astype(F32))

    lists = side_send[0, 0]
    side_lists = jnp.stack(
        [
            jnp.pad(lists[0], (sizes.margin, 0), constant_values=-1),
            jnp.pad(lists[1], (0, sizes.margin), constant_values=-1),
        ]
    )
    own_contacts, own_spheres = call(
        pack_body,
        [(sizes.contact_rows, LANES), (sizes.sphere_rows, LANES)],
        [
            block_counts[0, 0],
            velocity_free[0, 0],
            inverse_mass[0, 0],
            jacobian[0, 0],
            tiles(impulses[0, 0]),
            tiles(previous_impulses[0, 0]),
            tiles(compliance[0, 0]),
            tiles(offset[0, 0]),
            tiles(friction[0, 0]),
            tiles(body_near[0, 0]),
            tiles(body_far[0, 0]),
            layer_send[0],
            side_lists,
        ],
    )
    to_first, to_second = pair_swaps(cells, 0), pair_swaps(cells, 1)

    def swap(first, second):
        return lax.ppermute(first, "xy", to_first), lax.ppermute(second, "xy", to_second)

    def turned(array, step):
        return lax.ppermute(array, "gz", [((i + step) % slots, i) for i in range(slots)])

    sphere_arrays = [own_spheres] + [turned(own_spheres, step) for step in range(1, slots)]
    contact_arrays = []
    for slot in range(slots):
        held = own_contacts if slot == 0 else turned(own_contacts, slot)
        contact_arrays += [held, *swap(held, held)]
    inputs = [*contact_arrays, *sphere_arrays]

    def views(refs):
        sets = [[Contacts(refs[3 * s + w], sizes) for w in range(3)] for s in range(slots)]
        spheres = [Spheres(ref, sizes) for ref in refs[3 * slots : 4 * slots]]
        return sets, spheres, refs[4 * slots :]

    def chosen(*arrays):
        return [array for array in arrays if array is not None]

    state_shape = (slots, 3, 3, blocks, LANES)
    section_shape, sent_shape = (slots, 8, sizes.section), (slots, 8, sizes.sent)
    spans = (2 if slots > 1 else 1) * sizes.own_groups
    work = [
        pltpu.VMEM((sizes.own_groups * 16, sizes.contacts), BF16),
        pltpu.VMEM((LANES, sizes.contacts), BF16),
        pltpu.VMEM((spans * 16, 3 * sizes.contacts), BF16),
        pltpu.VMEM((LANES, 3 * sizes.contacts), BF16),
    ] * 2

    def put_velocities(sums, spheres, maps, flags, section_ref, first_ref, second_ref):
        velocity = [
            [spheres[s].free(g) + spheres[s].weight(g) * sums[s][g] for g in range(sizes.own_groups)]
            for s in range(slots)
        ]
        for slot in range(slots):
            table = list(velocity[slot])
            for rows in maps.upper(slot):
                upper = gather(velocity[(slot + 1) % slots], rows - 1)
                table.append(jnp.where(flags[3 + slot] != 0, upper, 0.0))
            for group, value in enumerate(table):
                section_ref[slot, :, pl.ds(group * LANES, LANES)] = value
            for which, sent_ref in ((1, first_ref), (2, second_ref)):
                for group, value in enumerate(velocity[slot]):
                    sent_ref[slot, :, pl.ds(group * LANES, LANES)] = value
                for group, rows in enumerate(maps.side(slot, which)):
                    lanes = pl.ds(sizes.own + group * LANES, LANES)
                    sent_ref[slot, :, lanes] = gather(table, rows - 1)

    def first_velocities():
        def body(flags, *refs):
            sets, spheres, refs = views(refs)
            section_ref, first_ref, second_ref, *scratch = refs
            maps = Maps(spheres, sizes, flags)
            values = [[[c.tile(GUESS + row) for row in range(3)] for c in row_sets] for row_sets in sets]
            sums = collected(sets, values, maps, sizes, scratch)
            put_velocities(sums, spheres, maps, flags, section_ref, first_ref, second_ref)

        return call(body, [section_shape, sent_shape, sent_shape], [flags, *inputs], work)

    def gradients(section, sent, got, state):
        def body(flags, section_ref, sent_first, sent_second, got_first, got_second, *refs):
            sets, spheres, refs = views(refs)
            if state is None:
                state_ref = None
            else:
                state_ref, *refs = refs
            grad_ref, parts_ref, rows_ref, *scratch = refs
            maps = Maps(spheres, sizes, flags)
            even = flags[0] == 0
            norm = soft = jnp.zeros((blocks, LANES), F32)
            lane = lax.broadcasted_iota(I32, (8, LANES), 1)
            edge = sizes.side % LANES

            def groups(ref, slot, start, count):
                return [ref[slot, :, pl.ds(start + g * LANES, LANES)] for g in range(count)]

            values = []
            for slot in range(slots):
                table = groups(section_ref, slot, 0, sizes.section_groups)
                first = groups(got_first, slot, sizes.own, sizes.window_groups)
                second = groups(got_second, slot, sizes.own, sizes.window_groups)
                first = [jnp.where(flags[1] != 0, value, 0.0) for value in first]
                second = [jnp.where(flags[2] != 0, value, 0.0) for value in second]
                low = [jnp.where(even, b, a) for a, b in zip(first, second)]
                high = [jnp.where(even, a, b) for a, b in zip(first, second)]
                if edge:
                    table += low[:-1] + [jnp.where(lane < edge, low[-1], high[0])] + high[1:]
                else:
                    table += low + high
                slot_values = []
                for which, pack in enumerate(sets[slot]):
                    far = pack.tile(FAR).astype(I32)
                    if which == 0:
                        rows_of(pack, table[: sizes.own_groups], table, far, sizes, rows_ref.at[slot, which])
                    else:
                        sent_ref = (sent_first, sent_second)[which - 1]
                        got_ref = (got_first, got_second)[which - 1]
                        own = groups(got_ref, slot, 0, sizes.own_groups)
                        listed = groups(sent_ref, slot, sizes.own, sizes.window_groups)
                        index = maps.window_index(far, which)
                        rows_of(pack, own, listed, index, sizes, rows_ref.at[slot, which])
                    alive, softness = pack.tile(ALIVE), pack.tile(SOFTNESS)
                    grad = []
                    for row in range(3):
                        guess = pack.tile(GUESS + row) if state_ref is None else state_ref[slot, which, row]
                        value = rows_ref[slot, which, row] + softness * guess
                        if row == 0:
                            value = value + pack.tile(OFFSET)
                        value = alive * value
                        grad_ref[slot, which, row] = value
                        grad.append(value)
                        if which == 0:
                            norm = norm + value * value
                            soft = soft + softness * value * value
                    slot_values.append(grad)
                values.append(slot_values)
            sums = collected(sets, values, maps, sizes, scratch)
            curve = jnp.sum(soft, axis=0, keepdims=True)
            norm = jnp.sum(norm, axis=0, keepdims=True)
            total = jnp.zeros((8, LANES), F32)
            for slot in range(slots):
                for group in range(sizes.own_groups):
                    value = sums[slot][group]
                    total = total + spheres[slot].weight(group) * value * value
            curve = curve + jnp.sum(total, axis=0, keepdims=True)
            both = jnp.concatenate([norm, curve, jnp.zeros((6, LANES), F32)], axis=0)
            for cell in range(cells):
                parts_ref[cell] = both

        return call(
            body,
            [state_shape, (cells, 8, LANES)],
            chosen(flags, section, *sent, *got, *inputs, state),
            [pltpu.VMEM(state_shape, F32), *work],
        )

    def updates(parts, grad, state, earlier, factor):
        last = factor is None

        def body(flags, part_ref, grad_ref, *refs):
            sets, spheres, refs = views(refs)
            if state is not None:
                state_ref, earlier_ref, *refs = refs
            if last:
                result_ref, velocity_ref, *scratch = refs
            else:
                result_ref, guess_ref, section_ref, first_ref, second_ref, *scratch = refs
            maps = Maps(spheres, sizes, flags)
            total = part_ref[0]
            for cell in range(1, cells):
                total = total + part_ref[cell]
            sums = jnp.sum(total, axis=1, keepdims=True)
            step = sums[0:1] / (sums[1:2] + EPSILON)
            values = []
            for slot in range(slots):
                slot_values = []
                for which, pack in enumerate(sets[slot]):
                    alive = pack.tile(ALIVE)
                    moved, before = [], []
                    for row in range(3):
                        if state is None:
                            guess, old = pack.tile(GUESS + row), pack.tile(CURRENT + row)
                        else:
                            guess, old = state_ref[slot, which, row], earlier_ref[slot, which, row]
                        before.append(old)
                        moved.append(guess - step * grad_ref[slot, which, row])
                    value = [alive * v for v in cone_project(moved, pack.tile(FRICTION))]
                    if not last:
                        guess = [alive * (v + factor * (v - b)) for v, b in zip(value, before)]
                        for row in range(3):
                            result_ref[slot, which, row] = value[row]
                            guess_ref[slot, which, row] = guess[row]
                        value = guess
                    elif slot == which == 0:
                        for row in range(3):
                            for block in range(blocks):
                                lanes = pl.ds(block * LANES, LANES)
                                result_ref[pl.ds(row, 1), lanes] = value[row][block : block + 1]
                    slot_values.append(value)
                values.append(slot_values)
            sums = collected(sets, values, maps, sizes, scratch)
            if last:
                for group in range(sizes.own_groups):
                    value = spheres[0].free(group) + spheres[0].weight(group) * sums[0][group]
                    velocity_ref[:, pl.ds(group * LANES, LANES)] = value[:6]
            else:
                put_velocities(sums, spheres, maps, flags, section_ref, first_ref, second_ref)

        if last:
            shapes = [(3, sizes.contacts), (6, sizes.own)]
        else:
            shapes = [state_shape, state_shape, section_shape, sent_shape, sent_shape]
        return call(body, shapes, chosen(flags, parts, grad, *inputs, state, earlier), work)

    state = earlier = None
    section, *sent = first_velocities()
    for iteration in range(ITERS):
        grad, parts = gradients(section, sent, swap(*sent), state)
        parts = lax.all_to_all(parts, "xy", 0, 0, tiled=True)
        if iteration + 1 < ITERS:
            earlier, state, section, *sent = updates(parts, grad, state, earlier, factors[iteration + 1])
    result, velocity = updates(parts, grad, state, earlier, None)
    return (result[None, None], velocity[None, None])


def solution(mesh):
    placed = (
        P("gz", "xy", None, None),
        P("gz", "xy", None, None),
        P("gz", "xy", None, None),
        P("gz", "xy", None, None),
        P("gz", "xy", None, None),
        P("gz", "xy", None),
        P("gz", "xy", None),
        P("gz", "xy", None),
        P("gz", "xy", None),
        P("gz", "xy", None),
        P("gz", "xy", None),
        P("gz", "xy", None),
        P("gz", "xy", None, None),
    )
    return jax.shard_map(
        on_device,
        mesh=mesh,
        in_specs=placed,
        out_specs=(P("gz", "xy", None, None), P("gz", "xy", None, None)),
        check_vma=False,
    )
```

profile of v0, /device:TPU:1, one launch (start us, length us, event | category | flops | bytes accessed | tf_op | source)
XLA Modules:
  0.0 81.9 jit_solution(15682446919243637289)
XLA Ops:
  0.6 0.0 copy-start.10
  0.6 0.8 fusion
  1.4 0.1 pad.8
  1.5 0.0 copy-done.10
  1.5 0.0 copy-start.1
  1.5 0.0 copy-start.2
  1.5 0.0 copy-start.3
  1.5 0.0 copy-start.4
  1.5 0.0 copy-start.5
  1.5 0.0 copy-start.6
  1.6 1.1 %copy.21 = f32[1,1,36,2048]{3,2,1,0:T(8,128)S(1)} copy(f32[1,1,36,2048]{3,1,2,0:T(1,128)} %param.15) | data formatting | bytes 589824
  2.6 0.0 copy-start
  2.7 0.0 copy-start.7
  2.7 0.0 copy-start.8
  2.7 0.0 copy-start.9
  2.7 0.0 copy-done.1
  2.7 0.0 copy-done.2
  2.7 0.0 copy-done.3
  2.7 0.0 copy-done.4
  2.7 0.0 copy-done.5
  2.8 0.0 copy-done.6
  2.8 0.6 copy-done
  3.4 0.0 copy-done.7
  3.4 0.0 copy-done.8
  3.4 0.0 copy-done.9
  3.4 0.7 shard_map.140
  4.1 2.1 %collective-permute-start.2 = (f32[768,128]{1,0:T(8,128)S(1)}, f32[768,128]{1,0:T(8,128)S(1)}, u32[]{:S(2)}, u32[]{:S(2)}) collective-permute-start(f32[768,128]{1,0:T(8,128)S(1)} %get-tuple-element.18.refs_0_), channel_id=1, source_target_pairs={{16,0},{0,16},{17,1},{1,17},{18,2},{2,18},{19,3},{3,19},{20,4},{4,... | collective-permute-start | bytes 1179656 | tf_op jit(solution)/shard_map/ppermute | solution.py:358
  6.2 3.9 %collective-permute-start.1 = (f32[768,128]{1,0:T(8,128)S(1)}, f32[768,128]{1,0:T(8,128)S(1)}, u32[]{:S(2)}, u32[]{:S(2)}) collective-permute-start(f32[768,128]{1,0:T(8,128)S(1)} %get-tuple-element.18.refs_0_), channel_id=1, source_target_pairs={{0,0},{1,2},{2,1},{3,4},{4,3},{5,6},{6,5},{7,8},{8,7},{9,10},{10,9... | collective-permute-start | bytes 1179656 | tf_op jit(solution)/shard_map/ppermute | solution.py:355
  10.2 0.1 collective-permute-start
  10.2 4.8 %collective-permute-done.2.refs_3_ = f32[768,128]{1,0:T(8,128)S(1)} collective-permute-done((f32[768,128]{1,0:T(8,128)S(1)}, f32[768,128]{1,0:T(8,128)S(1)}, u32[]{:S(2)}, u32[]{:S(2)}) %collective-permute-start.2) | collective-permute-done | bytes 393248 | tf_op jit(solution)/shard_map/ppermute | solution.py:358
  15.0 4.4 %collective-permute-start.4 = (f32[768,128]{1,0:T(8,128)S(1)}, f32[768,128]{1,0:T(8,128)S(1)}, u32[]{:S(2)}, u32[]{:S(2)}) collective-permute-start(f32[768,128]{1,0:T(8,128)S(1)} %collective-permute-done.2.refs_3_), channel_id=1, source_target_pairs={{0,0},{1,2},{2,1},{3,4},{4,3},{5,6},{6,5},{7,8},{8,7},{9,10},{10,9... | collective-permute-start | bytes 1179656 | tf_op jit(solution)/shard_map/ppermute | solution.py:355
  19.5 0.1 collective-permute-start.3
  19.6 1.3 %collective-permute-start.5 = (f32[88,128]{1,0:T(8,128)S(1)}, f32[88,128]{1,0:T(8,128)S(1)}, u32[]{:S(2)}, u32[]{:S(2)}) collective-permute-start(f32[88,128]{1,0:T(8,128)S(1)} %get-tuple-element.19.refs_6_), channel_id=1, source_target_pairs={{16,0},{0,16},{17,1},{1,17},{18,2},{2,18},{19,3},{3,19},{20,4},{4,... | collective-permute-start | bytes 135176 | tf_op jit(solution)/shard_map/ppermute | solution.py:358
  20.9 0.1 stack.48.flags
  21.0 1.6 %collective-permute-done.5.refs_7_ = f32[88,128]{1,0:T(8,128)S(1)} collective-permute-done((f32[88,128]{1,0:T(8,128)S(1)}, f32[88,128]{1,0:T(8,128)S(1)}, u32[]{:S(2)}, u32[]{:S(2)}) %collective-permute-start.5) | collective-permute-done | bytes 45088 | tf_op jit(solution)/shard_map/ppermute | solution.py:358
  22.5 0.0 collective-permute-done.1.refs_2_
  22.5 0.0 collective-permute-done.refs_1_
  22.5 5.9 %collective-permute-done.4.refs_5_ = f32[768,128]{1,0:T(8,128)S(1)} collective-permute-done((f32[768,128]{1,0:T(8,128)S(1)}, f32[768,128]{1,0:T(8,128)S(1)}, u32[]{:S(2)}, u32[]{:S(2)}) %collective-permute-start.4) | collective-permute-done | bytes 393248 | tf_op jit(solution)/shard_map/ppermute | solution.py:355
  28.4 0.0 collective-permute-done.3.refs_4_
  28.4 3.4 %shard_map.141 = (f32[2,8,640]{2,1,0:T(8,128)S(1)}, f32[2,8,768]{2,1,0:T(8,128)S(1)}, f32[2,8,768]{2,1,0:T(8,128)S(1)}) custom-call(s32[5]{0:T(128)S(1)} %stack.48.flags, f32[768,128]{1,0:T(8,128)S(1)} %get-tuple-element.18.refs_0_, f32[768,128]{1,0:T(8,128)S(1)} %collective-permute-done.refs_1_, f32[768,128]{1,0:T(8,128)S(1)} %collective-permute-done.1.refs_2_, ...), custom_call_target="tpu_custom_call" | custom-call | tf_op jit(solution)/shard_map/pallas_call | solution.py:240
  31.8 0.1 collective-permute-start.6
  31.9 4.4 %collective-permute-start.7 = (f32[2,8,768]{2,1,0:T(8,128)S(1)}, f32[2,8,768]{2,1,0:T(8,128)S(1)}, u32[]{:S(2)}, u32[]{:S(2)}) collective-permute-start(f32[2,8,768]{2,1,0:T(8,128)S(1)} %get-tuple-element.22.sent_second), channel_id=1, source_target_pairs={{0,0},{1,2},{2,1},{3,4},{4,3},{5,6},{6,5},{7,8},{8,7},{9,10},{10,9... | collective-permute-start | bytes 147464 | tf_op jit(solution)/shard_map/ppermute | solution.py:355
  36.3 0.0 collective-permute-done.6.got_first
  36.3 1.7 %collective-permute-done.7.got_second = f32[2,8,768]{2,1,0:T(8,128)S(1)} collective-permute-done((f32[2,8,768]{2,1,0:T(8,128)S(1)}, f32[2,8,768]{2,1,0:T(8,128)S(1)}, u32[]{:S(2)}, u32[]{:S(2)}) %collective-permute-start.7) | collective-permute-done | bytes 49184 | tf_op jit(solution)/shard_map/ppermute | solution.py:355
  38.1 4.2 %shard_map.142 = (f32[2,3,3,16,128]{4,3,2,1,0:T(8,128)S(1)}, f32[16,8,128]{2,1,0:T(8,128)S(1)}) custom-call(s32[5]{0:T(128)S(1)} %stack.48.flags, f32[2,8,640]{2,1,0:T(8,128)S(1)} %get-tuple-element.20.section_ref, f32[2,8,768]{2,1,0:T(8,128)S(1)} %get-tuple-element.21.sent_first, f32[2,8,768]{2,1,0:T(8,128)S(1)} %get-tuple-element.22.sent_second, ...), custom_call_target="tpu_custom_call" | custom-call | tf_op jit(solution)/shard_map/pallas_call | solution.py:240
  42.3 12.3 %all_to_all.10.part_ref = f32[16,8,128]{2,1,0:T(8,128)S(1)} all-to-all(f32[16,8,128]{2,1,0:T(8,128)S(1)} %get-tuple-element.23), channel_id=1, replica_groups=mesh['gz'=2,'xy'=16] {'xy'}, dimensions={0} | all-to-all | bytes 131072 | tf_op jit(solution)/shard_map/all_to_all | solution.py:554
  54.5 3.6 %shard_map.143 = (f32[2,3,3,16,128]{4,3,2,1,0:T(8,128)S(1)}, f32[2,3,3,16,128]{4,3,2,1,0:T(8,128)S(1)}, f32[2,8,640]{2,1,0:T(8,128)S(1)}, f32[2,8,768]{2,1,0:T(8,128)S(1)}, f32[2,8,768]{2,1,0:T(8,128)S(1)}) custom-call(s32[5]{0:T(128)S(1)} %stack.48.flags, f32[16,8,128]{2,1,0:T(8,128)S(1)} %all_to_all.10.part_ref, ...), custom_call_target="tpu_custom_call" | custom-call | tf_op jit(solution)/shard_map/pallas_call | solution.py:240
  58.1 1.0 %collective-permute-start.8 = (f32[2,8,768]{2,1,0:T(8,128)S(1)}, f32[2,8,768]{2,1,0:T(8,128)S(1)}, u32[]{:S(2)}, u32[]{:S(2)}) collective-permute-start(f32[2,8,768]{2,1,0:T(8,128)S(1)} %get-tuple-element.26.sent_first), channel_id=1, source_target_pairs={{0,1},{1,0},{2,3},{3,2},{4,5},{5,4},{6,7},{7,6},{8,9},{9,8},{10,11... | collective-permute-start | bytes 147464 | tf_op jit(solution)/shard_map/ppermute | solution.py:355
  59.1 1.9 %collective-permute-start.9 = (f32[2,8,768]{2,1,0:T(8,128)S(1)}, f32[2,8,768]{2,1,0:T(8,128)S(1)}, u32[]{:S(2)}, u32[]{:S(2)}) collective-permute-start(f32[2,8,768]{2,1,0:T(8,128)S(1)} %get-tuple-element.27.sent_second), channel_id=1, source_target_pairs={{0,0},{1,2},{2,1},{3,4},{4,3},{5,6},{6,5},{7,8},{8,7},{9,10},{10,9... | collective-permute-start | bytes 147464 | tf_op jit(solution)/shard_map/ppermute | solution.py:355
  61.0 0.0 collective-permute-done.8.got_first
  61.0 3.5 %collective-permute-done.9.got_second = f32[2,8,768]{2,1,0:T(8,128)S(1)} collective-permute-done((f32[2,8,768]{2,1,0:T(8,128)S(1)}, f32[2,8,768]{2,1,0:T(8,128)S(1)}, u32[]{:S(2)}, u32[]{:S(2)}) %collective-permute-start.9) | collective-permute-done | bytes 49184 | tf_op jit(solution)/shard_map/ppermute | solution.py:355
  64.5 4.2 %shard_map.144 = (f32[2,3,3,16,128]{4,3,2,1,0:T(8,128)S(1)}, f32[16,8,128]{2,1,0:T(8,128)S(1)}) custom-call(s32[5]{0:T(128)S(1)} %stack.48.flags, f32[2,8,640]{2,1,0:T(8,128)S(1)} %get-tuple-element.25.section_ref, f32[2,8,768]{2,1,0:T(8,128)S(1)} %get-tuple-element.26.sent_first, f32[2,8,768]{2,1,0:T(8,128)S(1)} %get-tuple-element.27.sent_second, ...), custom_call_target="tpu_custom_call" | custom-call | tf_op jit(solution)/shard_map/pallas_call | solution.py:240
  68.7 8.8 %all_to_all.11.part_ref = f32[16,8,128]{2,1,0:T(8,128)S(1)} all-to-all(f32[16,8,128]{2,1,0:T(8,128)S(1)} %get-tuple-element.29), channel_id=1, replica_groups=mesh['gz'=2,'xy'=16] {'xy'}, dimensions={0} | all-to-all | bytes 131072 | tf_op jit(solution)/shard_map/all_to_all | solution.py:554
  77.5 3.2 %shard_map.145 = (f32[3,2048]{1,0:T(4,128)S(1)}, f32[6,512]{1,0:T(8,128)S(1)}) custom-call(s32[5]{0:T(128)S(1)} %stack.48.flags, f32[16,8,128]{2,1,0:T(8,128)S(1)} %all_to_all.11.part_ref, f32[2,3,3,16,128]{4,3,2,1,0:T(8,128)S(1)} %get-tuple-element.30.grad_ref, f32[768,128]{1,0:T(8,128)S(1)} %get-tuple-element.18.refs_0_, ...), custom_call_target="tpu_custom_call" | custom-call | tf_op jit(solution)/shard_map/pallas_call | solution.py:240
  80.6 0.6 copy.15
  81.3 0.6 copy.16
  (3 shorter events, 0.0 us)
Async XLA Ops:
  0.6 0.9 %copy-start.10 = (f32[1,1,6,512]{3,1,2,0:T(1,128)S(1)}, f32[1,1,6,512]{3,1,2,0:T(1,128)}, u32[]{:S(2)}) copy-start(f32[1,1,6,512]{3,1,2,0:T(1,128)} %param.13) | copy-start | bytes 36868
  1.5 1.2 %copy-start.1 = (f32[1,1,3,2048]{3,1,2,0:T(1,128)S(1)}, f32[1,1,3,2048]{3,1,2,0:T(1,128)}, u32[]{:S(2)}) copy-start(f32[1,1,3,2048]{3,1,2,0:T(1,128)} %param.17) | copy-start | bytes 73732
  1.5 1.2 %copy-start.2 = (f32[1,1,2048]{2,1,0:T(1,128)S(1)}, f32[1,1,2048]{2,1,0:T(1,128)}, u32[]{:S(2)}) copy-start(f32[1,1,2048]{2,1,0:T(1,128)} %param.18) | copy-start | bytes 24580
  1.5 1.2 %copy-start.3 = (f32[1,1,2048]{2,1,0:T(1,128)S(1)}, f32[1,1,2048]{2,1,0:T(1,128)}, u32[]{:S(2)}) copy-start(f32[1,1,2048]{2,1,0:T(1,128)} %param.19) | copy-start | bytes 24580
  1.5 1.2 %copy-start.4 = (f32[1,1,2048]{2,1,0:T(1,128)S(1)}, f32[1,1,2048]{2,1,0:T(1,128)}, u32[]{:S(2)}) copy-start(f32[1,1,2048]{2,1,0:T(1,128)} %param.20) | copy-start | bytes 24580
  1.5 1.2 %copy-start.5 = (s32[1,1,2048]{2,1,0:T(1,128)S(1)}, s32[1,1,2048]{2,1,0:T(1,128)}, u32[]{:S(2)}) copy-start(s32[1,1,2048]{2,1,0:T(1,128)} %param.21) | copy-start | bytes 24580
  1.5 1.2 %copy-start.6 = (s32[1,1,2048]{2,1,0:T(1,128)S(1)}, s32[1,1,2048]{2,1,0:T(1,128)}, u32[]{:S(2)}) copy-start(s32[1,1,2048]{2,1,0:T(1,128)} %param.22) | copy-start | bytes 24580
  2.6 0.7 copy-start
  2.7 0.7 copy-start.7
  2.7 0.7 copy-start.8
  2.7 0.7 copy-start.9
  4.1 11.0 %collective-permute-start.2 = (f32[768,128]{1,0:T(8,128)S(1)}, f32[768,128]{1,0:T(8,128)S(1)}, u32[]{:S(2)}, u32[]{:S(2)}) collective-permute-start(f32[768,128]{1,0:T(8,128)S(1)} %get-tuple-element.18.refs_0_), channel_id=1, source_target_pairs={{16,0},{0,16},{17,1},{1,17},{18,2},{2,18},{19,3},{3,19},{20,4},{4,... | collective-permute-start | bytes 1179656 | tf_op jit(solution)/shard_map/ppermute | solution.py:358
  6.2 16.3 %collective-permute-start.1 = (f32[768,128]{1,0:T(8,128)S(1)}, f32[768,128]{1,0:T(8,128)S(1)}, u32[]{:S(2)}, u32[]{:S(2)}) collective-permute-start(f32[768,128]{1,0:T(8,128)S(1)} %get-tuple-element.18.refs_0_), channel_id=1, source_target_pairs={{0,0},{1,2},{2,1},{3,4},{4,3},{5,6},{6,5},{7,8},{8,7},{9,10},{10,9... | collective-permute-start | bytes 1179656 | tf_op jit(solution)/shard_map/ppermute | solution.py:355
  10.2 12.4 %collective-permute-start = (f32[768,128]{1,0:T(8,128)S(1)}, f32[768,128]{1,0:T(8,128)S(1)}, u32[]{:S(2)}, u32[]{:S(2)}) collective-permute-start(f32[768,128]{1,0:T(8,128)S(1)} %get-tuple-element.18.refs_0_), channel_id=1, source_target_pairs={{0,1},{1,0},{2,3},{3,2},{4,5},{5,4},{6,7},{7,6},{8,9},{9,8},{10,11... | collective-permute-start | bytes 1179656 | tf_op jit(solution)/shard_map/ppermute | solution.py:355
  15.0 13.4 %collective-permute-start.4 = (f32[768,128]{1,0:T(8,128)S(1)}, f32[768,128]{1,0:T(8,128)S(1)}, u32[]{:S(2)}, u32[]{:S(2)}) collective-permute-start(f32[768,128]{1,0:T(8,128)S(1)} %collective-permute-done.2.refs_3_), channel_id=1, source_target_pairs={{0,0},{1,2},{2,1},{3,4},{4,3},{5,6},{6,5},{7,8},{8,7},{9,10},{10,9... | collective-permute-start | bytes 1179656 | tf_op jit(solution)/shard_map/ppermute | solution.py:355
  19.5 8.9 %collective-permute-start.3 = (f32[768,128]{1,0:T(8,128)S(1)}, f32[768,128]{1,0:T(8,128)S(1)}, u32[]{:S(2)}, u32[]{:S(2)}) collective-permute-start(f32[768,128]{1,0:T(8,128)S(1)} %collective-permute-done.2.refs_3_), channel_id=1, source_target_pairs={{0,1},{1,0},{2,3},{3,2},{4,5},{5,4},{6,7},{7,6},{8,9},{9,8},{10,11... | collective-permute-start | bytes 1179656 | tf_op jit(solution)/shard_map/ppermute | solution.py:355
  19.6 3.0 %collective-permute-start.5 = (f32[88,128]{1,0:T(8,128)S(1)}, f32[88,128]{1,0:T(8,128)S(1)}, u32[]{:S(2)}, u32[]{:S(2)}) collective-permute-start(f32[88,128]{1,0:T(8,128)S(1)} %get-tuple-element.19.refs_6_), channel_id=1, source_target_pairs={{16,0},{0,16},{17,1},{1,17},{18,2},{2,18},{19,3},{3,19},{20,4},{4,... | collective-permute-start | bytes 135176 | tf_op jit(solution)/shard_map/ppermute | solution.py:358
  31.8 4.5 %collective-permute-start.6 = (f32[2,8,768]{2,1,0:T(8,128)S(1)}, f32[2,8,768]{2,1,0:T(8,128)S(1)}, u32[]{:S(2)}, u32[]{:S(2)}) collective-permute-start(f32[2,8,768]{2,1,0:T(8,128)S(1)} %get-tuple-element.21.sent_first), channel_id=1, source_target_pairs={{0,1},{1,0},{2,3},{3,2},{4,5},{5,4},{6,7},{7,6},{8,9},{9,8},{10,11... | collective-permute-start | bytes 147464 | tf_op jit(solution)/shard_map/ppermute | solution.py:355
  31.9 6.2 %collective-permute-start.7 = (f32[2,8,768]{2,1,0:T(8,128)S(1)}, f32[2,8,768]{2,1,0:T(8,128)S(1)}, u32[]{:S(2)}, u32[]{:S(2)}) collective-permute-start(f32[2,8,768]{2,1,0:T(8,128)S(1)} %get-tuple-element.22.sent_second), channel_id=1, source_target_pairs={{0,0},{1,2},{2,1},{3,4},{4,3},{5,6},{6,5},{7,8},{8,7},{9,10},{10,9... | collective-permute-start | bytes 147464 | tf_op jit(solution)/shard_map/ppermute | solution.py:355
  58.1 2.9 %collective-permute-start.8 = (f32[2,8,768]{2,1,0:T(8,128)S(1)}, f32[2,8,768]{2,1,0:T(8,128)S(1)}, u32[]{:S(2)}, u32[]{:S(2)}) collective-permute-start(f32[2,8,768]{2,1,0:T(8,128)S(1)} %get-tuple-element.26.sent_first), channel_id=1, source_target_pairs={{0,1},{1,0},{2,3},{3,2},{4,5},{5,4},{6,7},{7,6},{8,9},{9,8},{10,11... | collective-permute-start | bytes 147464 | tf_op jit(solution)/shard_map/ppermute | solution.py:355
  59.1 5.4 %collective-permute-start.9 = (f32[2,8,768]{2,1,0:T(8,128)S(1)}, f32[2,8,768]{2,1,0:T(8,128)S(1)}, u32[]{:S(2)}, u32[]{:S(2)}) collective-permute-start(f32[2,8,768]{2,1,0:T(8,128)S(1)} %get-tuple-element.27.sent_second), channel_id=1, source_target_pairs={{0,0},{1,2},{2,1},{3,4},{4,3},{5,6},{6,5},{7,8},{8,7},{9,10},{10,9... | collective-permute-start | bytes 147464 | tf_op jit(solution)/shard_map/ppermute | solution.py:355
where the time goes:
time: 83.2 us; the launch traced here: 81.9 us
  blocking collectives  21.1 us (25%)
  starting transfers between devices  19.3 us (23%)
  Pallas kernels  19.2 us (23%)
  waiting for transfers between devices  17.5 us (21%)
  local copies, waits for them, and re-layouts  3.93 us (5%)
  between operations  0.87 us (1%)
    all_to_all x2, blocking collectives, on_device(): parts = lax.all_to_all(parts, 'xy', 0, 0, tiled=True)  21.1 us
    pallas_call x6, Pallas kernels, call(): pl.pallas_call(body, out_shape=[jax.ShapeDtypeStruct(shape, F32) for shap...  19.2 us
    ppermute x4, starting transfers between devices, swap(): lax.ppermute(second, 'xy', to_second)  14.7 us
    ppermute x4, waiting for transfers between devices, swap(): lax.ppermute(second, 'xy', to_second)  11.1 us
    ppermute x2, waiting for transfers between devices, turned(): lax.ppermute(array, 'gz', [((i + step) % slots, i) for i in range(slots)])  6.38 us
    ppermute x2, starting transfers between devices, turned(): lax.ppermute(array, 'gz', [((i + step) % slots, i) for i in range(slots)])  3.44 us
    unnamed x26, local copies, waits for them, and re-layouts  3.01 us
  transfers between devices with their start and end apart: 10, of which 5 were waited for; matrix products, arithmetic and copies ran while one was open for 0% of the time, Pallas kernels for 0%

commit v1 on v0

v1 whole, which is shorter than its diff:
```python
import math

import jax
import jax.numpy as jnp
from jax import lax
from jax.experimental import pallas as pl
from jax.experimental.pallas import tpu as pltpu
from jax.sharding import PartitionSpec as P

ITERS = 2
EPSILON = 1e-06
THETA_START = 0.3
LANES = 128
WIDE = 256
F32 = jnp.float32
BF16 = jnp.bfloat16
I32 = jnp.int32


def theta_after(theta_value):
    return 0.5 * (
        -theta_value * theta_value + theta_value * math.sqrt(theta_value * theta_value + 4.0)
    )


def momentum_factors(iteration_count):
    thetas = [THETA_START]
    for iteration in range(iteration_count):
        thetas.append(theta_after(thetas[-1]))
    return [
        thetas[position]
        * (1.0 - thetas[position])
        / (thetas[position] * thetas[position] + thetas[position + 1])
        for position in range(iteration_count)
    ]


def pair_swaps(count, parity):
    target = list(range(count))
    for cell in range(parity, count - 1, 2):
        target[cell], target[cell + 1] = cell + 1, cell
    return list(enumerate(target))


class Sizes:
    def __init__(self, contacts, own, layer, side, slots, cells):
        self.contacts, self.own, self.layer, self.side = contacts, own, layer, side
        self.slots, self.cells = slots, cells
        self.blocks = contacts // LANES
        self.section = own + layer
        self.window = -(-side // LANES) * LANES
        self.margin = self.window - side
        self.own_groups = own // LANES
        self.layer_groups = layer // LANES
        self.section_groups = self.section // LANES
        self.total_groups = (self.section + 2 * side) // LANES
        self.window_groups = self.window // LANES
        self.layer_at = 2 * self.own_groups
        self.side_at = self.layer_at + self.layer_groups
        self.sphere_groups = self.side_at + self.window_groups
        self.mail_groups = self.section_groups + self.sphere_groups
        self.sent = own + self.window
        assert contacts % LANES == own % LANES == layer % LANES == 2 * side % LANES == 0
        assert self.blocks % 8 == 0


NEAR, FAR, ALIVE, FRICTION, SOFTNESS, OFFSET, CURRENT, GUESS = 36, 37, 38, 39, 40, 41, 42, 45
TILES = 48


class Contacts:
    def __init__(self, ref):
        self.ref = ref

    def tile(self, which):
        return self.ref[which]

    def entry(self, row, part, body, rows=slice(None)):
        return self.ref[12 * row + 6 * part + body, rows, :]


class Spheres:
    def __init__(self, ref, sizes, start=0):
        self.ref, self.sizes, self.start = ref, sizes, start

    def misc(self, group):
        return self.ref[:, pl.ds((self.start + group) * LANES, LANES)]

    def free(self, group):
        return self.misc(group)

    def weight(self, group):
        return self.misc(self.sizes.own_groups + group)

    def layer_list(self, group):
        return self.misc(self.sizes.layer_at + group)[0:1].astype(I32)

    def side_list(self, which, group):
        return self.misc(self.sizes.side_at + group)[which : which + 1].astype(I32)


def places(index, groups):
    index = jnp.broadcast_to(index, (8, LANES))
    which = index >> 7
    return index & (LANES - 1), [which == number for number in range(groups)]


def gather(groups, place):
    lane, inside = place
    out = jnp.zeros((8, LANES), groups[0].dtype)
    for group, here in zip(groups, inside):
        group = jnp.broadcast_to(group, (8, LANES))
        out = jnp.where(here, jnp.take_along_axis(group, lane, axis=1, mode="promise_in_bounds"), out)
    return out


def look_up(lists, index):
    pieces = [
        gather(lists, places(index[at : at + 8], len(lists))) for at in range(0, index.shape[0], 8)
    ]
    return jnp.concatenate(pieces, axis=0) - 1


def lay_hot(index, hot_ref):
    lane_of = (index & (LANES - 1)).astype(F32)
    row_number = lax.broadcasted_iota(I32, (LANES, LANES), 0).astype(F32).astype(BF16)
    zeros, ones = jnp.zeros((16, LANES), BF16), jnp.ones((16, LANES), BF16)
    for block in range(index.shape[0]):
        low = jnp.broadcast_to(lane_of[block : block + 1], (16, LANES)).astype(BF16)
        for piece in range(LANES // 16):
            rows = slice(piece * 16, piece * 16 + 16)
            hot = jnp.where(row_number[rows] == low, ones, zeros)
            hot_ref[pl.ds(piece * 16, 16), pl.ds(block * LANES, LANES)] = hot


def lay_terms(terms, index, groups, parts_ref, spread_ref):
    blocks = terms[0].shape[0]
    for body, term in enumerate(terms):
        upper = term.astype(BF16).astype(F32)
        parts_ref[pl.ds(body * blocks, blocks), :] = upper
        parts_ref[pl.ds((8 + body) * blocks, blocks), :] = term - upper
    group_of = (index >> 7).astype(F32)
    zeros = jnp.zeros((16, LANES), BF16)
    for block in range(blocks):
        both = parts_ref[pl.ds(block, 16, stride=blocks), :].astype(BF16)
        which = jnp.broadcast_to(group_of[block : block + 1], (16, LANES)).astype(BF16)
        for at, number in enumerate(groups):
            part = jnp.where(which == jnp.asarray(number, BF16), both, zeros)
            spread_ref[pl.ds(at * 16, 16), pl.ds(block * LANES, LANES)] = part


def summed(spread, hot):
    out = lax.dot_general(spread, hot, (((1,), (1,)), ((), ())), preferred_element_type=F32)
    return [out[at : at + 8] + out[at + 8 : at + 16] for at in range(0, out.shape[0], 16)]


def put_columns(values, lists, groups):
    result = [jnp.zeros((8, LANES), F32)] * groups
    row_number = lax.broadcasted_iota(I32, (LANES, LANES), 0)
    for value, index in zip(values, lists):
        upper = value.astype(BF16).astype(F32)
        both = jnp.concatenate([upper, value - upper], axis=0)
        which = jnp.broadcast_to(index >> 7, (16, LANES))
        spread = jnp.concatenate([jnp.where(which == g, both, 0.0) for g in range(groups)], axis=0)
        low = jnp.broadcast_to(index & (LANES - 1), (LANES, LANES))
        hot = jnp.where(row_number == low, 1.0, 0.0).astype(BF16)
        result = [a + b for a, b in zip(result, summed(spread.astype(BF16), hot))]
    return result


class Maps:
    def __init__(self, spheres, sizes, flags):
        self.spheres, self.sizes, self.flags = spheres, sizes, flags

    def upper(self, slot):
        above = self.spheres[(slot + 1) % self.sizes.slots]
        return [above.layer_list(group) for group in range(self.sizes.layer_groups)]

    def side(self, slot, which):
        picks = []
        for group in range(self.sizes.window_groups):
            to_lower = self.spheres[slot].side_list(0, group)
            to_higher = self.spheres[slot].side_list(1, group)
            higher = (self.flags[0] == 0) == (which == 1)
            picks.append(jnp.where(higher, to_higher, to_lower))
        return picks

    def window_index(self, far, which):
        sizes = self.sizes
        higher = (self.flags[0] == 0) == (which == 1)
        return far - jnp.where(higher, sizes.section, sizes.section + sizes.side - sizes.margin)

    def section_row(self, slot, which, far):
        if which == 0:
            return jnp.where(far < self.sizes.section, far, -1)
        row = look_up(self.side(slot, which), self.window_index(far, which))
        return jnp.where(self.flags[which] != 0, row, -1)


def set_terms(slot, which, pack, value, maps, sizes, hots, scratch, groups, new_hots=False):
    far_hot, near_hot = hots
    parts_ref, spread_ref, near_parts, near_spread = scratch
    far = maps.section_row(slot, which, pack.tile(FAR).astype(I32))
    own = [group for group in groups if group < sizes.own_groups] if which == 0 else []
    todo = [(1, far, groups, far_hot, parts_ref, spread_ref)]
    if own:
        todo.append((0, pack.tile(NEAR).astype(I32), own, near_hot, near_parts, near_spread))
    result = {}
    for part, index, wanted, hot_ref, to_parts, to_spread in todo:
        terms = [
            pack.entry(0, part, body) * value[0]
            + pack.entry(1, part, body) * value[1]
            + pack.entry(2, part, body) * value[2]
            for body in range(6)
        ]
        if new_hots:
            lay_hot(index, hot_ref)
        lay_terms(terms, index, wanted, to_parts, to_spread)
        sums = summed(to_spread[pl.ds(0, 16 * len(wanted)), :], hot_ref[...])
        for group, total in zip(wanted, sums):
            result[group] = result[group] + total if group in result else total
    return [result[group] for group in groups]


def added(lists):
    return [sum(values[1:], values[0]) for values in zip(*lists)]


def joined(sections, spheres, sizes, flags, slot):
    own = sections[slot][: sizes.own_groups]
    if sizes.slots > 1:
        below = (slot + sizes.slots - 1) % sizes.slots
        upper = [jnp.where(flags[3 + below] != 0, v, 0.0) for v in sections[below][-sizes.layer_groups :]]
        lists = [spheres[slot].layer_list(group) - 1 for group in range(sizes.layer_groups)]
        own = added([own, put_columns(upper, lists, sizes.own_groups)])
    return own


def rows_of(pack, near_rows, far_rows, far_index):
    near_index = pack.tile(NEAR).astype(I32)
    near_groups, far_groups = len(near_rows(0)), len(far_rows(0))
    halves = []
    for at in range(0, near_index.shape[0], 8):
        rows = slice(at, at + 8)
        totals = [None] * 3
        for part, table, place in (
            (0, near_rows, places(near_index[rows], near_groups)),
            (1, far_rows, places(far_index[rows], far_groups)),
        ):
            for body in range(6):
                picked = gather(table(body), place)
                for row in range(3):
                    term = pack.entry(row, part, body, rows) * picked
                    totals[row] = term if totals[row] is None else totals[row] + term
        halves.append(totals)
    return [jnp.concatenate([half[row] for half in halves], axis=0) for row in range(3)]


def cone_project(impulse_value, cone_friction):
    normal, first, second = impulse_value
    slide_norm = jnp.sqrt(first * first + second * second)
    inside_cone = slide_norm <= cone_friction * normal
    polar_cone = cone_friction * slide_norm <= -normal
    outside_both = jnp.logical_not(jnp.logical_or(inside_cone, polar_cone))
    onto_normal = (cone_friction * slide_norm + normal) / (cone_friction * cone_friction + 1.0)
    tangent_scale = cone_friction * onto_normal / jnp.where(outside_both, slide_norm, 1.0)
    scale = jnp.where(inside_cone, 1.0, jnp.where(polar_cone, 0.0, tangent_scale))
    new_normal = jnp.where(inside_cone, normal, jnp.where(polar_cone, 0.0, onto_normal))
    return [new_normal, scale * first, scale * second]


def call(body, out_shape, operands, scratch=(), space=pltpu.VMEM, room=40):
    specs = [pl.BlockSpec(memory_space=pltpu.SMEM)]
    specs += [pl.BlockSpec(memory_space=space)] * (len(operands) - 1)
    return pl.pallas_call(
        body,
        out_shape=[
            jax.ShapeDtypeStruct(*shape) if isinstance(shape[0], tuple) else jax.ShapeDtypeStruct(shape, F32)
            for shape in out_shape
        ],
        in_specs=specs,
        out_specs=[pl.BlockSpec(memory_space=pltpu.VMEM)] * len(out_shape),
        scratch_shapes=list(scratch),
        compiler_params=pltpu.CompilerParams(vmem_limit_bytes=room * 1024 * 1024),
    )(*operands)


def on_device(
    velocity_free,
    inverse_mass,
    jacobian,
    impulses,
    previous_impulses,
    compliance,
    offset,
    friction,
    body_near,
    body_far,
    block_counts,
    layer_send,
    side_send,
):
    slots, cells = lax.axis_size("gz"), lax.axis_size("xy")
    layer_at, cell_at = lax.axis_index("gz"), lax.axis_index("xy")
    sizes = Sizes(
        jacobian.shape[3], velocity_free.shape[3], layer_send.shape[2], side_send.shape[3], slots, cells
    )
    blocks, window = sizes.blocks, sizes.window
    factors = momentum_factors(ITERS)

    odd = cell_at % 2
    lower, higher = cell_at > 0, cell_at < cells - 1
    flags = jnp.stack(
        [odd, jnp.where(odd == 0, higher, lower), jnp.where(odd == 0, lower, higher)]
        + [(layer_at + slot) % slots != slots - 1 for slot in range(slots)]
    ).astype(I32)

    def tiles(array):
        return array.reshape(-1, blocks, LANES)

    def pack_body(counts, *refs):
        inputs, (out_ref, sphere_ref, *held, semaphores) = refs[:12], refs[12:]
        targets = [*held[:2], out_ref.at[pl.ds(0, 36)], *held[2:]]
        copies = [
            pltpu.make_async_copy(source, target, semaphores.at[at])
            for at, (source, target) in enumerate(zip(inputs, targets))
        ]
        for copy in copies:
            copy.start()
        for copy in copies:
            copy.wait()
        (free_ref, mass_ref, imp_ref, prev_ref, soft_ref, off_ref, fric_ref, near_ref, far_ref,
         layer_ref, side_ref) = held
        lane = lax.broadcasted_iota(I32, (1, LANES), 1)
        rows = [jnp.where(lane < counts[block], 1.0, 0.0) for block in range(blocks)]
        alive = jnp.concatenate(rows, axis=0)
        out_ref[NEAR] = near_ref[0].astype(F32)
        out_ref[FAR] = far_ref[0].astype(F32)
        out_ref[ALIVE] = alive
        out_ref[FRICTION] = fric_ref[0]
        out_ref[SOFTNESS] = soft_ref[0]
        out_ref[OFFSET] = off_ref[0]
        for row in range(3):
            current = alive * imp_ref[row]
            earlier = alive * prev_ref[row]
            out_ref[CURRENT + row] = current
            out_ref[GUESS + row] = alive * (current + factors[0] * (current - earlier))

        gap = jnp.zeros((2, LANES), F32)

        def misc(group, value):
            sphere_ref[:, pl.ds(group * LANES, LANES)] = value

        for group in range(sizes.own_groups):
            lanes = pl.ds(group * LANES, LANES)
            free = [free_ref[body, pl.ds(group, 1), :] for body in range(6)]
            misc(group, jnp.concatenate(free + [gap], axis=0))
            mass = mass_ref[:, lanes]
            linear = jnp.broadcast_to(mass[0:1], (3, LANES))
            angular = jnp.broadcast_to(mass[1:2], (3, LANES))
            misc(sizes.own_groups + group, jnp.concatenate([linear, angular, gap], axis=0))
        for group in range(sizes.layer_groups):
            lanes = pl.ds(group * LANES, LANES)
            rows = jnp.broadcast_to(layer_ref[:, lanes] + 1, (8, LANES))
            misc(sizes.layer_at + group, rows.astype(F32))
        side = side_ref[...] + 1
        if sizes.margin:
            none = jnp.zeros((1, sizes.margin), I32)
            to_lower = jnp.concatenate([none, side[0:1]], axis=1)
            to_higher = jnp.concatenate([side[1:2], none], axis=1)
            side = jnp.concatenate([to_lower, to_higher], axis=0)
        for group in range(sizes.window_groups):
            rows = jnp.concatenate([side[:, group * LANES : (group + 1) * LANES]] * 4, axis=0)
            misc(sizes.side_at + group, rows.astype(F32))

    loaded = [
        velocity_free[0, 0].reshape(6, sizes.own_groups, LANES),
        inverse_mass[0, 0],
        tiles(jacobian[0, 0]),
        tiles(impulses[0, 0]),
        tiles(previous_impulses[0, 0]),
        tiles(compliance[0, 0]),
        tiles(offset[0, 0]),
        tiles(friction[0, 0]),
        tiles(body_near[0, 0]),
        tiles(body_far[0, 0]),
        layer_send[0],
        side_send[0, 0],
    ]
    own_contacts, own_spheres = call(
        pack_body,
        [(TILES, blocks, LANES), (8, sizes.sphere_groups * LANES)],
        [block_counts[0, 0], *loaded],
        [pltpu.VMEM(array.shape, array.dtype) for at, array in enumerate(loaded) if at != 2]
        + [pltpu.SemaphoreType.DMA((len(loaded),))],
        pl.ANY,
        62,
    )
    to_first, to_second = pair_swaps(cells, 0), pair_swaps(cells, 1)

    def swap(first, second):
        return lax.ppermute(first, "xy", to_first), lax.ppermute(second, "xy", to_second)

    def turned(array, step):
        return lax.ppermute(array, "gz", [((i + step) % slots, i) for i in range(slots)])

    contact_arrays = []
    for slot in range(slots):
        held = own_contacts if slot == 0 else turned(own_contacts, slot)
        contact_arrays.append([held, *swap(held, held)])

    def views(refs):
        sets = [[Contacts(refs[3 * s + w]) for w in range(3)] for s in range(slots)]
        refs = refs[3 * slots :]
        spheres = [Spheres(ref, sizes, sizes.section_groups) for ref in refs[:slots]]
        refs = refs[slots:]
        hots = [
            [(refs[4 * s + 1 + w], refs[4 * s] if w == 0 else None) for w in range(3)] for s in range(slots)
        ]
        return sets, spheres, hots, refs[4 * slots :]

    def chosen(*arrays):
        return [array for array in arrays if array is not None]

    state_shape = (slots, 3, 3, blocks, LANES)
    section_shape, sent_shape = (slots, 8, sizes.section), (slots, 8, sizes.sent)
    hot_shape = ((LANES, sizes.contacts), BF16)

    def scratch_of(own):
        split = pltpu.VMEM((16 * blocks, LANES), F32)
        spread = [pltpu.VMEM((16 * n, sizes.contacts), BF16) for n in (sizes.section_groups, sizes.own_groups)]
        return [split, spread[0]] + ([split, spread[1]] if own else [])

    work = scratch_of(True) + scratch_of(False) * 2

    def places_of(scratch, slot, which):
        base = (slot % 2) * len(work)
        if which == 0:
            return scratch[base : base + 4]
        return [*scratch[base + 2 + 2 * which : base + 4 + 2 * which], None, None]

    def clear(scratch):
        gap = jnp.zeros((2 * blocks, LANES), F32)
        for ref in scratch[::2]:
            ref[pl.ds(6 * blocks, 2 * blocks), :] = gap
            ref[pl.ds(14 * blocks, 2 * blocks), :] = gap

    def slot_sections(sets, values, maps, hots, scratch, wanted):
        clear(scratch)
        return [
            added(
                [
                    set_terms(
                        s, w, sets[s][w], values[s][w], maps, sizes, hots[s][w], places_of(scratch, s, w), groups
                    )
                    for w in range(3)
                ]
            )
            if groups
            else None
            for s, groups in enumerate(wanted)
        ]

    every = list(range(sizes.section_groups))

    def put_velocities(sums, spheres, maps, flags, section_ref, first_ref, second_ref):
        velocity = [
            [spheres[s].free(g) + spheres[s].weight(g) * sums[s][g] for g in range(sizes.own_groups)]
            for s in range(slots)
        ]
        for slot in range(slots):
            table = list(velocity[slot])
            for rows in maps.upper(slot):
                upper = gather(velocity[(slot + 1) % slots], places(rows - 1, sizes.own_groups))
                table.append(jnp.where(flags[3 + slot] != 0, upper, 0.0))
            for group, value in enumerate(table):
                section_ref[slot, :, pl.ds(group * LANES, LANES)] = value
            for which, sent_ref in ((1, first_ref), (2, second_ref)):
                for group, value in enumerate(velocity[slot]):
                    sent_ref[slot, :, pl.ds(group * LANES, LANES)] = value
                for group, rows in enumerate(maps.side(slot, which)):
                    lanes = pl.ds(sizes.own + group * LANES, LANES)
                    sent_ref[slot, :, lanes] = gather(table, places(rows - 1, sizes.section_groups))

    def first_terms():
        def guess_of(pack):
            return [pack.tile(GUESS + row) for row in range(3)]

        def early(flags, own_ref, first_ref, sphere_ref, out_ref, near_hot, far_hot, first_hot, *scratch):
            clear(scratch)
            maps = Maps([Spheres(sphere_ref, sizes)], sizes, flags)
            sets = [Contacts(own_ref), Contacts(first_ref)]
            hots = [(far_hot, near_hot), (first_hot, None)]
            sums = added(
                [
                    set_terms(
                        0, w, sets[w], guess_of(sets[w]), maps, sizes, hots[w], places_of(scratch, 0, w),
                        every, True,
                    )
                    for w in range(2)
                ]
            )
            for group, value in enumerate(sums):
                out_ref[:, pl.ds(group * LANES, LANES)] = value

        def late(flags, part_ref, second_ref, sphere_ref, out_ref, hot_ref, *scratch):
            clear(scratch)
            maps = Maps([Spheres(sphere_ref, sizes)], sizes, flags)
            pack = Contacts(second_ref)
            sums = set_terms(
                0, 2, pack, guess_of(pack), maps, sizes, (hot_ref, None), [*scratch, None, None], every, True
            )
            for group, value in enumerate(sums):
                lanes = pl.ds(group * LANES, LANES)
                out_ref[:, lanes] = part_ref[:, lanes] + value
            out_ref[:, pl.ds(sizes.section, sizes.sphere_groups * LANES)] = sphere_ref[...]

        own, first, second = contact_arrays[0]
        part, near_hot, far_hot, first_hot = call(
            early, [(8, sizes.section), hot_shape, hot_shape, hot_shape], [flags, own, first, own_spheres], work[:6]
        )
        mail, second_hot = call(
            late,
            [(8, sizes.mail_groups * LANES), hot_shape],
            [flags, part, second, own_spheres],
            work[4:6],
        )
        return mail, [near_hot, far_hot, first_hot, second_hot]

    def one_hots(slot, mail):
        def body(flags, own_ref, first_ref, second_ref, mail_ref, near_hot, *hot_refs):
            spheres = {slot: Spheres(mail_ref, sizes, sizes.section_groups)}
            maps = Maps(spheres, sizes, flags)
            packs = [Contacts(ref) for ref in (own_ref, first_ref, second_ref)]
            lay_hot(packs[0].tile(NEAR).astype(I32), near_hot)
            for which, pack in enumerate(packs):
                lay_hot(maps.section_row(slot, which, pack.tile(FAR).astype(I32)), hot_refs[which])

        return call(body, [hot_shape] * 4, [flags, *contact_arrays[slot], mail])

    mail, hots = first_terms()
    mails = [mail] + [turned(mail, step) for step in range(1, slots)]
    for slot in range(1, slots):
        hots = [*hots, *one_hots(slot, mails[slot])]
    inputs = [*sum(contact_arrays, []), *mails, *hots]

    def first_velocities():
        def body(flags, *refs):
            mail_refs, refs = refs[:slots], refs[slots:]
            spheres = [Spheres(ref, sizes, sizes.section_groups) for ref in mail_refs]
            maps = Maps(spheres, sizes, flags)
            sections = [[ref[:, pl.ds(group * LANES, LANES)] for group in every] for ref in mail_refs]
            sums = [joined(sections, spheres, sizes, flags, slot) for slot in range(slots)]
            put_velocities(sums, spheres, maps, flags, *refs)

        return call(body, [section_shape, sent_shape, sent_shape], [flags, *mails])

    def gradients(section, sent, got, state):
        def body(flags, section_ref, sent_first, sent_second, got_first, got_second, *refs):
            sets, spheres, hots, refs = views(refs)
            if state is None:
                state_ref = None
            else:
                state_ref, *refs = refs
            grad_ref, parts_ref, table_ref, *scratch = refs
            maps = Maps(spheres, sizes, flags)
            even = flags[0] == 0
            norm = soft = jnp.zeros((blocks, LANES), F32)
            lane = lax.broadcasted_iota(I32, (8, LANES), 1)
            edge = sizes.side % LANES

            def rows_from(ref, slot, start, count):
                def rows(body):
                    return [ref[slot, pl.ds(body, 1), pl.ds(start + g * LANES, LANES)] for g in range(count)]

                return rows

            values = []
            for slot in range(slots):
                low, high = [], []
                for group in range(sizes.window_groups):
                    lanes = pl.ds(sizes.own + group * LANES, LANES)
                    first = jnp.where(flags[1] != 0, got_first[slot, :, lanes], 0.0)
                    second = jnp.where(flags[2] != 0, got_second[slot, :, lanes], 0.0)
                    low.append(jnp.where(even, second, first))
                    high.append(jnp.where(even, first, second))
                if edge:
                    extended = low[:-1] + [jnp.where(lane < edge, low[-1], high[0])] + high[1:]
                else:
                    extended = low + high
                table_ref[slot, :, pl.ds(0, sizes.section)] = section_ref[slot]
                for group, value in enumerate(extended):
                    table_ref[slot, :, pl.ds(sizes.section + group * LANES, LANES)] = value
                slot_values = []
                for which, pack in enumerate(sets[slot]):
                    far = pack.tile(FAR).astype(I32)
                    if which == 0:
                        near_rows = rows_from(table_ref, slot, 0, sizes.own_groups)
                        far_rows = rows_from(table_ref, slot, 0, sizes.total_groups)
                    else:
                        got_ref = (got_first, got_second)[which - 1]
                        sent_ref = (sent_first, sent_second)[which - 1]
                        near_rows = rows_from(got_ref, slot, 0, sizes.own_groups)
                        far_rows = rows_from(sent_ref, slot, sizes.own, sizes.window_groups)
                        far = maps.window_index(far, which)
                    contact_rows = rows_of(pack, near_rows, far_rows, far)
                    alive, softness = pack.tile(ALIVE), pack.tile(SOFTNESS)
                    grad = []
                    for row in range(3):
                        guess = pack.tile(GUESS + row) if state_ref is None else state_ref[slot, which, row]
                        value = contact_rows[row] + softness * guess
                        if row == 0:
                            value = value + pack.tile(OFFSET)
                        value = alive * value
                        grad_ref[slot, which, row] = value
                        grad.append(value)
                        if which == 0:
                            norm = norm + value * value
                            soft = soft + softness * value * value
                    slot_values.append(grad)
                values.append(slot_values)
            sections = slot_sections(sets, values, maps, hots, scratch, [every] * slots)
            sums = [joined(sections, spheres, sizes, flags, slot) for slot in range(slots)]
            curve = jnp.sum(soft, axis=0, keepdims=True)
            norm = jnp.sum(norm, axis=0, keepdims=True)
            total = jnp.zeros((8, LANES), F32)
            for slot in range(slots):
                for group in range(sizes.own_groups):
                    value = sums[slot][group]
                    total = total + spheres[slot].weight(group) * value * value
            curve = curve + jnp.sum(total, axis=0, keepdims=True)
            half = LANES // 2
            norm = norm + pltpu.roll(norm, half, 1)
            curve = curve + pltpu.roll(curve, half, 1)
            both = jnp.where(lax.broadcasted_iota(I32, (1, LANES), 1) < half, norm, curve)
            for cell in range(cells):
                parts_ref[cell] = both

        return call(
            body,
            [state_shape, (cells, 1, LANES)],
            chosen(flags, section, *sent, *got, *inputs, state),
            [pltpu.VMEM((slots, 8, sizes.total_groups * LANES), F32), *work, *work],
        )

    def updates(parts, grad, state, earlier, factor):
        last = factor is None

        def body(flags, part_ref, grad_ref, *refs):
            sets, spheres, hots, refs = views(refs)
            if state is not None:
                state_ref, earlier_ref, *refs = refs
            if last:
                result_ref, velocity_ref, *scratch = refs
            else:
                result_ref, guess_ref, section_ref, first_ref, second_ref, *scratch = refs
            maps = Maps(spheres, sizes, flags)
            total = part_ref[0]
            for cell in range(1, cells):
                total = total + part_ref[cell]
            lane = lax.broadcasted_iota(I32, (1, LANES), 1)
            norm = jnp.sum(jnp.where(lane < LANES // 2, total, 0.0), axis=1, keepdims=True)
            curve = jnp.sum(jnp.where(lane < LANES // 2, 0.0, total), axis=1, keepdims=True)
            step = norm / (curve + EPSILON)
            values = []
            for slot in range(slots):
                slot_values = []
                for which, pack in enumerate(sets[slot]):
                    alive = pack.tile(ALIVE)
                    moved, before = [], []
                    for row in range(3):
                        if state is None:
                            guess, old = pack.tile(GUESS + row), pack.tile(CURRENT + row)
                        else:
                            guess, old = state_ref[slot, which, row], earlier_ref[slot, which, row]
                        before.append(old)
                        moved.append(guess - step * grad_ref[slot, which, row])
                    value = [alive * v for v in cone_project(moved, pack.tile(FRICTION))]
                    if not last:
                        guess = [alive * (v + factor * (v - b)) for v, b in zip(value, before)]
                        for row in range(3):
                            result_ref[slot, which, row] = value[row]
                            guess_ref[slot, which, row] = guess[row]
                        value = guess
                    elif slot == which == 0:
                        for row in range(3):
                            result_ref[row] = value[row]
                    slot_values.append(value)
                values.append(slot_values)
            wanted = [every] * slots
            if last:
                wanted = [[] for _ in range(slots)]
                wanted[-1] = every[sizes.own_groups :]
                wanted[0] = every[: sizes.own_groups]
            sections = slot_sections(sets, values, maps, hots, scratch, wanted)
            if last:
                total = joined(sections, spheres, sizes, flags, 0)
                for group in range(sizes.own_groups):
                    value = spheres[0].free(group) + spheres[0].weight(group) * total[group]
                    for body_row in range(6):
                        velocity_ref[body_row, pl.ds(group, 1), :] = value[body_row : body_row + 1]
            else:
                sums = [joined(sections, spheres, sizes, flags, slot) for slot in range(slots)]
                put_velocities(sums, spheres, maps, flags, section_ref, first_ref, second_ref)

        if last:
            shapes = [(3, blocks, LANES), (6, sizes.own_groups, LANES)]
        else:
            shapes = [state_shape, state_shape, section_shape, sent_shape, sent_shape]
        return call(body, shapes, chosen(flags, parts, grad, *inputs, state, earlier), [*work, *work])

    state = earlier = None
    section, *sent = first_velocities()
    for iteration in range(ITERS):
        grad, parts = gradients(section, sent, swap(*sent), state)
        parts = lax.all_to_all(parts, "xy", 0, 0, tiled=True)
        if iteration + 1 < ITERS:
            earlier, state, section, *sent = updates(parts, grad, state, earlier, factors[iteration + 1])
    result, velocity = updates(parts, grad, state, earlier, None)
    return (
        result.reshape(1, 1, 3, sizes.contacts),
        velocity.reshape(1, 1, 6, sizes.own),
    )


def solution(mesh):
    placed = (
        P("gz", "xy", None, None),
        P("gz", "xy", None, None),
        P("gz", "xy", None, None),
        P("gz", "xy", None, None),
        P("gz", "xy", None, None),
        P("gz", "xy", None),
        P("gz", "xy", None),
        P("gz", "xy", None),
        P("gz", "xy", None),
        P("gz", "xy", None),
        P("gz", "xy", None),
        P("gz", "xy", None),
        P("gz", "xy", None, None),
    )
    return jax.shard_map(
        on_device,
        mesh=mesh,
        in_specs=placed,
        out_specs=(P("gz", "xy", None, None), P("gz", "xy", None, None)),
        check_vma=False,
    )
```

time: 83.2 us -> 73.1 us (0.88)
  waiting for transfers between devices: 17.5 us -> 11.6 us
  local copies, waits for them, and re-layouts: 3.93 us -> 1.74 us
  blocking collectives: 21.1 us -> 19.9 us
  Pallas kernels: 19.2 us -> 18.3 us
    ppermute x4, waiting for transfers between devices: 11.1 us -> 4.61 us  [swap(): lax.ppermute(second, 'xy', to_second)]
    ppermute x4, starting transfers between devices: 1.21 us -> 3.52 us  [swap(): lax.ppermute(first, 'xy', to_first)]
    ppermute x4, starting transfers between devices: 14.7 us -> 12.7 us  [swap(): lax.ppermute(second, 'xy', to_second)]
    unnamed x26 -> x6, local copies, waits for them, and re-layouts: 3.01 us -> 1.66 us
    all_to_all x2, blocking collectives: 21.1 us -> 19.9 us  [on_device(): parts = lax.all_to_all(parts, 'xy', 0, 0, tiled=True)]
    pallas_call x6 -> x9, Pallas kernels: 19.2 us -> 18.3 us  [call(): pl.pallas_call(body, out_shape=[jax.ShapeDtypeStruct(*shape) if isinstanc...]
  transfers between devices with their start and end apart: 10 -> 10, of which waited for: 5 -> 4; matrix products, arithmetic and copies ran while one was open for 0% -> 0% of each run, Pallas kernels for 0% -> 6%
where the time goes in v1:
time: 73.1 us; the launch traced here: 72.1 us
  blocking collectives  19.9 us (27%)
  starting transfers between devices  19.6 us (27%)
  Pallas kernels  18.3 us (25%)
  waiting for transfers between devices  11.6 us (16%)
  local copies, waits for them, and re-layouts  1.74 us (2%)
  between operations  0.81 us (1%)
    all_to_all x2, blocking collectives, on_device(): parts = lax.all_to_all(parts, 'xy', 0, 0, tiled=True)  19.9 us
    pallas_call x9, Pallas kernels, call(): pl.pallas_call(body, out_shape=[jax.ShapeDtypeStruct(*shape) if isinstanc...  18.3 us
    ppermute x4, starting transfers between devices, swap(): lax.ppermute(second, 'xy', to_second)  12.7 us
    ppermute x2, waiting for transfers between devices, turned(): lax.ppermute(array, 'gz', [((i + step) % slots, i) for i in range(slots)])  6.97 us
    ppermute x4, waiting for transfers between devices, swap(): lax.ppermute(second, 'xy', to_second)  4.61 us
    ppermute x4, starting transfers between devices, swap(): lax.ppermute(first, 'xy', to_first)  3.52 us
    ppermute x2, starting transfers between devices, turned(): lax.ppermute(array, 'gz', [((i + step) % slots, i) for i in range(slots)])  3.44 us
    unnamed x6, local copies, waits for them, and re-layouts  1.66 us
  transfers between devices with their start and end apart: 10, of which 4 were waited for; matrix products, arithmetic and copies ran while one was open for 0% of the time, Pallas kernels for 6%

profile of v1, /device:TPU:1, one launch (start us, length us, event | category | flops | bytes accessed | tf_op | source)
XLA Modules:
  0.0 72.1 jit_solution(9114735637795586510)
XLA Ops:
  0.6 2.6 %shard_map.140 = (f32[48,16,128]{2,1,0:T(8,128)}, f32[8,1408]{1,0:T(8,128)}) custom-call(s32[16]{0:T(128)} %bitcast.31, f32[6,4,128]{2,1,0:T(4,128)} %bitcast.23, f32[2,512]{1,0:T(2,128)} %bitcast.29, f32[36,16,128]{2,1,0:T(8,128)} %bitcast.20, f32[3,16,128]{2,1,0:T(8,128)} %bitcast.21, f32[3,16,128]{2,1,0:T(8,128)} %bitcast.22, f32[1,16,128]{2,1,0:T(8,128)} %bitcast.24, ...), custom_call_target="tpu_custom_call" | custom-call | tf_op jit(solution)/shard_map/pallas_call | solution.py:275
  3.2 2.1 %collective-permute-start.5 = (f32[48,16,128]{2,1,0:T(8,128)}, f32[48,16,128]{2,1,0:T(8,128)S(1)}, u32[]{:S(2)}, u32[]{:S(2)}) collective-permute-start(f32[48,16,128]{2,1,0:T(8,128)} %get-tuple-element.28.own_ref.refs_0_), channel_id=1, source_target_pairs={{16,0},{0,16},{17,1},{1,17},{18,2},{2,18},{19,3},{3,19},{20,4},{4,... | collective-permute-start | bytes 1179656 | tf_op jit(solution)/shard_map/ppermute | solution.py:405
  5.3 1.0 %collective-permute-start = (f32[48,16,128]{2,1,0:T(8,128)}, f32[48,16,128]{2,1,0:T(8,128)S(1)}, u32[]{:S(2)}, u32[]{:S(2)}) collective-permute-start(f32[48,16,128]{2,1,0:T(8,128)} %get-tuple-element.28.own_ref.refs_0_), channel_id=1, source_target_pairs={{0,1},{1,0},{2,3},{3,2},{4,5},{5,4},{6,7},{7,6},{8,9},{9,8},{10,11... | collective-permute-start | bytes 1179656 | tf_op jit(solution)/shard_map/ppermute | solution.py:402
  6.3 3.0 %collective-permute-start.1 = (f32[48,16,128]{2,1,0:T(8,128)}, f32[48,16,128]{2,1,0:T(8,128)S(1)}, u32[]{:S(2)}, u32[]{:S(2)}) collective-permute-start(f32[48,16,128]{2,1,0:T(8,128)} %get-tuple-element.28.own_ref.refs_0_), channel_id=1, source_target_pairs={{0,0},{1,2},{2,1},{3,4},{4,3},{5,6},{6,5},{7,8},{8,7},{9,10},{10,9... | collective-permute-start | bytes 1179656 | tf_op jit(solution)/shard_map/ppermute | solution.py:402
  9.3 5.1 %collective-permute-done.5.own_ref.refs_3_ = f32[48,16,128]{2,1,0:T(8,128)S(1)} collective-permute-done((f32[48,16,128]{2,1,0:T(8,128)}, f32[48,16,128]{2,1,0:T(8,128)S(1)}, u32[]{:S(2)}, u32[]{:S(2)}) %collective-permute-start.5) | collective-permute-done | bytes 393248 | tf_op jit(solution)/shard_map/ppermute | solution.py:405
  14.4 4.4 %collective-permute-start.7 = (f32[48,16,128]{2,1,0:T(8,128)S(1)}, f32[48,16,128]{2,1,0:T(8,128)S(1)}, u32[]{:S(2)}, u32[]{:S(2)}) collective-permute-start(f32[48,16,128]{2,1,0:T(8,128)S(1)} %collective-permute-done.5.own_ref.refs_3_), channel_id=1, source_target_pairs={{0,0},{1,2},{2,1},{3,4},{4,3},{5,6},{6,5},{7,8},{8,7},{9,10},{10,9... | collective-permute-start | bytes 1179656 | tf_op jit(solution)/shard_map/ppermute | solution.py:402
  18.8 0.1 collective-permute-start.6
  18.9 0.0 copy-start.2
  19.0 0.1 stack.39.flags
  19.1 0.0 collective-permute-done.first_ref.refs_1_
  19.1 0.7 copy-done.2
  19.7 0.0 copy-start
  19.7 1.0 %copy-done = f32[48,16,128]{2,1,0:T(8,128)S(1)} copy-done((f32[48,16,128]{2,1,0:T(8,128)S(1)}, f32[48,16,128]{2,1,0:T(8,128)}, u32[]{:S(2)}) %copy-start) | copy-done | bytes 393240
  20.7 1.5 %shard_map.141 = (f32[8,640]{1,0:T(8,128)S(1)}, bf16[128,2048]{1,0:T(8,128)(2,1)S(1)}, bf16[128,2048]{1,0:T(8,128)(2,1)S(1)}, bf16[128,2048]{1,0:T(8,128)(2,1)S(1)}) custom-call(s32[5]{0:T(128)S(1)} %stack.39.flags, f32[48,16,128]{2,1,0:T(8,128)S(1)} %copy-done, f32[48,16,128]{2,1,0:T(8,128)S(1)} %collective-permute-done.first_ref.refs_1_, ...), custom_call_target="tpu_custom_call" | custom-call | tf_op jit(solution)/shard_map/pallas_call | solution.py:275
  22.2 0.0 collective-permute-done.1.second_ref.refs_2_
  22.2 1.0 %shard_map.142 = (f32[8,2048]{1,0:T(8,128)S(1)}, bf16[128,2048]{1,0:T(8,128)(2,1)S(1)}) custom-call(s32[5]{0:T(128)S(1)} %stack.39.flags, f32[8,640]{1,0:T(8,128)S(1)} %get-tuple-element.30.part_ref, f32[48,16,128]{2,1,0:T(8,128)S(1)} %collective-permute-done.1.second_ref.refs_2_, f32[8,1408]{1,0:T(8,128)S(1)} %copy-done.2), custom_call_target="tpu_custom_call" | custom-call | tf_op jit(solution)/shard_map/pallas_call | solution.py:275
  23.3 1.3 %collective-permute-start.2 = (f32[8,2048]{1,0:T(8,128)S(1)}, f32[8,2048]{1,0:T(8,128)S(1)}, u32[]{:S(2)}, u32[]{:S(2)}) collective-permute-start(f32[8,2048]{1,0:T(8,128)S(1)} %get-tuple-element.31.refs_0_.refs_6_), channel_id=1, source_target_pairs={{16,0},{0,16},{17,1},{1,17},{18,2},{2,18},{19,3},{3,19},{20,4},{4,... | collective-permute-start | bytes 196616 | tf_op jit(solution)/shard_map/ppermute | solution.py:405
  24.6 1.9 %collective-permute-done.2.refs_1_.mail_ref.refs_7_ = f32[8,2048]{1,0:T(8,128)S(1)} collective-permute-done((f32[8,2048]{1,0:T(8,128)S(1)}, f32[8,2048]{1,0:T(8,128)S(1)}, u32[]{:S(2)}, u32[]{:S(2)}) %collective-permute-start.2) | collective-permute-done | bytes 65568 | tf_op jit(solution)/shard_map/ppermute | solution.py:405
  26.4 0.9 %shard_map.143 = (f32[2,8,640]{2,1,0:T(8,128)S(1)}, f32[2,8,768]{2,1,0:T(8,128)S(1)}, f32[2,8,768]{2,1,0:T(8,128)S(1)}) custom-call(s32[5]{0:T(128)S(1)} %stack.39.flags, f32[8,2048]{1,0:T(8,128)S(1)} %get-tuple-element.31.refs_0_.refs_6_, f32[8,2048]{1,0:T(8,128)S(1)} %collective-permute-done.2.refs_1_.mail_ref.refs_7_), custom_call_target="tpu_custom_call" | custom-call | tf_op jit(solution)/shard_map/pallas_call | solution.py:275
  27.3 1.7 %collective-permute-start.3 = (f32[2,8,768]{2,1,0:T(8,128)S(1)}, f32[2,8,768]{2,1,0:T(8,128)S(1)}, u32[]{:S(2)}, u32[]{:S(2)}) collective-permute-start(f32[2,8,768]{2,1,0:T(8,128)S(1)} %get-tuple-element.33.sent_first), channel_id=1, source_target_pairs={{0,1},{1,0},{2,3},{3,2},{4,5},{5,4},{6,7},{7,6},{8,9},{9,8},{10,11... | collective-permute-start | bytes 147464 | tf_op jit(solution)/shard_map/ppermute | solution.py:402
  29.0 0.0 copy-start.1
  29.0 3.2 %collective-permute-start.4 = (f32[2,8,768]{2,1,0:T(8,128)S(1)}, f32[2,8,768]{2,1,0:T(8,128)S(1)}, u32[]{:S(2)}, u32[]{:S(2)}) collective-permute-start(f32[2,8,768]{2,1,0:T(8,128)S(1)} %get-tuple-element.34.sent_second), channel_id=1, source_target_pairs={{0,0},{1,2},{2,1},{3,4},{4,3},{5,6},{6,5},{7,8},{8,7},{9,10},{10,9... | collective-permute-start | bytes 147464 | tf_op jit(solution)/shard_map/ppermute | solution.py:402
  32.2 0.0 collective-permute-done.7.second_ref.refs_5_
  32.3 0.0 collective-permute-done.6.first_ref.refs_4_
  32.3 1.0 %shard_map.144 = (bf16[128,2048]{1,0:T(8,128)(2,1)S(1)}, bf16[128,2048]{1,0:T(8,128)(2,1)S(1)}, bf16[128,2048]{1,0:T(8,128)(2,1)S(1)}, bf16[128,2048]{1,0:T(8,128)(2,1)S(1)}) custom-call(s32[5]{0:T(128)S(1)} %stack.39.flags, f32[48,16,128]{2,1,0:T(8,128)S(1)} %collective-permute-done.5.own_ref.refs_3_, ...), custom_call_target="tpu_custom_call" | custom-call | tf_op jit(solution)/shard_map/pallas_call | solution.py:275
  33.3 0.0 collective-permute-done.3.got_first
  33.3 1.3 %collective-permute-done.4.got_second = f32[2,8,768]{2,1,0:T(8,128)S(1)} collective-permute-done((f32[2,8,768]{2,1,0:T(8,128)S(1)}, f32[2,8,768]{2,1,0:T(8,128)S(1)}, u32[]{:S(2)}, u32[]{:S(2)}) %collective-permute-start.4) | collective-permute-done | bytes 49184 | tf_op jit(solution)/shard_map/ppermute | solution.py:402
  34.6 0.0 copy-done.1
  34.6 2.9 %shard_map.145 = (f32[2,3,3,16,128]{4,3,2,1,0:T(8,128)S(1)}, f32[16,1,128]{2,1,0:T(1,128)S(1)}) custom-call(s32[5]{0:T(128)S(1)} %stack.39.flags, f32[2,8,640]{2,1,0:T(8,128)S(1)} %get-tuple-element.32.section_ref, f32[2,8,768]{2,1,0:T(8,128)S(1)} %get-tuple-element.33.sent_first, f32[2,8,768]{2,1,0:T(8,128)S(1)} %get-tuple-element.34.sent_second, ...), custom_call_target="tpu_custom_call" | custom-call | tf_op jit(solution)/shard_map/pallas_call | solution.py:275
  37.5 11.5 %all_to_all.10.part_ref = f32[16,1,128]{2,1,0:T(1,128)S(1)} all-to-all(f32[16,1,128]{2,1,0:T(1,128)S(1)} %get-tuple-element.43), channel_id=1, replica_groups=mesh['gz'=2,'xy'=16] {'xy'}, dimensions={0} | all-to-all | bytes 16384 | tf_op jit(solution)/shard_map/all_to_all | solution.py:716
  49.0 2.6 %shard_map.146 = (f32[2,3,3,16,128]{4,3,2,1,0:T(8,128)S(1)}, f32[2,3,3,16,128]{4,3,2,1,0:T(8,128)S(1)}, f32[2,8,640]{2,1,0:T(8,128)S(1)}, f32[2,8,768]{2,1,0:T(8,128)S(1)}, f32[2,8,768]{2,1,0:T(8,128)S(1)}) custom-call(s32[5]{0:T(128)S(1)} %stack.39.flags, f32[16,1,128]{2,1,0:T(1,128)S(1)} %all_to_all.10.part_ref, ...), custom_call_target="tpu_custom_call" | custom-call | tf_op jit(solution)/shard_map/pallas_call | solution.py:275
  51.6 0.8 %collective-permute-start.8 = (f32[2,8,768]{2,1,0:T(8,128)S(1)}, f32[2,8,768]{2,1,0:T(8,128)S(1)}, u32[]{:S(2)}, u32[]{:S(2)}) collective-permute-start(f32[2,8,768]{2,1,0:T(8,128)S(1)} %get-tuple-element.46.sent_first), channel_id=1, source_target_pairs={{0,1},{1,0},{2,3},{3,2},{4,5},{5,4},{6,7},{7,6},{8,9},{9,8},{10,11... | collective-permute-start | bytes 147464 | tf_op jit(solution)/shard_map/ppermute | solution.py:402
  52.4 2.0 %collective-permute-start.9 = (f32[2,8,768]{2,1,0:T(8,128)S(1)}, f32[2,8,768]{2,1,0:T(8,128)S(1)}, u32[]{:S(2)}, u32[]{:S(2)}) collective-permute-start(f32[2,8,768]{2,1,0:T(8,128)S(1)} %get-tuple-element.47.sent_second), channel_id=1, source_target_pairs={{0,0},{1,2},{2,1},{3,4},{4,3},{5,6},{6,5},{7,8},{8,7},{9,10},{10,9... | collective-permute-start | bytes 147464 | tf_op jit(solution)/shard_map/ppermute | solution.py:402
  54.4 0.0 collective-permute-done.8.got_first
  54.4 3.3 %collective-permute-done.9.got_second = f32[2,8,768]{2,1,0:T(8,128)S(1)} collective-permute-done((f32[2,8,768]{2,1,0:T(8,128)S(1)}, f32[2,8,768]{2,1,0:T(8,128)S(1)}, u32[]{:S(2)}, u32[]{:S(2)}) %collective-permute-start.9) | collective-permute-done | bytes 49184 | tf_op jit(solution)/shard_map/ppermute | solution.py:402
  57.8 2.9 %shard_map.147 = (f32[2,3,3,16,128]{4,3,2,1,0:T(8,128)S(1)}, f32[16,1,128]{2,1,0:T(1,128)S(1)}) custom-call(s32[5]{0:T(128)S(1)} %stack.39.flags, f32[2,8,640]{2,1,0:T(8,128)S(1)} %get-tuple-element.45.section_ref, f32[2,8,768]{2,1,0:T(8,128)S(1)} %get-tuple-element.46.sent_first, f32[2,8,768]{2,1,0:T(8,128)S(1)} %get-tuple-element.47.sent_second, ...), custom_call_target="tpu_custom_call" | custom-call | tf_op jit(solution)/shard_map/pallas_call | solution.py:275
  60.7 8.4 %all_to_all.11.part_ref = f32[16,1,128]{2,1,0:T(1,128)S(1)} all-to-all(f32[16,1,128]{2,1,0:T(1,128)S(1)} %get-tuple-element.49), channel_id=1, replica_groups=mesh['gz'=2,'xy'=16] {'xy'}, dimensions={0} | all-to-all | bytes 16384 | tf_op jit(solution)/shard_map/all_to_all | solution.py:716
  69.2 2.9 %shard_map.148 = (f32[3,16,128]{2,1,0:T(8,128)}, f32[6,4,128]{2,1,0:T(4,128)}) custom-call(s32[5]{0:T(128)S(1)} %stack.39.flags, f32[16,1,128]{2,1,0:T(1,128)S(1)} %all_to_all.11.part_ref, f32[2,3,3,16,128]{4,3,2,1,0:T(8,128)S(1)} %get-tuple-element.50.grad_ref, f32[48,16,128]{2,1,0:T(8,128)S(1)} %copy-done.1, ...), custom_call_target="tpu_custom_call" | custom-call | tf_op jit(solution)/shard_map/pallas_call | solution.py:275
Async XLA Ops:
  3.2 11.2 %collective-permute-start.5 = (f32[48,16,128]{2,1,0:T(8,128)}, f32[48,16,128]{2,1,0:T(8,128)S(1)}, u32[]{:S(2)}, u32[]{:S(2)}) collective-permute-start(f32[48,16,128]{2,1,0:T(8,128)} %get-tuple-element.28.own_ref.refs_0_), channel_id=1, source_target_pairs={{16,0},{0,16},{17,1},{1,17},{18,2},{2,18},{19,3},{3,19},{20,4},{4,... | collective-permute-start | bytes 1179656 | tf_op jit(solution)/shard_map/ppermute | solution.py:405
  5.3 13.7 %collective-permute-start = (f32[48,16,128]{2,1,0:T(8,128)}, f32[48,16,128]{2,1,0:T(8,128)S(1)}, u32[]{:S(2)}, u32[]{:S(2)}) collective-permute-start(f32[48,16,128]{2,1,0:T(8,128)} %get-tuple-element.28.own_ref.refs_0_), channel_id=1, source_target_pairs={{0,1},{1,0},{2,3},{3,2},{4,5},{5,4},{6,7},{7,6},{8,9},{9,8},{10,11... | collective-permute-start | bytes 1179656 | tf_op jit(solution)/shard_map/ppermute | solution.py:402
  6.3 15.9 %collective-permute-start.1 = (f32[48,16,128]{2,1,0:T(8,128)}, f32[48,16,128]{2,1,0:T(8,128)S(1)}, u32[]{:S(2)}, u32[]{:S(2)}) collective-permute-start(f32[48,16,128]{2,1,0:T(8,128)} %get-tuple-element.28.own_ref.refs_0_), channel_id=1, source_target_pairs={{0,0},{1,2},{2,1},{3,4},{4,3},{5,6},{6,5},{7,8},{8,7},{9,10},{10,9... | collective-permute-start | bytes 1179656 | tf_op jit(solution)/shard_map/ppermute | solution.py:402
  14.4 17.9 %collective-permute-start.7 = (f32[48,16,128]{2,1,0:T(8,128)S(1)}, f32[48,16,128]{2,1,0:T(8,128)S(1)}, u32[]{:S(2)}, u32[]{:S(2)}) collective-permute-start(f32[48,16,128]{2,1,0:T(8,128)S(1)} %collective-permute-done.5.own_ref.refs_3_), channel_id=1, source_target_pairs={{0,0},{1,2},{2,1},{3,4},{4,3},{5,6},{6,5},{7,8},{8,7},{9,10},{10,9... | collective-permute-start | bytes 1179656 | tf_op jit(solution)/shard_map/ppermute | solution.py:402
  18.8 13.4 %collective-permute-start.6 = (f32[48,16,128]{2,1,0:T(8,128)S(1)}, f32[48,16,128]{2,1,0:T(8,128)S(1)}, u32[]{:S(2)}, u32[]{:S(2)}) collective-permute-start(f32[48,16,128]{2,1,0:T(8,128)S(1)} %collective-permute-done.5.own_ref.refs_3_), channel_id=1, source_target_pairs={{0,1},{1,0},{2,3},{3,2},{4,5},{5,4},{6,7},{7,6},{8,9},{9,8},{10,11... | collective-permute-start | bytes 1179656 | tf_op jit(solution)/shard_map/ppermute | solution.py:402
  18.9 0.8 %copy-start.2 = (f32[8,1408]{1,0:T(8,128)S(1)}, f32[8,1408]{1,0:T(8,128)}, u32[]{:S(2)}) copy-start(f32[8,1408]{1,0:T(8,128)} %get-tuple-element.29.sphere_ref) | copy-start | bytes 135172
  19.7 1.0 %copy-start = (f32[48,16,128]{2,1,0:T(8,128)S(1)}, f32[48,16,128]{2,1,0:T(8,128)}, u32[]{:S(2)}) copy-start(f32[48,16,128]{2,1,0:T(8,128)} %get-tuple-element.28.own_ref.refs_0_) | copy-start | bytes 1179652
  23.3 3.2 %collective-permute-start.2 = (f32[8,2048]{1,0:T(8,128)S(1)}, f32[8,2048]{1,0:T(8,128)S(1)}, u32[]{:S(2)}, u32[]{:S(2)}) collective-permute-start(f32[8,2048]{1,0:T(8,128)S(1)} %get-tuple-element.31.refs_0_.refs_6_), channel_id=1, source_target_pairs={{16,0},{0,16},{17,1},{1,17},{18,2},{2,18},{19,3},{3,19},{20,4},{4,... | collective-permute-start | bytes 196616 | tf_op jit(solution)/shard_map/ppermute | solution.py:405
  27.3 6.0 %collective-permute-start.3 = (f32[2,8,768]{2,1,0:T(8,128)S(1)}, f32[2,8,768]{2,1,0:T(8,128)S(1)}, u32[]{:S(2)}, u32[]{:S(2)}) collective-permute-start(f32[2,8,768]{2,1,0:T(8,128)S(1)} %get-tuple-element.33.sent_first), channel_id=1, source_target_pairs={{0,1},{1,0},{2,3},{3,2},{4,5},{5,4},{6,7},{7,6},{8,9},{9,8},{10,11... | collective-permute-start | bytes 147464 | tf_op jit(solution)/shard_map/ppermute | solution.py:402
  29.0 5.5 %copy-start.1 = (f32[48,16,128]{2,1,0:T(8,128)S(1)}, f32[48,16,128]{2,1,0:T(8,128)}, u32[]{:S(2)}) copy-start(f32[48,16,128]{2,1,0:T(8,128)} %get-tuple-element.28.own_ref.refs_0_) | copy-start | bytes 1179652
  29.0 5.5 %collective-permute-start.4 = (f32[2,8,768]{2,1,0:T(8,128)S(1)}, f32[2,8,768]{2,1,0:T(8,128)S(1)}, u32[]{:S(2)}, u32[]{:S(2)}) collective-permute-start(f32[2,8,768]{2,1,0:T(8,128)S(1)} %get-tuple-element.34.sent_second), channel_id=1, source_target_pairs={{0,0},{1,2},{2,1},{3,4},{4,3},{5,6},{6,5},{7,8},{8,7},{9,10},{10,9... | collective-permute-start | bytes 147464 | tf_op jit(solution)/shard_map/ppermute | solution.py:402
  51.6 2.8 %collective-permute-start.8 = (f32[2,8,768]{2,1,0:T(8,128)S(1)}, f32[2,8,768]{2,1,0:T(8,128)S(1)}, u32[]{:S(2)}, u32[]{:S(2)}) collective-permute-start(f32[2,8,768]{2,1,0:T(8,128)S(1)} %get-tuple-element.46.sent_first), channel_id=1, source_target_pairs={{0,1},{1,0},{2,3},{3,2},{4,5},{5,4},{6,7},{7,6},{8,9},{9,8},{10,11... | collective-permute-start | bytes 147464 | tf_op jit(solution)/shard_map/ppermute | solution.py:402
  52.4 5.4 %collective-permute-start.9 = (f32[2,8,768]{2,1,0:T(8,128)S(1)}, f32[2,8,768]{2,1,0:T(8,128)S(1)}, u32[]{:S(2)}, u32[]{:S(2)}) collective-permute-start(f32[2,8,768]{2,1,0:T(8,128)S(1)} %get-tuple-element.47.sent_second), channel_id=1, source_target_pairs={{0,0},{1,2},{2,1},{3,4},{4,3},{5,6},{6,5},{7,8},{8,7},{9,10},{10,9... | collective-permute-start | bytes 147464 | tf_op jit(solution)/shard_map/ppermute | solution.py:402

commit v2 on v1

--- a/solution.py
+++ b/solution.py
@@ -269,17 +269,15 @@
     return [new_normal, scale * first, scale * second]
 
 
-def call(body, out_shape, operands, scratch=(), space=pltpu.VMEM, room=40):
-    specs = [pl.BlockSpec(memory_space=pltpu.SMEM)]
-    specs += [pl.BlockSpec(memory_space=space)] * (len(operands) - 1)
+def call(body, out_shape, operands, scratch=(), space=pltpu.VMEM, room=40, out_space=pltpu.VMEM):
     return pl.pallas_call(
         body,
         out_shape=[
             jax.ShapeDtypeStruct(*shape) if isinstance(shape[0], tuple) else jax.ShapeDtypeStruct(shape, F32)
             for shape in out_shape
         ],
-        in_specs=specs,
-        out_specs=[pl.BlockSpec(memory_space=pltpu.VMEM)] * len(out_shape),
+        in_specs=[pl.BlockSpec(memory_space=space)] * len(operands),
+        out_specs=[pl.BlockSpec(memory_space=out_space)] * len(out_shape),
         scratch_shapes=list(scratch),
         compiler_params=pltpu.CompilerParams(vmem_limit_bytes=room * 1024 * 1024),
     )(*operands)
@@ -301,36 +299,42 @@
     side_send,
 ):
     slots, cells = lax.axis_size("gz"), lax.axis_size("xy")
-    layer_at, cell_at = lax.axis_index("gz"), lax.axis_index("xy")
     sizes = Sizes(
         jacobian.shape[3], velocity_free.shape[3], layer_send.shape[2], side_send.shape[3], slots, cells
     )
     blocks, window = sizes.blocks, sizes.window
     factors = momentum_factors(ITERS)
 
-    odd = cell_at % 2
-    lower, higher = cell_at > 0, cell_at < cells - 1
-    flags = jnp.stack(
-        [odd, jnp.where(odd == 0, higher, lower), jnp.where(odd == 0, lower, higher)]
-        + [(layer_at + slot) % slots != slots - 1 for slot in range(slots)]
-    ).astype(I32)
+    def flags_here():
+        layer_at, cell_at = lax.axis_index("gz"), lax.axis_index("xy")
+        odd = cell_at % 2
+        lower, higher = cell_at > 0, cell_at < cells - 1
+        places = [odd, jnp.where(odd == 0, higher, lower), jnp.where(odd == 0, lower, higher)]
+        places += [(layer_at + slot) % slots != slots - 1 for slot in range(slots)]
+        return [place.astype(I32) for place in places]
 
     def tiles(array):
         return array.reshape(-1, blocks, LANES)
 
-    def pack_body(counts, *refs):
-        inputs, (out_ref, sphere_ref, *held, semaphores) = refs[:12], refs[12:]
-        targets = [*held[:2], out_ref.at[pl.ds(0, 36)], *held[2:]]
+    def pack_body(*refs):
+        inputs, (contact_out, sphere_out, *held, out_ref, sphere_ref, semaphores) = refs[:13], refs[13:]
+        targets = [*held[:2], out_ref.at[pl.ds(0, NEAR)], *held[2:]]
         copies = [
             pltpu.make_async_copy(source, target, semaphores.at[at])
             for at, (source, target) in enumerate(zip(inputs, targets))
         ]
         for copy in copies:
             copy.start()
-        for copy in copies:
-            copy.wait()
+        jacobian_out = pltpu.make_async_copy(
+            out_ref.at[pl.ds(0, NEAR)], contact_out.at[pl.ds(0, NEAR)], semaphores.at[15]
+        )
+        copies[2].wait()
+        jacobian_out.start()
+        for at, copy in enumerate(copies):
+            if at != 2:
+                copy.wait()
         (free_ref, mass_ref, imp_ref, prev_ref, soft_ref, off_ref, fric_ref, near_ref, far_ref,
-         layer_ref, side_ref) = held
+         layer_ref, side_ref, counts) = held
         lane = lax.broadcasted_iota(I32, (1, LANES), 1)
         rows = [jnp.where(lane < counts[block], 1.0, 0.0) for block in range(blocks)]
         alive = jnp.concatenate(rows, axis=0)
@@ -372,6 +376,18 @@
         for group in range(sizes.window_groups):
             rows = jnp.concatenate([side[:, group * LANES : (group + 1) * LANES]] * 4, axis=0)
             misc(sizes.side_at + group, rows.astype(F32))
+        last = [
+            pltpu.make_async_copy(
+                out_ref.at[pl.ds(NEAR, TILES - NEAR)],
+                contact_out.at[pl.ds(NEAR, TILES - NEAR)],
+                semaphores.at[13],
+            ),
+            pltpu.make_async_copy(sphere_ref, sphere_out, semaphores.at[14]),
+        ]
+        for copy in last:
+            copy.start()
+        for copy in (jacobian_out, *last):
+            copy.wait()
 
     loaded = [
         velocity_free[0, 0].reshape(6, sizes.own_groups, LANES),
@@ -386,15 +402,22 @@
         tiles(body_far[0, 0]),
         layer_send[0],
         side_send[0, 0],
+        block_counts[0, 0],
     ]
     own_contacts, own_spheres = call(
         pack_body,
         [(TILES, blocks, LANES), (8, sizes.sphere_groups * LANES)],
-        [block_counts[0, 0], *loaded],
-        [pltpu.VMEM(array.shape, array.dtype) for at, array in enumerate(loaded) if at != 2]
-        + [pltpu.SemaphoreType.DMA((len(loaded),))],
+        loaded,
+        [pltpu.VMEM(array.shape, array.dtype) for at, array in enumerate(loaded[:-1]) if at != 2]
+        + [
+            pltpu.SMEM(block_counts.shape[2:], I32),
+            pltpu.VMEM((TILES, blocks, LANES), F32),
+            pltpu.VMEM((8, sizes.sphere_groups * LANES), F32),
+            pltpu.SemaphoreType.DMA((len(loaded) + 3,)),
+        ],
         pl.ANY,
         62,
+        pl.ANY,
     )
     to_first, to_second = pair_swaps(cells, 0), pair_swaps(cells, 1)
 
@@ -404,10 +427,8 @@
     def turned(array, step):
         return lax.ppermute(array, "gz", [((i + step) % slots, i) for i in range(slots)])
 
-    contact_arrays = []
-    for slot in range(slots):
-        held = own_contacts if slot == 0 else turned(own_contacts, slot)
-        contact_arrays.append([held, *swap(held, held)])
+    contact_arrays = [[own_contacts, *swap(own_contacts, own_contacts)]]
+    above_contacts = [turned(own_contacts, slot) for slot in range(1, slots)]
 
     def views(refs):
         sets = [[Contacts(refs[3 * s + w]) for w in range(3)] for s in range(slots)]
@@ -486,7 +507,8 @@
         def guess_of(pack):
             return [pack.tile(GUESS + row) for row in range(3)]
 
-        def early(flags, own_ref, first_ref, sphere_ref, out_ref, near_hot, far_hot, first_hot, *scratch):
+        def early(own_ref, first_ref, sphere_ref, out_ref, near_hot, far_hot, first_hot, *scratch):
+            flags = flags_here()
             clear(scratch)
             maps = Maps([Spheres(sphere_ref, sizes)], sizes, flags)
             sets = [Contacts(own_ref), Contacts(first_ref)]
@@ -503,7 +525,8 @@
             for group, value in enumerate(sums):
                 out_ref[:, pl.ds(group * LANES, LANES)] = value
 
-        def late(flags, part_ref, second_ref, sphere_ref, out_ref, hot_ref, *scratch):
+        def late(part_ref, second_ref, sphere_ref, out_ref, hot_ref, *scratch):
+            flags = flags_here()
             clear(scratch)
             maps = Maps([Spheres(sphere_ref, sizes)], sizes, flags)
             pack = Contacts(second_ref)
@@ -517,18 +540,24 @@
 
         own, first, second = contact_arrays[0]
         part, near_hot, far_hot, first_hot = call(
-            early, [(8, sizes.section), hot_shape, hot_shape, hot_shape], [flags, own, first, own_spheres], work[:6]
+            early, [(8, sizes.section), hot_shape, hot_shape, hot_shape], [own, first, own_spheres], work[:6]
         )
+        part, *others = lax.optimization_barrier((part, *above_contacts))
+        seconds = [lax.ppermute(held, "xy", to_second) for held in others]
         mail, second_hot = call(
             late,
             [(8, sizes.mail_groups * LANES), hot_shape],
-            [flags, part, second, own_spheres],
+            [part, second, own_spheres],
             work[4:6],
         )
+        mail, *others = lax.optimization_barrier((mail, *others))
+        for held, got in zip(others, seconds):
+            contact_arrays.append([held, lax.ppermute(held, "xy", to_first), got])
         return mail, [near_hot, far_hot, first_hot, second_hot]
 
     def one_hots(slot, mail):
-        def body(flags, own_ref, first_ref, second_ref, mail_ref, near_hot, *hot_refs):
+        def body(own_ref, first_ref, second_ref, mail_ref, near_hot, *hot_refs):
+            flags = flags_here()
             spheres = {slot: Spheres(mail_ref, sizes, sizes.section_groups)}
             maps = Maps(spheres, sizes, flags)
             packs = [Contacts(ref) for ref in (own_ref, first_ref, second_ref)]
@@ -536,7 +565,7 @@
             for which, pack in enumerate(packs):
                 lay_hot(maps.section_row(slot, which, pack.tile(FAR).astype(I32)), hot_refs[which])
 
-        return call(body, [hot_shape] * 4, [flags, *contact_arrays[slot], mail])
+        return call(body, [hot_shape] * 4, [*contact_arrays[slot], mail])
 
     mail, hots = first_terms()
     mails = [mail] + [turned(mail, step) for step in range(1, slots)]
@@ -545,7 +574,8 @@
     inputs = [*sum(contact_arrays, []), *mails, *hots]
 
     def first_velocities():
-        def body(flags, *refs):
+        def body(*refs):
+            flags = flags_here()
             mail_refs, refs = refs[:slots], refs[slots:]
             spheres = [Spheres(ref, sizes, sizes.section_groups) for ref in mail_refs]
             maps = Maps(spheres, sizes, flags)
@@ -553,10 +583,11 @@
             sums = [joined(sections, spheres, sizes, flags, slot) for slot in range(slots)]
             put_velocities(sums, spheres, maps, flags, *refs)
 
-        return call(body, [section_shape, sent_shape, sent_shape], [flags, *mails])
+        return call(body, [section_shape, sent_shape, sent_shape], [*mails])
 
     def gradients(section, sent, got, state):
-        def body(flags, section_ref, sent_first, sent_second, got_first, got_second, *refs):
+        def body(section_ref, sent_first, sent_second, got_first, got_second, *refs):
+            flags = flags_here()
             sets, spheres, hots, refs = views(refs)
             if state is None:
                 state_ref = None
@@ -639,14 +670,15 @@
         return call(
             body,
             [state_shape, (cells, 1, LANES)],
-            chosen(flags, section, *sent, *got, *inputs, state),
+            chosen(section, *sent, *got, *inputs, state),
             [pltpu.VMEM((slots, 8, sizes.total_groups * LANES), F32), *work, *work],
         )
 
     def updates(parts, grad, state, earlier, factor):
         last = factor is None
 
-        def body(flags, part_ref, grad_ref, *refs):
+        def body(part_ref, grad_ref, *refs):
+            flags = flags_here()
             sets, spheres, hots, refs = views(refs)
             if state is not None:
                 state_ref, earlier_ref, *refs = refs
@@ -707,7 +739,7 @@
             shapes = [(3, blocks, LANES), (6, sizes.own_groups, LANES)]
         else:
             shapes = [state_shape, state_shape, section_shape, sent_shape, sent_shape]
-        return call(body, shapes, chosen(flags, parts, grad, *inputs, state, earlier), [*work, *work])
+        return call(body, shapes, chosen(parts, grad, *inputs, state, earlier), [*work, *work])
 
     state = earlier = None
     section, *sent = first_velocities()

time: 73.1 us -> 66.4 us (0.908)
  Pallas kernels: 18.3 us -> 13.1 us
  waiting for transfers between devices: 11.6 us -> 10.6 us
    pallas_call x9, Pallas kernels: 18.3 us -> 13.1 us  [call(): pl.pallas_call(body, out_shape=[jax.ShapeDtypeStruct(*shape) if isinstanc...]
    ppermute x4 -> x3, starting transfers between devices: 12.7 us -> 8.59 us  [swap(): lax.ppermute(second, 'xy', to_second)]
    ppermute x0 -> x2, starting transfers between devices: none -> 3.96 us  [the longest x1 3.89 us: first_terms(): seconds = [lax.ppermute(held, 'xy', to_second) for held in others]]
    ppermute x2, waiting for transfers between devices: 6.97 us -> 5.4 us  [turned(): lax.ppermute(array, 'gz', [((i + step) % slots, i) for i in range(slots)])]
    ppermute x4 -> x3, starting transfers between devices: 3.52 us -> 2.56 us  [swap(): lax.ppermute(first, 'xy', to_first)]
    ppermute x4 -> x3, waiting for transfers between devices: 4.61 us -> 5.14 us  [swap(): lax.ppermute(second, 'xy', to_second)]
  transfers between devices with their start and end apart: 10 -> 10, of which waited for: 4 -> 4; matrix products, arithmetic and copies ran while one was open for 0% -> 0% of each run, Pallas kernels for 6% -> 3%
where the time goes in v2:
time: 66.4 us; the launch traced here: 65.3 us
  blocking collectives  19.9 us (30%)
  starting transfers between devices  19.1 us (29%)
  Pallas kernels  13.1 us (20%)
  waiting for transfers between devices  10.6 us (16%)
  local copies, waits for them, and re-layouts  1.78 us (3%)
  between operations  0.77 us (1%)
    all_to_all x2, blocking collectives, on_device(): parts = lax.all_to_all(parts, 'xy', 0, 0, tiled=True)  19.9 us
    pallas_call x9, Pallas kernels, call(): pl.pallas_call(body, out_shape=[jax.ShapeDtypeStruct(*shape) if isinstanc...  13.1 us
    ppermute x3, starting transfers between devices, swap(): lax.ppermute(second, 'xy', to_second)  8.59 us
    ppermute x2, waiting for transfers between devices, turned(): lax.ppermute(array, 'gz', [((i + step) % slots, i) for i in range(slots)])  5.4 us
    ppermute x3, waiting for transfers between devices, swap(): lax.ppermute(second, 'xy', to_second)  5.14 us
    ppermute x2, starting transfers between devices, turned(): lax.ppermute(array, 'gz', [((i + step) % slots, i) for i in range(slots)])  4.01 us
    ppermute x1, starting transfers between devices, first_terms(): seconds = [lax.ppermute(held, 'xy', to_second) for held in others]  3.89 us
    ppermute x3, starting transfers between devices, swap(): lax.ppermute(first, 'xy', to_first)  2.56 us
  transfers between devices with their start and end apart: 10, of which 4 were waited for; matrix products, arithmetic and copies ran while one was open for 0% of the time, Pallas kernels for 3%

profile of v2, /device:TPU:1, one launch (start us, length us, event | category | flops | bytes accessed | tf_op | source)
XLA Modules:
  0.0 65.3 jit_solution(15619794691983894009)
XLA Ops:
  0.6 1.9 %shard_map.140 = (f32[48,16,128]{2,1,0:T(8,128)}, f32[8,1408]{1,0:T(8,128)}) custom-call(f32[6,4,128]{2,1,0:T(4,128)} %bitcast.18, f32[2,512]{1,0:T(2,128)} %bitcast.24, f32[36,16,128]{2,1,0:T(8,128)} %bitcast.15, f32[3,16,128]{2,1,0:T(8,128)} %bitcast.16, f32[3,16,128]{2,1,0:T(8,128)} %bitcast.17, f32[1,16,128]{2,1,0:T(8,128)} %bitcast.19, ...), custom_call_target="tpu_custom_call" | custom-call | tf_op jit(solution)/shard_map/pallas_call | solution.py:273
  2.5 0.1 collective-permute-start
  2.7 2.7 %collective-permute-start.1 = (f32[48,16,128]{2,1,0:T(8,128)}, f32[48,16,128]{2,1,0:T(8,128)S(1)}, u32[]{:S(2)}, u32[]{:S(2)}) collective-permute-start(f32[48,16,128]{2,1,0:T(8,128)} %get-tuple-element.32.own_ref.refs_0_), channel_id=1, source_target_pairs={{16,0},{0,16},{17,1},{1,17},{18,2},{2,18},{19,3},{3,19},{20,4},{4,... | collective-permute-start | bytes 1179656 | tf_op jit(solution)/shard_map/ppermute | solution.py:428
  5.4 3.3 %collective-permute-start.2 = (f32[48,16,128]{2,1,0:T(8,128)}, f32[48,16,128]{2,1,0:T(8,128)S(1)}, u32[]{:S(2)}, u32[]{:S(2)}) collective-permute-start(f32[48,16,128]{2,1,0:T(8,128)} %get-tuple-element.32.own_ref.refs_0_), channel_id=1, source_target_pairs={{0,0},{1,2},{2,1},{3,4},{4,3},{5,6},{6,5},{7,8},{8,7},{9,10},{10,9... | collective-permute-start | bytes 1179656 | tf_op jit(solution)/shard_map/ppermute | solution.py:425
  8.7 0.0 collective-permute-done.first_ref.refs_1_
  8.7 0.0 copy-start
  8.7 1.0 %copy-done = f32[48,16,128]{2,1,0:T(8,128)S(1)} copy-done((f32[48,16,128]{2,1,0:T(8,128)S(1)}, f32[48,16,128]{2,1,0:T(8,128)}, u32[]{:S(2)}) %copy-start) | copy-done | bytes 393240
  9.7 0.0 copy-start.2
  9.7 0.8 %copy-done.2 = f32[8,1408]{1,0:T(8,128)S(1)} copy-done((f32[8,1408]{1,0:T(8,128)S(1)}, f32[8,1408]{1,0:T(8,128)}, u32[]{:S(2)}) %copy-start.2) | copy-done | bytes 45080
  10.5 0.9 %shard_map.141 = (f32[8,640]{1,0:T(8,128)S(1)}, bf16[128,2048]{1,0:T(8,128)(2,1)S(1)}, bf16[128,2048]{1,0:T(8,128)(2,1)S(1)}, bf16[128,2048]{1,0:T(8,128)(2,1)S(1)}) custom-call(f32[48,16,128]{2,1,0:T(8,128)S(1)} %copy-done, f32[48,16,128]{2,1,0:T(8,128)S(1)} %collective-permute-done.first_ref.refs_1_, f32[8,1408]{1,0:T(8,128)S(1)} %copy-done.2), custom_call_target="tpu_custom_call" | custom-call | tf_op jit(solution)/shard_map/pallas_call | solution.py:273
  11.4 3.5 %collective-permute-done.1.own_ref.refs_3_ = f32[48,16,128]{2,1,0:T(8,128)S(1)} collective-permute-done((f32[48,16,128]{2,1,0:T(8,128)}, f32[48,16,128]{2,1,0:T(8,128)S(1)}, u32[]{:S(2)}, u32[]{:S(2)}) %collective-permute-start.1) | collective-permute-done | bytes 393248 | tf_op jit(solution)/shard_map/ppermute | solution.py:428
  15.0 3.9 %collective-permute-start.7 = (f32[48,16,128]{2,1,0:T(8,128)S(1)}, f32[48,16,128]{2,1,0:T(8,128)S(1)}, u32[]{:S(2)}, u32[]{:S(2)}) collective-permute-start(f32[48,16,128]{2,1,0:T(8,128)S(1)} %collective-permute-done.1.own_ref.refs_3_), channel_id=1, source_target_pairs={{0,0},{1,2},{2,1},{3,4},{4,3},{5,6},{6,5},{7,8},{8,7},{9,10},{10,9... | collective-permute-start | bytes 1179656 | tf_op jit(solution)/shard_map/ppermute | solution.py:546
  18.9 0.0 collective-permute-done.2.second_ref.refs_2_
  18.9 0.5 shard_map.142
  19.4 0.1 collective-permute-start.6
  19.5 1.3 %collective-permute-start.3 = (f32[8,2048]{1,0:T(8,128)S(1)}, f32[8,2048]{1,0:T(8,128)S(1)}, u32[]{:S(2)}, u32[]{:S(2)}) collective-permute-start(f32[8,2048]{1,0:T(8,128)S(1)} %get-tuple-element.38.refs_0_.refs_6_), channel_id=1, source_target_pairs={{16,0},{0,16},{17,1},{1,17},{18,2},{2,18},{19,3},{3,19},{20,4},{4,... | collective-permute-start | bytes 196616 | tf_op jit(solution)/shard_map/ppermute | solution.py:428
  20.8 1.9 %collective-permute-done.3.refs_1_.mail_ref.refs_7_ = f32[8,2048]{1,0:T(8,128)S(1)} collective-permute-done((f32[8,2048]{1,0:T(8,128)S(1)}, f32[8,2048]{1,0:T(8,128)S(1)}, u32[]{:S(2)}, u32[]{:S(2)}) %collective-permute-start.3) | collective-permute-done | bytes 65568 | tf_op jit(solution)/shard_map/ppermute | solution.py:428
  22.6 0.3 shard_map.143
  23.0 1.6 %collective-permute-start.4 = (f32[2,8,768]{2,1,0:T(8,128)S(1)}, f32[2,8,768]{2,1,0:T(8,128)S(1)}, u32[]{:S(2)}, u32[]{:S(2)}) collective-permute-start(f32[2,8,768]{2,1,0:T(8,128)S(1)} %get-tuple-element.40.sent_first), channel_id=1, source_target_pairs={{0,1},{1,0},{2,3},{3,2},{4,5},{5,4},{6,7},{7,6},{8,9},{9,8},{10,11... | collective-permute-start | bytes 147464 | tf_op jit(solution)/shard_map/ppermute | solution.py:425
  24.6 0.0 copy-start.1
  24.6 3.2 %collective-permute-start.5 = (f32[2,8,768]{2,1,0:T(8,128)S(1)}, f32[2,8,768]{2,1,0:T(8,128)S(1)}, u32[]{:S(2)}, u32[]{:S(2)}) collective-permute-start(f32[2,8,768]{2,1,0:T(8,128)S(1)} %get-tuple-element.41.sent_second), channel_id=1, source_target_pairs={{0,0},{1,2},{2,1},{3,4},{4,3},{5,6},{6,5},{7,8},{8,7},{9,10},{10,9... | collective-permute-start | bytes 147464 | tf_op jit(solution)/shard_map/ppermute | solution.py:425
  27.8 0.0 collective-permute-done.7.second_ref.refs_5_
  27.9 0.0 collective-permute-done.6.first_ref.refs_4_
  27.9 0.5 shard_map.144
  28.3 0.0 collective-permute-done.4.got_first
  28.4 1.8 %collective-permute-done.5.got_second = f32[2,8,768]{2,1,0:T(8,128)S(1)} collective-permute-done((f32[2,8,768]{2,1,0:T(8,128)S(1)}, f32[2,8,768]{2,1,0:T(8,128)S(1)}, u32[]{:S(2)}, u32[]{:S(2)}) %collective-permute-start.5) | collective-permute-done | bytes 49184 | tf_op jit(solution)/shard_map/ppermute | solution.py:425
  30.1 0.0 copy-done.1
  30.1 2.3 %shard_map.145 = (f32[2,3,3,16,128]{4,3,2,1,0:T(8,128)S(1)}, f32[16,1,128]{2,1,0:T(1,128)S(1)}) custom-call(f32[2,8,640]{2,1,0:T(8,128)S(1)} %get-tuple-element.39.section_ref, f32[2,8,768]{2,1,0:T(8,128)S(1)} %get-tuple-element.40.sent_first, f32[2,8,768]{2,1,0:T(8,128)S(1)} %get-tuple-element.41.sent_second, ...), custom_call_target="tpu_custom_call" | custom-call | tf_op jit(solution)/shard_map/pallas_call | solution.py:273
  32.5 11.5 %all_to_all.10.part_ref = f32[16,1,128]{2,1,0:T(1,128)S(1)} all-to-all(f32[16,1,128]{2,1,0:T(1,128)S(1)} %get-tuple-element.51), channel_id=1, replica_groups=mesh['gz'=2,'xy'=16] {'xy'}, dimensions={0} | all-to-all | bytes 16384 | tf_op jit(solution)/shard_map/all_to_all | solution.py:748
  44.0 2.0 %shard_map.146 = (f32[2,3,3,16,128]{4,3,2,1,0:T(8,128)S(1)}, f32[2,3,3,16,128]{4,3,2,1,0:T(8,128)S(1)}, f32[2,8,640]{2,1,0:T(8,128)S(1)}, f32[2,8,768]{2,1,0:T(8,128)S(1)}, f32[2,8,768]{2,1,0:T(8,128)S(1)}) custom-call(f32[16,1,128]{2,1,0:T(1,128)S(1)} %all_to_all.10.part_ref, f32[2,3,3,16,128]{4,3,2,1,0:T(8,128)S(1)} %get-tuple-element.52.grad_ref, ...), custom_call_target="tpu_custom_call" | custom-call | tf_op jit(solution)/shard_map/pallas_call | solution.py:273
  46.0 0.8 %collective-permute-start.8 = (f32[2,8,768]{2,1,0:T(8,128)S(1)}, f32[2,8,768]{2,1,0:T(8,128)S(1)}, u32[]{:S(2)}, u32[]{:S(2)}) collective-permute-start(f32[2,8,768]{2,1,0:T(8,128)S(1)} %get-tuple-element.54.sent_first), channel_id=1, source_target_pairs={{0,1},{1,0},{2,3},{3,2},{4,5},{5,4},{6,7},{7,6},{8,9},{9,8},{10,11... | collective-permute-start | bytes 147464 | tf_op jit(solution)/shard_map/ppermute | solution.py:425
  46.8 2.0 %collective-permute-start.9 = (f32[2,8,768]{2,1,0:T(8,128)S(1)}, f32[2,8,768]{2,1,0:T(8,128)S(1)}, u32[]{:S(2)}, u32[]{:S(2)}) collective-permute-start(f32[2,8,768]{2,1,0:T(8,128)S(1)} %get-tuple-element.55.sent_second), channel_id=1, source_target_pairs={{0,0},{1,2},{2,1},{3,4},{4,3},{5,6},{6,5},{7,8},{8,7},{9,10},{10,9... | collective-permute-start | bytes 147464 | tf_op jit(solution)/shard_map/ppermute | solution.py:425
  48.9 0.0 collective-permute-done.8.got_first
  48.9 3.3 %collective-permute-done.9.got_second = f32[2,8,768]{2,1,0:T(8,128)S(1)} collective-permute-done((f32[2,8,768]{2,1,0:T(8,128)S(1)}, f32[2,8,768]{2,1,0:T(8,128)S(1)}, u32[]{:S(2)}, u32[]{:S(2)}) %collective-permute-start.9) | collective-permute-done | bytes 49184 | tf_op jit(solution)/shard_map/ppermute | solution.py:425
  52.2 2.3 %shard_map.147 = (f32[2,3,3,16,128]{4,3,2,1,0:T(8,128)S(1)}, f32[16,1,128]{2,1,0:T(1,128)S(1)}) custom-call(f32[2,8,640]{2,1,0:T(8,128)S(1)} %get-tuple-element.53.section_ref, f32[2,8,768]{2,1,0:T(8,128)S(1)} %get-tuple-element.54.sent_first, f32[2,8,768]{2,1,0:T(8,128)S(1)} %get-tuple-element.55.sent_second, ...), custom_call_target="tpu_custom_call" | custom-call | tf_op jit(solution)/shard_map/pallas_call | solution.py:273
  54.6 8.4 %all_to_all.11.part_ref = f32[16,1,128]{2,1,0:T(1,128)S(1)} all-to-all(f32[16,1,128]{2,1,0:T(1,128)S(1)} %get-tuple-element.57), channel_id=1, replica_groups=mesh['gz'=2,'xy'=16] {'xy'}, dimensions={0} | all-to-all | bytes 16384 | tf_op jit(solution)/shard_map/all_to_all | solution.py:748
  63.0 2.3 %shard_map.148 = (f32[3,16,128]{2,1,0:T(8,128)}, f32[6,4,128]{2,1,0:T(4,128)}) custom-call(f32[16,1,128]{2,1,0:T(1,128)S(1)} %all_to_all.11.part_ref, f32[2,3,3,16,128]{4,3,2,1,0:T(8,128)S(1)} %get-tuple-element.58.grad_ref, f32[48,16,128]{2,1,0:T(8,128)S(1)} %copy-done.1, f32[48,16,128]{2,1,0:T(8,128)S(1)} %collective-permute-done.first_ref.refs_1_, ...), custom_call_target="tpu_custom_call" | custom-call | tf_op jit(solution)/shard_map/pallas_call | solution.py:273
Async XLA Ops:
  2.5 6.2 %collective-permute-start = (f32[48,16,128]{2,1,0:T(8,128)}, f32[48,16,128]{2,1,0:T(8,128)S(1)}, u32[]{:S(2)}, u32[]{:S(2)}) collective-permute-start(f32[48,16,128]{2,1,0:T(8,128)} %get-tuple-element.32.own_ref.refs_0_), channel_id=1, source_target_pairs={{0,1},{1,0},{2,3},{3,2},{4,5},{5,4},{6,7},{7,6},{8,9},{9,8},{10,11... | collective-permute-start | bytes 1179656 | tf_op jit(solution)/shard_map/ppermute | solution.py:425
  2.7 12.3 %collective-permute-start.1 = (f32[48,16,128]{2,1,0:T(8,128)}, f32[48,16,128]{2,1,0:T(8,128)S(1)}, u32[]{:S(2)}, u32[]{:S(2)}) collective-permute-start(f32[48,16,128]{2,1,0:T(8,128)} %get-tuple-element.32.own_ref.refs_0_), channel_id=1, source_target_pairs={{16,0},{0,16},{17,1},{1,17},{18,2},{2,18},{19,3},{3,19},{20,4},{4,... | collective-permute-start | bytes 1179656 | tf_op jit(solution)/shard_map/ppermute | solution.py:428
  5.4 13.5 %collective-permute-start.2 = (f32[48,16,128]{2,1,0:T(8,128)}, f32[48,16,128]{2,1,0:T(8,128)S(1)}, u32[]{:S(2)}, u32[]{:S(2)}) collective-permute-start(f32[48,16,128]{2,1,0:T(8,128)} %get-tuple-element.32.own_ref.refs_0_), channel_id=1, source_target_pairs={{0,0},{1,2},{2,1},{3,4},{4,3},{5,6},{6,5},{7,8},{8,7},{9,10},{10,9... | collective-permute-start | bytes 1179656 | tf_op jit(solution)/shard_map/ppermute | solution.py:425
  8.7 1.0 %copy-start = (f32[48,16,128]{2,1,0:T(8,128)S(1)}, f32[48,16,128]{2,1,0:T(8,128)}, u32[]{:S(2)}) copy-start(f32[48,16,128]{2,1,0:T(8,128)} %get-tuple-element.32.own_ref.refs_0_) | copy-start | bytes 1179652
  9.7 0.8 %copy-start.2 = (f32[8,1408]{1,0:T(8,128)S(1)}, f32[8,1408]{1,0:T(8,128)}, u32[]{:S(2)}) copy-start(f32[8,1408]{1,0:T(8,128)} %get-tuple-element.33.sphere_ref) | copy-start | bytes 135172
  15.0 12.9 %collective-permute-start.7 = (f32[48,16,128]{2,1,0:T(8,128)S(1)}, f32[48,16,128]{2,1,0:T(8,128)S(1)}, u32[]{:S(2)}, u32[]{:S(2)}) collective-permute-start(f32[48,16,128]{2,1,0:T(8,128)S(1)} %collective-permute-done.1.own_ref.refs_3_), channel_id=1, source_target_pairs={{0,0},{1,2},{2,1},{3,4},{4,3},{5,6},{6,5},{7,8},{8,7},{9,10},{10,9... | collective-permute-start | bytes 1179656 | tf_op jit(solution)/shard_map/ppermute | solution.py:546
  19.4 8.5 %collective-permute-start.6 = (f32[48,16,128]{2,1,0:T(8,128)S(1)}, f32[48,16,128]{2,1,0:T(8,128)S(1)}, u32[]{:S(2)}, u32[]{:S(2)}) collective-permute-start(f32[48,16,128]{2,1,0:T(8,128)S(1)} %collective-permute-done.1.own_ref.refs_3_), channel_id=1, source_target_pairs={{0,1},{1,0},{2,3},{3,2},{4,5},{5,4},{6,7},{7,6},{8,9},{9,8},{10,11... | collective-permute-start | bytes 1179656 | tf_op jit(solution)/shard_map/ppermute | solution.py:555
  19.5 3.2 %collective-permute-start.3 = (f32[8,2048]{1,0:T(8,128)S(1)}, f32[8,2048]{1,0:T(8,128)S(1)}, u32[]{:S(2)}, u32[]{:S(2)}) collective-permute-start(f32[8,2048]{1,0:T(8,128)S(1)} %get-tuple-element.38.refs_0_.refs_6_), channel_id=1, source_target_pairs={{16,0},{0,16},{17,1},{1,17},{18,2},{2,18},{19,3},{3,19},{20,4},{4,... | collective-permute-start | bytes 196616 | tf_op jit(solution)/shard_map/ppermute | solution.py:428
  23.0 5.4 %collective-permute-start.4 = (f32[2,8,768]{2,1,0:T(8,128)S(1)}, f32[2,8,768]{2,1,0:T(8,128)S(1)}, u32[]{:S(2)}, u32[]{:S(2)}) collective-permute-start(f32[2,8,768]{2,1,0:T(8,128)S(1)} %get-tuple-element.40.sent_first), channel_id=1, source_target_pairs={{0,1},{1,0},{2,3},{3,2},{4,5},{5,4},{6,7},{7,6},{8,9},{9,8},{10,11... | collective-permute-start | bytes 147464 | tf_op jit(solution)/shard_map/ppermute | solution.py:425
  24.6 5.5 %copy-start.1 = (f32[48,16,128]{2,1,0:T(8,128)S(1)}, f32[48,16,128]{2,1,0:T(8,128)}, u32[]{:S(2)}) copy-start(f32[48,16,128]{2,1,0:T(8,128)} %get-tuple-element.32.own_ref.refs_0_) | copy-start | bytes 1179652
  24.6 5.5 %collective-permute-start.5 = (f32[2,8,768]{2,1,0:T(8,128)S(1)}, f32[2,8,768]{2,1,0:T(8,128)S(1)}, u32[]{:S(2)}, u32[]{:S(2)}) collective-permute-start(f32[2,8,768]{2,1,0:T(8,128)S(1)} %get-tuple-element.41.sent_second), channel_id=1, source_target_pairs={{0,0},{1,2},{2,1},{3,4},{4,3},{5,6},{6,5},{7,8},{8,7},{9,10},{10,9... | collective-permute-start | bytes 147464 | tf_op jit(solution)/shard_map/ppermute | solution.py:425
  46.0 2.8 %collective-permute-start.8 = (f32[2,8,768]{2,1,0:T(8,128)S(1)}, f32[2,8,768]{2,1,0:T(8,128)S(1)}, u32[]{:S(2)}, u32[]{:S(2)}) collective-permute-start(f32[2,8,768]{2,1,0:T(8,128)S(1)} %get-tuple-element.54.sent_first), channel_id=1, source_target_pairs={{0,1},{1,0},{2,3},{3,2},{4,5},{5,4},{6,7},{7,6},{8,9},{9,8},{10,11... | collective-permute-start | bytes 147464 | tf_op jit(solution)/shard_map/ppermute | solution.py:425
  46.8 5.4 %collective-permute-start.9 = (f32[2,8,768]{2,1,0:T(8,128)S(1)}, f32[2,8,768]{2,1,0:T(8,128)S(1)}, u32[]{:S(2)}, u32[]{:S(2)}) collective-permute-start(f32[2,8,768]{2,1,0:T(8,128)S(1)} %get-tuple-element.55.sent_second), channel_id=1, source_target_pairs={{0,0},{1,2},{2,1},{3,4},{4,3},{5,6},{6,5},{7,8},{8,7},{9,10},{10,9... | collective-permute-start | bytes 147464 | tf_op jit(solution)/shard_map/ppermute | solution.py:425

commit v3 on v2

--- a/solution.py
+++ b/solution.py
@@ -59,13 +59,13 @@
         self.side_at = self.layer_at + self.layer_groups
         self.sphere_groups = self.side_at + self.window_groups
         self.mail_groups = self.section_groups + self.sphere_groups
-        self.sent = own + self.window
+        self.sent_rows = 3 * self.blocks + 8 * self.window_groups
         assert contacts % LANES == own % LANES == layer % LANES == 2 * side % LANES == 0
         assert self.blocks % 8 == 0
 
 
-NEAR, FAR, ALIVE, FRICTION, SOFTNESS, OFFSET, CURRENT, GUESS = 36, 37, 38, 39, 40, 41, 42, 45
-TILES = 48
+FAR, ALIVE, FRICTION, SOFTNESS, CURRENT, GUESS, NEAR_PART, NEAR, OFFSET = 18, 19, 20, 21, 22, 25, 28, 46, 47
+SHARED, TILES = 28, 48
 
 
 class Contacts:
@@ -76,7 +76,7 @@
         return self.ref[which]
 
     def entry(self, row, part, body, rows=slice(None)):
-        return self.ref[12 * row + 6 * part + body, rows, :]
+        return self.ref[6 * row + body + (0 if part else NEAR_PART), rows, :]
 
 
 class Spheres:
@@ -139,6 +139,9 @@
         upper = term.astype(BF16).astype(F32)
         parts_ref[pl.ds(body * blocks, blocks), :] = upper
         parts_ref[pl.ds((8 + body) * blocks, blocks), :] = term - upper
+    gap = jnp.zeros((2 * blocks, LANES), F32)
+    parts_ref[pl.ds(6 * blocks, 2 * blocks), :] = gap
+    parts_ref[pl.ds(14 * blocks, 2 * blocks), :] = gap
     group_of = (index >> 7).astype(F32)
     zeros = jnp.zeros((16, LANES), BF16)
     for block in range(blocks):
@@ -197,7 +200,10 @@
         return jnp.where(self.flags[which] != 0, row, -1)
 
 
-def set_terms(slot, which, pack, value, maps, sizes, hots, scratch, groups, new_hots=False):
+def set_terms(slot, which, pack, value, maps, sizes, hots, scratch, groups, new_hots=False, live=None):
+    rows = slice(0, live)
+    columns = pl.ds(0, (live or sizes.blocks) * LANES)
+    value = [v[rows] for v in value]
     far_hot, near_hot = hots
     parts_ref, spread_ref, near_parts, near_spread = scratch
     far = maps.section_row(slot, which, pack.tile(FAR).astype(I32))
@@ -208,15 +214,15 @@
     result = {}
     for part, index, wanted, hot_ref, to_parts, to_spread in todo:
         terms = [
-            pack.entry(0, part, body) * value[0]
-            + pack.entry(1, part, body) * value[1]
-            + pack.entry(2, part, body) * value[2]
+            pack.entry(0, part, body, rows) * value[0]
+            + pack.entry(1, part, body, rows) * value[1]
+            + pack.entry(2, part, body, rows) * value[2]
             for body in range(6)
         ]
         if new_hots:
             lay_hot(index, hot_ref)
-        lay_terms(terms, index, wanted, to_parts, to_spread)
-        sums = summed(to_spread[pl.ds(0, 16 * len(wanted)), :], hot_ref[...])
+        lay_terms(terms, index[rows], wanted, to_parts, to_spread)
+        sums = summed(to_spread[pl.ds(0, 16 * len(wanted)), columns], hot_ref[:, columns])
         for group, total in zip(wanted, sums):
             result[group] = result[group] + total if group in result else total
     return [result[group] for group in groups]
@@ -227,33 +233,37 @@
 
 
 def joined(sections, spheres, sizes, flags, slot):
-    own = sections[slot][: sizes.own_groups]
+    own = [sections[slot][group] for group in range(sizes.own_groups)]
     if sizes.slots > 1:
         below = (slot + sizes.slots - 1) % sizes.slots
-        upper = [jnp.where(flags[3 + below] != 0, v, 0.0) for v in sections[below][-sizes.layer_groups :]]
+        above = [sections[below][group] for group in range(sizes.own_groups, sizes.section_groups)]
+        upper = [jnp.where(flags[3 + below] != 0, value, 0.0) for value in above]
         lists = [spheres[slot].layer_list(group) - 1 for group in range(sizes.layer_groups)]
         own = added([own, put_columns(upper, lists, sizes.own_groups)])
     return own
 
 
-def rows_of(pack, near_rows, far_rows, far_index):
-    near_index = pack.tile(NEAR).astype(I32)
-    near_groups, far_groups = len(near_rows(0)), len(far_rows(0))
+def rows_of(pack, part, table, index):
+    groups = len(table(0))
     halves = []
-    for at in range(0, near_index.shape[0], 8):
+    for at in range(0, index.shape[0], 8):
         rows = slice(at, at + 8)
+        place = places(index[rows], groups)
         totals = [None] * 3
-        for part, table, place in (
-            (0, near_rows, places(near_index[rows], near_groups)),
-            (1, far_rows, places(far_index[rows], far_groups)),
-        ):
-            for body in range(6):
-                picked = gather(table(body), place)
-                for row in range(3):
-                    term = pack.entry(row, part, body, rows) * picked
-                    totals[row] = term if totals[row] is None else totals[row] + term
+        for body in range(6):
+            picked = gather(table(body), place)
+            for row in range(3):
+                term = pack.entry(row, part, body, rows) * picked
+                totals[row] = term if totals[row] is None else totals[row] + term
         halves.append(totals)
     return [jnp.concatenate([half[row] for half in halves], axis=0) for row in range(3)]
+
+
+def rows_from(ref, slot, start, count):
+    def rows(body):
+        return [ref[slot, pl.ds(body, 1), pl.ds(start + g * LANES, LANES)] for g in range(count)]
+
+    return rows
 
 
 def cone_project(impulse_value, cone_friction):
@@ -317,22 +327,25 @@
         return array.reshape(-1, blocks, LANES)
 
     def pack_body(*refs):
-        inputs, (contact_out, sphere_out, *held, out_ref, sphere_ref, semaphores) = refs[:13], refs[13:]
-        targets = [*held[:2], out_ref.at[pl.ds(0, NEAR)], *held[2:]]
-        copies = [
-            pltpu.make_async_copy(source, target, semaphores.at[at])
-            for at, (source, target) in enumerate(zip(inputs, targets))
-        ]
-        for copy in copies:
+        inputs, (contact_out, shared_out, sphere_out, *held, out_ref, sphere_ref, semaphores) = refs[:13], refs[13:]
+        moves = list(zip([*inputs[:2], *inputs[3:]], held))
+        for row in range(3):
+            near, far = pl.ds(12 * row, 6), pl.ds(12 * row + 6, 6)
+            moves.append((inputs[2].at[far], out_ref.at[pl.ds(6 * row, 6)]))
+            moves.append((inputs[2].at[near], out_ref.at[pl.ds(NEAR_PART + 6 * row, 6)]))
+        count = len(moves)
+        ends = [(0, FAR), (FAR, SHARED), (NEAR_PART, NEAR), (NEAR, TILES)]
+        for start, end in ends:
+            moves.append((out_ref.at[pl.ds(start, end - start)], contact_out.at[pl.ds(start, end - start)]))
+        for start, end in ends[:2]:
+            moves.append((out_ref.at[pl.ds(start, end - start)], shared_out.at[pl.ds(start, end - start)]))
+        moves.append((sphere_ref, sphere_out))
+        copies = [pltpu.make_async_copy(*move, semaphores.at[at]) for at, move in enumerate(moves)]
+        arrays, jacobians, out = copies[: count - 6], copies[count - 6 : count], copies[count:]
+        for copy in [*jacobians, *arrays]:
             copy.start()
-        jacobian_out = pltpu.make_async_copy(
-            out_ref.at[pl.ds(0, NEAR)], contact_out.at[pl.ds(0, NEAR)], semaphores.at[15]
-        )
-        copies[2].wait()
-        jacobian_out.start()
-        for at, copy in enumerate(copies):
-            if at != 2:
-                copy.wait()
+        for copy in arrays:
+            copy.wait()
         (free_ref, mass_ref, imp_ref, prev_ref, soft_ref, off_ref, fric_ref, near_ref, far_ref,
          layer_ref, side_ref, counts) = held
         lane = lax.broadcasted_iota(I32, (1, LANES), 1)
@@ -376,17 +389,11 @@
         for group in range(sizes.window_groups):
             rows = jnp.concatenate([side[:, group * LANES : (group + 1) * LANES]] * 4, axis=0)
             misc(sizes.side_at + group, rows.astype(F32))
-        last = [
-            pltpu.make_async_copy(
-                out_ref.at[pl.ds(NEAR, TILES - NEAR)],
-                contact_out.at[pl.ds(NEAR, TILES - NEAR)],
-                semaphores.at[13],
-            ),
-            pltpu.make_async_copy(sphere_ref, sphere_out, semaphores.at[14]),
-        ]
-        for copy in last:
+        for copy in jacobians:
+            copy.wait()
+        for copy in out:
             copy.start()
-        for copy in (jacobian_out, *last):
+        for copy in out:
             copy.wait()
 
     loaded = [
@@ -404,16 +411,16 @@
         side_send[0, 0],
         block_counts[0, 0],
     ]
-    own_contacts, own_spheres = call(
+    own_contacts, own_shared, own_spheres = call(
         pack_body,
-        [(TILES, blocks, LANES), (8, sizes.sphere_groups * LANES)],
+        [(TILES, blocks, LANES), (SHARED, blocks, LANES), (8, sizes.sphere_groups * LANES)],
         loaded,
         [pltpu.VMEM(array.shape, array.dtype) for at, array in enumerate(loaded[:-1]) if at != 2]
         + [
             pltpu.SMEM(block_counts.shape[2:], I32),
             pltpu.VMEM((TILES, blocks, LANES), F32),
             pltpu.VMEM((8, sizes.sphere_groups * LANES), F32),
-            pltpu.SemaphoreType.DMA((len(loaded) + 3,)),
+            pltpu.SemaphoreType.DMA((len(loaded) - 1 + 6 + 7,)),
         ],
         pl.ANY,
         62,
@@ -427,7 +434,7 @@
     def turned(array, step):
         return lax.ppermute(array, "gz", [((i + step) % slots, i) for i in range(slots)])
 
-    contact_arrays = [[own_contacts, *swap(own_contacts, own_contacts)]]
+    contact_arrays = [[own_contacts, *swap(own_shared, own_shared)]]
     above_contacts = [turned(own_contacts, slot) for slot in range(1, slots)]
 
     def views(refs):
@@ -444,7 +451,7 @@
         return [array for array in arrays if array is not None]
 
     state_shape = (slots, 3, 3, blocks, LANES)
-    section_shape, sent_shape = (slots, 8, sizes.section), (slots, 8, sizes.sent)
+    section_shape, sent_shape = (slots, 8, sizes.section), (slots, sizes.sent_rows, LANES)
     hot_shape = ((LANES, sizes.contacts), BF16)
 
     def scratch_of(own):
@@ -460,31 +467,42 @@
             return scratch[base : base + 4]
         return [*scratch[base + 2 + 2 * which : base + 4 + 2 * which], None, None]
 
-    def clear(scratch):
-        gap = jnp.zeros((2 * blocks, LANES), F32)
-        for ref in scratch[::2]:
-            ref[pl.ds(6 * blocks, 2 * blocks), :] = gap
-            ref[pl.ds(14 * blocks, 2 * blocks), :] = gap
-
-    def slot_sections(sets, values, maps, hots, scratch, wanted):
-        clear(scratch)
+    def slot_sections(sets, values, maps, hots, scratch, wanted, section_ref):
+        half = blocks // 2 if blocks % 16 == 0 else blocks
+
+        def fill(s, live):
+            packs = list(zip(sets[s], values[s], hots[s]))
+            terms = [
+                set_terms(
+                    s, w, pack, value, maps, sizes, hot, places_of(scratch, s, w), wanted[s], live=live
+                )
+                for w, (pack, value, hot) in enumerate(packs)
+            ]
+            for group, total in zip(wanted[s], added(terms)):
+                section_ref[s, :, pl.ds(group * LANES, LANES)] = total
+
+        for s, groups in enumerate(wanted):
+            if not groups:
+                continue
+            alive = [pack.tile(ALIVE)[half:] for pack in sets[s]]
+            if half == blocks:
+                fill(s, blocks)
+                continue
+            more = jnp.max(jnp.maximum(jnp.maximum(alive[0], alive[1]), alive[2])) > 0.0
+            pl.when(more)(lambda s=s: fill(s, blocks))
+            pl.when(jnp.logical_not(more))(lambda s=s: fill(s, half))
         return [
-            added(
-                [
-                    set_terms(
-                        s, w, sets[s][w], values[s][w], maps, sizes, hots[s][w], places_of(scratch, s, w), groups
-                    )
-                    for w in range(3)
-                ]
-            )
-            if groups
-            else None
+            {group: section_ref[s, :, pl.ds(group * LANES, LANES)] for group in groups}
             for s, groups in enumerate(wanted)
         ]
 
     every = list(range(sizes.section_groups))
-
-    def put_velocities(sums, spheres, maps, flags, section_ref, first_ref, second_ref):
+    held_sections = pltpu.VMEM(section_shape, F32)
+
+    def window_rows(group):
+        return pl.ds(3 * blocks + 8 * group, 8)
+
+    def put_velocities(sums, spheres, maps, flags, owns, section_ref, first_ref, second_ref):
         velocity = [
             [spheres[s].free(g) + spheres[s].weight(g) * sums[s][g] for g in range(sizes.own_groups)]
             for s in range(slots)
@@ -497,11 +515,15 @@
             for group, value in enumerate(table):
                 section_ref[slot, :, pl.ds(group * LANES, LANES)] = value
             for which, sent_ref in ((1, first_ref), (2, second_ref)):
-                for group, value in enumerate(velocity[slot]):
-                    sent_ref[slot, :, pl.ds(group * LANES, LANES)] = value
                 for group, rows in enumerate(maps.side(slot, which)):
-                    lanes = pl.ds(sizes.own + group * LANES, LANES)
-                    sent_ref[slot, :, lanes] = gather(table, places(rows - 1, sizes.section_groups))
+                    sent_ref[slot, window_rows(group), :] = gather(table, places(rows - 1, sizes.section_groups))
+            pack = owns[slot]
+            rows = rows_from(section_ref, slot, 0, sizes.own_groups)
+            near = rows_of(pack, 0, rows, pack.tile(NEAR).astype(I32))
+            near[0] = near[0] + pack.tile(OFFSET)
+            for row in range(3):
+                first_ref[slot, pl.ds(row * blocks, blocks), :] = near[row]
+                second_ref[slot, pl.ds(row * blocks, blocks), :] = near[row]
 
     def first_terms():
         def guess_of(pack):
@@ -509,7 +531,6 @@
 
         def early(own_ref, first_ref, sphere_ref, out_ref, near_hot, far_hot, first_hot, *scratch):
             flags = flags_here()
-            clear(scratch)
             maps = Maps([Spheres(sphere_ref, sizes)], sizes, flags)
             sets = [Contacts(own_ref), Contacts(first_ref)]
             hots = [(far_hot, near_hot), (first_hot, None)]
@@ -527,7 +548,6 @@
 
         def late(part_ref, second_ref, sphere_ref, out_ref, hot_ref, *scratch):
             flags = flags_here()
-            clear(scratch)
             maps = Maps([Spheres(sphere_ref, sizes)], sizes, flags)
             pack = Contacts(second_ref)
             sums = set_terms(
@@ -542,17 +562,15 @@
         part, near_hot, far_hot, first_hot = call(
             early, [(8, sizes.section), hot_shape, hot_shape, hot_shape], [own, first, own_spheres], work[:6]
         )
-        part, *others = lax.optimization_barrier((part, *above_contacts))
-        seconds = [lax.ppermute(held, "xy", to_second) for held in others]
         mail, second_hot = call(
             late,
             [(8, sizes.mail_groups * LANES), hot_shape],
             [part, second, own_spheres],
             work[4:6],
         )
-        mail, *others = lax.optimization_barrier((mail, *others))
-        for held, got in zip(others, seconds):
-            contact_arrays.append([held, lax.ppermute(held, "xy", to_first), got])
+        mail, *others = lax.optimization_barrier((mail, *above_contacts))
+        for held in others:
+            contact_arrays.append([held, *swap(held[:SHARED], held[:SHARED])])
         return mail, [near_hot, far_hot, first_hot, second_hot]
 
     def one_hots(slot, mail):
@@ -576,14 +594,15 @@
     def first_velocities():
         def body(*refs):
             flags = flags_here()
-            mail_refs, refs = refs[:slots], refs[slots:]
+            mail_refs, own_refs, refs = refs[:slots], refs[slots : 2 * slots], refs[2 * slots :]
             spheres = [Spheres(ref, sizes, sizes.section_groups) for ref in mail_refs]
             maps = Maps(spheres, sizes, flags)
             sections = [[ref[:, pl.ds(group * LANES, LANES)] for group in every] for ref in mail_refs]
             sums = [joined(sections, spheres, sizes, flags, slot) for slot in range(slots)]
-            put_velocities(sums, spheres, maps, flags, *refs)
-
-        return call(body, [section_shape, sent_shape, sent_shape], [*mails])
+            put_velocities(sums, spheres, maps, flags, [Contacts(ref) for ref in own_refs], *refs)
+
+        owns = [contact_arrays[slot][0] for slot in range(slots)]
+        return call(body, [section_shape, sent_shape, sent_shape], [*mails, *owns])
 
     def gradients(section, sent, got, state):
         def body(section_ref, sent_first, sent_second, got_first, got_second, *refs):
@@ -600,19 +619,12 @@
             lane = lax.broadcasted_iota(I32, (8, LANES), 1)
             edge = sizes.side % LANES
 
-            def rows_from(ref, slot, start, count):
-                def rows(body):
-                    return [ref[slot, pl.ds(body, 1), pl.ds(start + g * LANES, LANES)] for g in range(count)]
-
-                return rows
-
             values = []
             for slot in range(slots):
                 low, high = [], []
                 for group in range(sizes.window_groups):
-                    lanes = pl.ds(sizes.own + group * LANES, LANES)
-                    first = jnp.where(flags[1] != 0, got_first[slot, :, lanes], 0.0)
-                    second = jnp.where(flags[2] != 0, got_second[slot, :, lanes], 0.0)
+                    first = jnp.where(flags[1] != 0, got_first[slot, window_rows(group), :], 0.0)
+                    second = jnp.where(flags[2] != 0, got_second[slot, window_rows(group), :], 0.0)
                     low.append(jnp.where(even, second, first))
                     high.append(jnp.where(even, first, second))
                 if edge:
@@ -626,23 +638,24 @@
                 for which, pack in enumerate(sets[slot]):
                     far = pack.tile(FAR).astype(I32)
                     if which == 0:
-                        near_rows = rows_from(table_ref, slot, 0, sizes.own_groups)
-                        far_rows = rows_from(table_ref, slot, 0, sizes.total_groups)
+                        near_ref = sent_first
+                        table = rows_from(table_ref, slot, 0, sizes.total_groups)
                     else:
-                        got_ref = (got_first, got_second)[which - 1]
-                        sent_ref = (sent_first, sent_second)[which - 1]
-                        near_rows = rows_from(got_ref, slot, 0, sizes.own_groups)
-                        far_rows = rows_from(sent_ref, slot, sizes.own, sizes.window_groups)
+                        near_ref = (got_first, got_second)[which - 1]
+                        listed = (sent_first, sent_second)[which - 1]
                         far = maps.window_index(far, which)
-                    contact_rows = rows_of(pack, near_rows, far_rows, far)
+
+                        def table(body, listed=listed):
+                            rows = [pl.ds(3 * blocks + 8 * g + body, 1) for g in range(sizes.window_groups)]
+                            return [listed[slot, row, :] for row in rows]
+
+                    contact_rows = rows_of(pack, 1, table, far)
                     alive, softness = pack.tile(ALIVE), pack.tile(SOFTNESS)
                     grad = []
                     for row in range(3):
                         guess = pack.tile(GUESS + row) if state_ref is None else state_ref[slot, which, row]
-                        value = contact_rows[row] + softness * guess
-                        if row == 0:
-                            value = value + pack.tile(OFFSET)
-                        value = alive * value
+                        near = near_ref[slot, pl.ds(row * blocks, blocks), :]
+                        value = alive * (near + contact_rows[row] + softness * guess)
                         grad_ref[slot, which, row] = value
                         grad.append(value)
                         if which == 0:
@@ -650,7 +663,7 @@
                             soft = soft + softness * value * value
                     slot_values.append(grad)
                 values.append(slot_values)
-            sections = slot_sections(sets, values, maps, hots, scratch, [every] * slots)
+            sections = slot_sections(sets, values, maps, hots, scratch[1:], [every] * slots, scratch[0])
             sums = [joined(sections, spheres, sizes, flags, slot) for slot in range(slots)]
             curve = jnp.sum(soft, axis=0, keepdims=True)
             norm = jnp.sum(norm, axis=0, keepdims=True)
@@ -671,7 +684,7 @@
             body,
             [state_shape, (cells, 1, LANES)],
             chosen(section, *sent, *got, *inputs, state),
-            [pltpu.VMEM((slots, 8, sizes.total_groups * LANES), F32), *work, *work],
+            [pltpu.VMEM((slots, 8, sizes.total_groups * LANES), F32), held_sections, *work, *work],
         )
 
     def updates(parts, grad, state, earlier, factor):
@@ -724,7 +737,7 @@
                 wanted = [[] for _ in range(slots)]
                 wanted[-1] = every[sizes.own_groups :]
                 wanted[0] = every[: sizes.own_groups]
-            sections = slot_sections(sets, values, maps, hots, scratch, wanted)
+            sections = slot_sections(sets, values, maps, hots, scratch[1:], wanted, scratch[0])
             if last:
                 total = joined(sections, spheres, sizes, flags, 0)
                 for group in range(sizes.own_groups):
@@ -733,13 +746,14 @@
                         velocity_ref[body_row, pl.ds(group, 1), :] = value[body_row : body_row + 1]
             else:
                 sums = [joined(sections, spheres, sizes, flags, slot) for slot in range(slots)]
-                put_velocities(sums, spheres, maps, flags, section_ref, first_ref, second_ref)
+                owns = [sets[slot][0] for slot in range(slots)]
+                put_velocities(sums, spheres, maps, flags, owns, section_ref, first_ref, second_ref)
 
         if last:
             shapes = [(3, blocks, LANES), (6, sizes.own_groups, LANES)]
         else:
             shapes = [state_shape, state_shape, section_shape, sent_shape, sent_shape]
-        return call(body, shapes, chosen(parts, grad, *inputs, state, earlier), [*work, *work])
+        return call(body, shapes, chosen(parts, grad, *inputs, state, earlier), [held_sections, *work, *work])
 
     state = earlier = None
     section, *sent = first_velocities()

time: 66.4 us -> 65.5 us (0.986)
  starting transfers between devices: 19.1 us -> 17.4 us
  waiting for transfers between devices: 10.6 us -> 12.3 us
  blocking collectives: 19.9 us -> 19.1 us
    ppermute x3 -> x4, waiting for transfers between devices: 5.14 us -> 9.41 us  [swap(): lax.ppermute(second, 'xy', to_second)]
    ppermute x2 -> x0, starting transfers between devices: 3.96 us -> none  [the longest x1 3.89 us: first_terms(): seconds = [lax.ppermute(held, 'xy', to_second) for held in others]]
    ppermute x3 -> x4, starting transfers between devices: 8.59 us -> 11.4 us  [swap(): lax.ppermute(second, 'xy', to_second)]
    ppermute x2, waiting for transfers between devices: 5.4 us -> 2.83 us  [turned(): lax.ppermute(array, 'gz', [((i + step) % slots, i) for i in range(slots)])]
    ppermute x2, starting transfers between devices: 4.01 us -> 2.49 us  [turned(): lax.ppermute(array, 'gz', [((i + step) % slots, i) for i in range(slots)])]
    ppermute x3 -> x4, starting transfers between devices: 2.56 us -> 3.45 us  [swap(): lax.ppermute(first, 'xy', to_first)]
    all_to_all x2, blocking collectives: 19.9 us -> 19.1 us  [on_device(): parts = lax.all_to_all(parts, 'xy', 0, 0, tiled=True)]
  transfers between devices with their start and end apart: 10 -> 10, of which waited for: 4 -> 4; matrix products, arithmetic and copies ran while one was open for 0% -> 0% of each run, Pallas kernels for 3% -> 4%
where the time goes in v3:
time: 65.5 us; the launch traced here: 64.4 us
  blocking collectives  19.1 us (29%)
  starting transfers between devices  17.4 us (27%)
  Pallas kernels  13 us (20%)
  waiting for transfers between devices  12.3 us (19%)
  local copies, waits for them, and re-layouts  1.8 us (3%)
  between operations  0.78 us (1%)
    all_to_all x2, blocking collectives, on_device(): parts = lax.all_to_all(parts, 'xy', 0, 0, tiled=True)  19.1 us
    pallas_call x9, Pallas kernels, call(): pl.pallas_call(body, out_shape=[jax.ShapeDtypeStruct(*shape) if isinstanc...  13 us
    ppermute x4, starting transfers between devices, swap(): lax.ppermute(second, 'xy', to_second)  11.4 us
    ppermute x4, waiting for transfers between devices, swap(): lax.ppermute(second, 'xy', to_second)  9.41 us
    ppermute x4, starting transfers between devices, swap(): lax.ppermute(first, 'xy', to_first)  3.45 us
    ppermute x2, waiting for transfers between devices, turned(): lax.ppermute(array, 'gz', [((i + step) % slots, i) for i in range(slots)])  2.83 us
    ppermute x2, starting transfers between devices, turned(): lax.ppermute(array, 'gz', [((i + step) % slots, i) for i in range(slots)])  2.49 us
    unnamed x6, local copies, waits for them, and re-layouts  1.78 us
  transfers between devices with their start and end apart: 10, of which 4 were waited for; matrix products, arithmetic and copies ran while one was open for 0% of the time, Pallas kernels for 4%

profile of v3, /device:TPU:1, one launch (start us, length us, event | category | flops | bytes accessed | tf_op | source)
XLA Modules:
  0.0 64.4 jit_solution(12351535060000259012)
XLA Ops:
  0.6 2.1 %shard_map.140 = (f32[48,16,128]{2,1,0:T(8,128)}, f32[28,16,128]{2,1,0:T(8,128)}, f32[8,1408]{1,0:T(8,128)}) custom-call(f32[6,4,128]{2,1,0:T(4,128)} %bitcast.18, f32[2,512]{1,0:T(2,128)} %bitcast.24, f32[36,16,128]{2,1,0:T(8,128)} %bitcast.15, f32[3,16,128]{2,1,0:T(8,128)} %bitcast.16, f32[3,16,128]{2,1,0:T(8,128)} %bitcast.17, f32[1,16,128]{2,1,0:T(8,128)} %bitcast.19, ...), custom_call_target="tpu_custom_call" | custom-call | tf_op jit(solution)/shard_map/pallas_call | solution.py:283
  2.8 2.1 %collective-permute-start.2 = (f32[48,16,128]{2,1,0:T(8,128)}, f32[48,16,128]{2,1,0:T(8,128)S(1)}, u32[]{:S(2)}, u32[]{:S(2)}) collective-permute-start(f32[48,16,128]{2,1,0:T(8,128)} %get-tuple-element.31.own_ref.refs_2_.refs_0_), channel_id=1, source_target_pairs={{16,0},{0,16},{17,1},{1,17},{18,2},{2,18},{19,3},{3,19},{20,4},{4,... | collective-permute-start | bytes 1179656 | tf_op jit(solution)/shard_map/ppermute | solution.py:435
  4.9 1.0 %collective-permute-start = (f32[28,16,128]{2,1,0:T(8,128)}, f32[28,16,128]{2,1,0:T(8,128)S(1)}, u32[]{:S(2)}, u32[]{:S(2)}) collective-permute-start(f32[28,16,128]{2,1,0:T(8,128)} %get-tuple-element.32), channel_id=1, source_target_pairs={{0,1},{1,0},{2,3},{3,2},{4,5},{5,4},{6,7},{7,6},{8,9},{9,8},{10,11... | collective-permute-start | bytes 688136 | tf_op jit(solution)/shard_map/ppermute | solution.py:432
  5.8 3.0 %collective-permute-start.1 = (f32[28,16,128]{2,1,0:T(8,128)}, f32[28,16,128]{2,1,0:T(8,128)S(1)}, u32[]{:S(2)}, u32[]{:S(2)}) collective-permute-start(f32[28,16,128]{2,1,0:T(8,128)} %get-tuple-element.32), channel_id=1, source_target_pairs={{0,0},{1,2},{2,1},{3,4},{4,3},{5,6},{6,5},{7,8},{8,7},{9,10},{10,9... | collective-permute-start | bytes 688136 | tf_op jit(solution)/shard_map/ppermute | solution.py:432
  8.8 0.0 collective-permute-done.first_ref.refs_1_
  8.9 0.0 copy-start
  8.9 1.0 %copy-done = f32[48,16,128]{2,1,0:T(8,128)S(1)} copy-done((f32[48,16,128]{2,1,0:T(8,128)S(1)}, f32[48,16,128]{2,1,0:T(8,128)}, u32[]{:S(2)}) %copy-start) | copy-done | bytes 393240
  9.9 0.0 copy-start.2
  9.9 0.8 %copy-done.2 = f32[8,1408]{1,0:T(8,128)S(1)} copy-done((f32[8,1408]{1,0:T(8,128)S(1)}, f32[8,1408]{1,0:T(8,128)}, u32[]{:S(2)}) %copy-start.2) | copy-done | bytes 45080
  10.6 0.9 %shard_map.141 = (f32[8,640]{1,0:T(8,128)S(1)}, bf16[128,2048]{1,0:T(8,128)(2,1)S(1)}, bf16[128,2048]{1,0:T(8,128)(2,1)S(1)}, bf16[128,2048]{1,0:T(8,128)(2,1)S(1)}) custom-call(f32[48,16,128]{2,1,0:T(8,128)S(1)} %copy-done, f32[28,16,128]{2,1,0:T(8,128)S(1)} %collective-permute-done.first_ref.refs_1_, f32[8,1408]{1,0:T(8,128)S(1)} %copy-done.2), custom_call_target="tpu_custom_call" | custom-call | tf_op jit(solution)/shard_map/pallas_call | solution.py:283
  11.6 0.0 copy-start.1
  11.6 3.0 %collective-permute-done.1.second_ref.refs_2_ = f32[28,16,128]{2,1,0:T(8,128)S(1)} collective-permute-done((f32[28,16,128]{2,1,0:T(8,128)}, f32[28,16,128]{2,1,0:T(8,128)S(1)}, u32[]{:S(2)}, u32[]{:S(2)}) %collective-permute-start.1) | collective-permute-done | bytes 229408 | tf_op jit(solution)/shard_map/ppermute | solution.py:432
  14.6 0.5 shard_map.142
  15.0 0.0 collective-permute-done.2.refs_3_.own_ref
  15.1 4.3 %collective-permute-start.7 = (f32[28,16,128]{2,1,0:T(8,128)S(1)}, f32[28,16,128]{2,1,0:T(8,128)S(1)}, u32[]{:S(2)}, u32[]{:S(2)}) collective-permute-start(f32[28,16,128]{2,1,0:T(8,128)S(1)} %slice.4), channel_id=1, source_target_pairs={{0,0},{1,2},{2,1},{3,4},{4,3},{5,6},{6,5},{7,8},{8,7},{9,10},{10,9... | collective-permute-start | bytes 688136 | tf_op jit(solution)/shard_map/ppermute | solution.py:432
  19.4 0.1 collective-permute-start.6
  19.4 0.4 collective-permute-start.3
  19.8 2.8 %collective-permute-done.3.refs_1_.mail_ref.refs_7_ = f32[8,2048]{1,0:T(8,128)S(1)} collective-permute-done((f32[8,2048]{1,0:T(8,128)S(1)}, f32[8,2048]{1,0:T(8,128)S(1)}, u32[]{:S(2)}, u32[]{:S(2)}) %collective-permute-start.3) | collective-permute-done | bytes 65568 | tf_op jit(solution)/shard_map/ppermute | solution.py:435
  22.6 0.0 copy-done.1
  22.6 0.5 shard_map.143
  23.1 1.6 %collective-permute-start.4 = (f32[2,64,128]{2,1,0:T(8,128)S(1)}, f32[2,64,128]{2,1,0:T(8,128)S(1)}, u32[]{:S(2)}, u32[]{:S(2)}) collective-permute-start(f32[2,64,128]{2,1,0:T(8,128)S(1)} %get-tuple-element.39.sent_first), channel_id=1, source_target_pairs={{0,1},{1,0},{2,3},{3,2},{4,5},{5,4},{6,7},{7,6},{8,9},{9,8},{10,11... | collective-permute-start | bytes 196616 | tf_op jit(solution)/shard_map/ppermute | solution.py:432
  24.8 2.1 %collective-permute-start.5 = (f32[2,64,128]{2,1,0:T(8,128)S(1)}, f32[2,64,128]{2,1,0:T(8,128)S(1)}, u32[]{:S(2)}, u32[]{:S(2)}) collective-permute-start(f32[2,64,128]{2,1,0:T(8,128)S(1)} %get-tuple-element.40.sent_second), channel_id=1, source_target_pairs={{0,0},{1,2},{2,1},{3,4},{4,3},{5,6},{6,5},{7,8},{8,7},{9,10},{10,9... | collective-permute-start | bytes 196616 | tf_op jit(solution)/shard_map/ppermute | solution.py:432
  26.9 0.0 collective-permute-done.7.second_ref.refs_5_
  26.9 0.0 collective-permute-done.6.first_ref.refs_4_
  26.9 0.5 shard_map.144
  27.4 0.0 collective-permute-done.4.got_first
  27.4 2.9 %collective-permute-done.5.got_second = f32[2,64,128]{2,1,0:T(8,128)S(1)} collective-permute-done((f32[2,64,128]{2,1,0:T(8,128)S(1)}, f32[2,64,128]{2,1,0:T(8,128)S(1)}, u32[]{:S(2)}, u32[]{:S(2)}) %collective-permute-start.5) | collective-permute-done | bytes 65568 | tf_op jit(solution)/shard_map/ppermute | solution.py:432
  30.3 2.1 %shard_map.145 = (f32[2,3,3,16,128]{4,3,2,1,0:T(8,128)S(1)}, f32[16,1,128]{2,1,0:T(1,128)S(1)}) custom-call(f32[2,8,640]{2,1,0:T(8,128)S(1)} %get-tuple-element.38.section_ref, f32[2,64,128]{2,1,0:T(8,128)S(1)} %get-tuple-element.39.sent_first, f32[2,64,128]{2,1,0:T(8,128)S(1)} %get-tuple-element.40.sent_second, ...), custom_call_target="tpu_custom_call" | custom-call | tf_op jit(solution)/shard_map/pallas_call | solution.py:283
  32.5 10.7 %all_to_all.10.part_ref = f32[16,1,128]{2,1,0:T(1,128)S(1)} all-to-all(f32[16,1,128]{2,1,0:T(1,128)S(1)} %get-tuple-element.49), channel_id=1, replica_groups=mesh['gz'=2,'xy'=16] {'xy'}, dimensions={0} | all-to-all | bytes 16384 | tf_op jit(solution)/shard_map/all_to_all | solution.py:762
  43.2 2.1 %shard_map.146 = (f32[2,3,3,16,128]{4,3,2,1,0:T(8,128)S(1)}, f32[2,3,3,16,128]{4,3,2,1,0:T(8,128)S(1)}, f32[2,8,640]{2,1,0:T(8,128)S(1)}, f32[2,64,128]{2,1,0:T(8,128)S(1)}, f32[2,64,128]{2,1,0:T(8,128)S(1)}) custom-call(f32[16,1,128]{2,1,0:T(1,128)S(1)} %all_to_all.10.part_ref, f32[2,3,3,16,128]{4,3,2,1,0:T(8,128)S(1)} %get-tuple-element.50.grad_ref, ...), custom_call_target="tpu_custom_call" | custom-call | tf_op jit(solution)/shard_map/pallas_call | solution.py:283
  45.3 0.8 %collective-permute-start.8 = (f32[2,64,128]{2,1,0:T(8,128)S(1)}, f32[2,64,128]{2,1,0:T(8,128)S(1)}, u32[]{:S(2)}, u32[]{:S(2)}) collective-permute-start(f32[2,64,128]{2,1,0:T(8,128)S(1)} %get-tuple-element.52.sent_first), channel_id=1, source_target_pairs={{0,1},{1,0},{2,3},{3,2},{4,5},{5,4},{6,7},{7,6},{8,9},{9,8},{10,11... | collective-permute-start | bytes 196616 | tf_op jit(solution)/shard_map/ppermute | solution.py:432
  46.1 2.0 %collective-permute-start.9 = (f32[2,64,128]{2,1,0:T(8,128)S(1)}, f32[2,64,128]{2,1,0:T(8,128)S(1)}, u32[]{:S(2)}, u32[]{:S(2)}) collective-permute-start(f32[2,64,128]{2,1,0:T(8,128)S(1)} %get-tuple-element.53.sent_second), channel_id=1, source_target_pairs={{0,0},{1,2},{2,1},{3,4},{4,3},{5,6},{6,5},{7,8},{8,7},{9,10},{10,9... | collective-permute-start | bytes 196616 | tf_op jit(solution)/shard_map/ppermute | solution.py:432
  48.1 0.0 collective-permute-done.8.got_first
  48.1 3.5 %collective-permute-done.9.got_second = f32[2,64,128]{2,1,0:T(8,128)S(1)} collective-permute-done((f32[2,64,128]{2,1,0:T(8,128)S(1)}, f32[2,64,128]{2,1,0:T(8,128)S(1)}, u32[]{:S(2)}, u32[]{:S(2)}) %collective-permute-start.9) | collective-permute-done | bytes 65568 | tf_op jit(solution)/shard_map/ppermute | solution.py:432
  51.7 2.1 %shard_map.147 = (f32[2,3,3,16,128]{4,3,2,1,0:T(8,128)S(1)}, f32[16,1,128]{2,1,0:T(1,128)S(1)}) custom-call(f32[2,8,640]{2,1,0:T(8,128)S(1)} %get-tuple-element.51.section_ref, f32[2,64,128]{2,1,0:T(8,128)S(1)} %get-tuple-element.52.sent_first, f32[2,64,128]{2,1,0:T(8,128)S(1)} %get-tuple-element.53.sent_second, ...), custom_call_target="tpu_custom_call" | custom-call | tf_op jit(solution)/shard_map/pallas_call | solution.py:283
  53.8 8.4 %all_to_all.11.part_ref = f32[16,1,128]{2,1,0:T(1,128)S(1)} all-to-all(f32[16,1,128]{2,1,0:T(1,128)S(1)} %get-tuple-element.55), channel_id=1, replica_groups=mesh['gz'=2,'xy'=16] {'xy'}, dimensions={0} | all-to-all | bytes 16384 | tf_op jit(solution)/shard_map/all_to_all | solution.py:762
  62.2 2.2 %shard_map.148 = (f32[3,16,128]{2,1,0:T(8,128)}, f32[6,4,128]{2,1,0:T(4,128)}) custom-call(f32[16,1,128]{2,1,0:T(1,128)S(1)} %all_to_all.11.part_ref, f32[2,3,3,16,128]{4,3,2,1,0:T(8,128)S(1)} %get-tuple-element.56.grad_ref, f32[48,16,128]{2,1,0:T(8,128)S(1)} %copy-done.1, f32[28,16,128]{2,1,0:T(8,128)S(1)} %collective-permute-done.first_ref.refs_1_, ...), custom_call_target="tpu_custom_call" | custom-call | tf_op jit(solution)/shard_map/pallas_call | solution.py:283
  (1 shorter events, 0.0 us)
Async XLA Ops:
  2.8 12.3 %collective-permute-start.2 = (f32[48,16,128]{2,1,0:T(8,128)}, f32[48,16,128]{2,1,0:T(8,128)S(1)}, u32[]{:S(2)}, u32[]{:S(2)}) collective-permute-start(f32[48,16,128]{2,1,0:T(8,128)} %get-tuple-element.31.own_ref.refs_2_.refs_0_), channel_id=1, source_target_pairs={{16,0},{0,16},{17,1},{1,17},{18,2},{2,18},{19,3},{3,19},{20,4},{4,... | collective-permute-start | bytes 1179656 | tf_op jit(solution)/shard_map/ppermute | solution.py:435
  4.9 4.0 %collective-permute-start = (f32[28,16,128]{2,1,0:T(8,128)}, f32[28,16,128]{2,1,0:T(8,128)S(1)}, u32[]{:S(2)}, u32[]{:S(2)}) collective-permute-start(f32[28,16,128]{2,1,0:T(8,128)} %get-tuple-element.32), channel_id=1, source_target_pairs={{0,1},{1,0},{2,3},{3,2},{4,5},{5,4},{6,7},{7,6},{8,9},{9,8},{10,11... | collective-permute-start | bytes 688136 | tf_op jit(solution)/shard_map/ppermute | solution.py:432
  5.8 8.7 %collective-permute-start.1 = (f32[28,16,128]{2,1,0:T(8,128)}, f32[28,16,128]{2,1,0:T(8,128)S(1)}, u32[]{:S(2)}, u32[]{:S(2)}) collective-permute-start(f32[28,16,128]{2,1,0:T(8,128)} %get-tuple-element.32), channel_id=1, source_target_pairs={{0,0},{1,2},{2,1},{3,4},{4,3},{5,6},{6,5},{7,8},{8,7},{9,10},{10,9... | collective-permute-start | bytes 688136 | tf_op jit(solution)/shard_map/ppermute | solution.py:432
  8.9 1.0 %copy-start = (f32[48,16,128]{2,1,0:T(8,128)S(1)}, f32[48,16,128]{2,1,0:T(8,128)}, u32[]{:S(2)}) copy-start(f32[48,16,128]{2,1,0:T(8,128)} %get-tuple-element.31.own_ref.refs_2_.refs_0_) | copy-start | bytes 1179652
  9.9 0.8 %copy-start.2 = (f32[8,1408]{1,0:T(8,128)S(1)}, f32[8,1408]{1,0:T(8,128)}, u32[]{:S(2)}) copy-start(f32[8,1408]{1,0:T(8,128)} %get-tuple-element.33.sphere_ref) | copy-start | bytes 135172
  11.6 11.0 %copy-start.1 = (f32[48,16,128]{2,1,0:T(8,128)S(1)}, f32[48,16,128]{2,1,0:T(8,128)}, u32[]{:S(2)}) copy-start(f32[48,16,128]{2,1,0:T(8,128)} %get-tuple-element.31.own_ref.refs_2_.refs_0_) | copy-start | bytes 1179652
  15.1 11.8 %collective-permute-start.7 = (f32[28,16,128]{2,1,0:T(8,128)S(1)}, f32[28,16,128]{2,1,0:T(8,128)S(1)}, u32[]{:S(2)}, u32[]{:S(2)}) collective-permute-start(f32[28,16,128]{2,1,0:T(8,128)S(1)} %slice.4), channel_id=1, source_target_pairs={{0,0},{1,2},{2,1},{3,4},{4,3},{5,6},{6,5},{7,8},{8,7},{9,10},{10,9... | collective-permute-start | bytes 688136 | tf_op jit(solution)/shard_map/ppermute | solution.py:432
  19.4 7.5 %collective-permute-start.6 = (f32[28,16,128]{2,1,0:T(8,128)S(1)}, f32[28,16,128]{2,1,0:T(8,128)S(1)}, u32[]{:S(2)}, u32[]{:S(2)}) collective-permute-start(f32[28,16,128]{2,1,0:T(8,128)S(1)} %slice.4), channel_id=1, source_target_pairs={{0,1},{1,0},{2,3},{3,2},{4,5},{5,4},{6,7},{7,6},{8,9},{9,8},{10,11... | collective-permute-start | bytes 688136 | tf_op jit(solution)/shard_map/ppermute | solution.py:432
  19.4 3.2 %collective-permute-start.3 = (f32[8,2048]{1,0:T(8,128)S(1)}, f32[8,2048]{1,0:T(8,128)S(1)}, u32[]{:S(2)}, u32[]{:S(2)}) collective-permute-start(f32[8,2048]{1,0:T(8,128)S(1)} %get-tuple-element.36.refs_0_.refs_6_), channel_id=1, source_target_pairs={{16,0},{0,16},{17,1},{1,17},{18,2},{2,18},{19,3},{3,19},{20,4},{4,... | collective-permute-start | bytes 196616 | tf_op jit(solution)/shard_map/ppermute | solution.py:435
  23.1 4.3 %collective-permute-start.4 = (f32[2,64,128]{2,1,0:T(8,128)S(1)}, f32[2,64,128]{2,1,0:T(8,128)S(1)}, u32[]{:S(2)}, u32[]{:S(2)}) collective-permute-start(f32[2,64,128]{2,1,0:T(8,128)S(1)} %get-tuple-element.39.sent_first), channel_id=1, source_target_pairs={{0,1},{1,0},{2,3},{3,2},{4,5},{5,4},{6,7},{7,6},{8,9},{9,8},{10,11... | collective-permute-start | bytes 196616 | tf_op jit(solution)/shard_map/ppermute | solution.py:432
  24.8 5.6 %collective-permute-start.5 = (f32[2,64,128]{2,1,0:T(8,128)S(1)}, f32[2,64,128]{2,1,0:T(8,128)S(1)}, u32[]{:S(2)}, u32[]{:S(2)}) collective-permute-start(f32[2,64,128]{2,1,0:T(8,128)S(1)} %get-tuple-element.40.sent_second), channel_id=1, source_target_pairs={{0,0},{1,2},{2,1},{3,4},{4,3},{5,6},{6,5},{7,8},{8,7},{9,10},{10,9... | collective-permute-start | bytes 196616 | tf_op jit(solution)/shard_map/ppermute | solution.py:432
  45.3 2.8 %collective-permute-start.8 = (f32[2,64,128]{2,1,0:T(8,128)S(1)}, f32[2,64,128]{2,1,0:T(8,128)S(1)}, u32[]{:S(2)}, u32[]{:S(2)}) collective-permute-start(f32[2,64,128]{2,1,0:T(8,128)S(1)} %get-tuple-element.52.sent_first), channel_id=1, source_target_pairs={{0,1},{1,0},{2,3},{3,2},{4,5},{5,4},{6,7},{7,6},{8,9},{9,8},{10,11... | collective-permute-start | bytes 196616 | tf_op jit(solution)/shard_map/ppermute | solution.py:432
  46.1 5.6 %collective-permute-start.9 = (f32[2,64,128]{2,1,0:T(8,128)S(1)}, f32[2,64,128]{2,1,0:T(8,128)S(1)}, u32[]{:S(2)}, u32[]{:S(2)}) collective-permute-start(f32[2,64,128]{2,1,0:T(8,128)S(1)} %get-tuple-element.53.sent_second), channel_id=1, source_target_pairs={{0,0},{1,2},{2,1},{3,4},{4,3},{5,6},{6,5},{7,8},{8,7},{9,10},{10,9... | collective-permute-start | bytes 196616 | tf_op jit(solution)/shard_map/ppermute | solution.py:432

commit v4 on v3

--- a/solution.py
+++ b/solution.py
@@ -69,14 +69,14 @@
 
 
 class Contacts:
-    def __init__(self, ref):
-        self.ref = ref
+    def __init__(self, ref, rest_ref=None):
+        self.ref, self.rest_ref = ref, rest_ref
 
     def tile(self, which):
-        return self.ref[which]
+        return self.ref[which] if which < SHARED else self.rest_ref[which - SHARED]
 
     def entry(self, row, part, body, rows=slice(None)):
-        return self.ref[6 * row + body + (0 if part else NEAR_PART), rows, :]
+        return (self.ref if part else self.rest_ref)[6 * row + body, rows, :]
 
 
 class Spheres:
@@ -327,18 +327,18 @@
         return array.reshape(-1, blocks, LANES)
 
     def pack_body(*refs):
-        inputs, (contact_out, shared_out, sphere_out, *held, out_ref, sphere_ref, semaphores) = refs[:13], refs[13:]
+        inputs, (shared_out, rest_out, sphere_out, *held, out_ref, sphere_ref, semaphores) = refs[:13], refs[13:]
         moves = list(zip([*inputs[:2], *inputs[3:]], held))
         for row in range(3):
             near, far = pl.ds(12 * row, 6), pl.ds(12 * row + 6, 6)
             moves.append((inputs[2].at[far], out_ref.at[pl.ds(6 * row, 6)]))
             moves.append((inputs[2].at[near], out_ref.at[pl.ds(NEAR_PART + 6 * row, 6)]))
         count = len(moves)
-        ends = [(0, FAR), (FAR, SHARED), (NEAR_PART, NEAR), (NEAR, TILES)]
-        for start, end in ends:
-            moves.append((out_ref.at[pl.ds(start, end - start)], contact_out.at[pl.ds(start, end - start)]))
-        for start, end in ends[:2]:
+        for start, end in ((0, FAR), (FAR, SHARED)):
             moves.append((out_ref.at[pl.ds(start, end - start)], shared_out.at[pl.ds(start, end - start)]))
+        for start, end in ((NEAR_PART, NEAR), (NEAR, TILES)):
+            rows = pl.ds(start - SHARED, end - start)
+            moves.append((out_ref.at[pl.ds(start, end - start)], rest_out.at[rows]))
         moves.append((sphere_ref, sphere_out))
         copies = [pltpu.make_async_copy(*move, semaphores.at[at]) for at, move in enumerate(moves)]
         arrays, jacobians, out = copies[: count - 6], copies[count - 6 : count], copies[count:]
@@ -411,16 +411,16 @@
         side_send[0, 0],
         block_counts[0, 0],
     ]
-    own_contacts, own_shared, own_spheres = call(
+    own_shared, own_rest, own_spheres = call(
         pack_body,
-        [(TILES, blocks, LANES), (SHARED, blocks, LANES), (8, sizes.sphere_groups * LANES)],
+        [(SHARED, blocks, LANES), (TILES - SHARED, blocks, LANES), (8, sizes.sphere_groups * LANES)],
         loaded,
         [pltpu.VMEM(array.shape, array.dtype) for at, array in enumerate(loaded[:-1]) if at != 2]
         + [
             pltpu.SMEM(block_counts.shape[2:], I32),
             pltpu.VMEM((TILES, blocks, LANES), F32),
             pltpu.VMEM((8, sizes.sphere_groups * LANES), F32),
-            pltpu.SemaphoreType.DMA((len(loaded) - 1 + 6 + 7,)),
+            pltpu.SemaphoreType.DMA((len(loaded) - 1 + 6 + 5,)),
         ],
         pl.ANY,
         62,
@@ -434,12 +434,16 @@
     def turned(array, step):
         return lax.ppermute(array, "gz", [((i + step) % slots, i) for i in range(slots)])
 
-    contact_arrays = [[own_contacts, *swap(own_shared, own_shared)]]
-    above_contacts = [turned(own_contacts, slot) for slot in range(1, slots)]
+    contact_arrays = [[own_shared, own_rest, *swap(own_shared, own_shared)]]
+    above_shared = [turned(own_shared, slot) for slot in range(1, slots)]
+    above_rest = [turned(own_rest, slot) for slot in range(1, slots)]
+
+    def three(refs):
+        return [Contacts(refs[0], refs[1]), Contacts(refs[2]), Contacts(refs[3])]
 
     def views(refs):
-        sets = [[Contacts(refs[3 * s + w]) for w in range(3)] for s in range(slots)]
-        refs = refs[3 * slots :]
+        sets = [three(refs[4 * s : 4 * s + 4]) for s in range(slots)]
+        refs = refs[4 * slots :]
         spheres = [Spheres(ref, sizes, sizes.section_groups) for ref in refs[:slots]]
         refs = refs[slots:]
         hots = [
@@ -529,10 +533,10 @@
         def guess_of(pack):
             return [pack.tile(GUESS + row) for row in range(3)]
 
-        def early(own_ref, first_ref, sphere_ref, out_ref, near_hot, far_hot, first_hot, *scratch):
+        def early(own_ref, rest_ref, first_ref, sphere_ref, out_ref, near_hot, far_hot, first_hot, *scratch):
             flags = flags_here()
             maps = Maps([Spheres(sphere_ref, sizes)], sizes, flags)
-            sets = [Contacts(own_ref), Contacts(first_ref)]
+            sets = [Contacts(own_ref, rest_ref), Contacts(first_ref)]
             hots = [(far_hot, near_hot), (first_hot, None)]
             sums = added(
                 [
@@ -558,27 +562,27 @@
                 out_ref[:, lanes] = part_ref[:, lanes] + value
             out_ref[:, pl.ds(sizes.section, sizes.sphere_groups * LANES)] = sphere_ref[...]
 
-        own, first, second = contact_arrays[0]
+        own, rest, first, second = contact_arrays[0]
         part, near_hot, far_hot, first_hot = call(
-            early, [(8, sizes.section), hot_shape, hot_shape, hot_shape], [own, first, own_spheres], work[:6]
+            early, [(8, sizes.section), hot_shape, hot_shape, hot_shape], [own, rest, first, own_spheres], work[:6]
         )
+        part, *others = lax.optimization_barrier((part, *above_shared))
+        for held, held_rest in zip(others, above_rest):
+            contact_arrays.append([held, held_rest, *swap(held, held)])
         mail, second_hot = call(
             late,
             [(8, sizes.mail_groups * LANES), hot_shape],
             [part, second, own_spheres],
             work[4:6],
         )
-        mail, *others = lax.optimization_barrier((mail, *above_contacts))
-        for held in others:
-            contact_arrays.append([held, *swap(held[:SHARED], held[:SHARED])])
         return mail, [near_hot, far_hot, first_hot, second_hot]
 
     def one_hots(slot, mail):
-        def body(own_ref, first_ref, second_ref, mail_ref, near_hot, *hot_refs):
+        def body(own_ref, rest_ref, first_ref, second_ref, mail_ref, near_hot, *hot_refs):
             flags = flags_here()
             spheres = {slot: Spheres(mail_ref, sizes, sizes.section_groups)}
             maps = Maps(spheres, sizes, flags)
-            packs = [Contacts(ref) for ref in (own_ref, first_ref, second_ref)]
+            packs = three([own_ref, rest_ref, first_ref, second_ref])
             lay_hot(packs[0].tile(NEAR).astype(I32), near_hot)
             for which, pack in enumerate(packs):
                 lay_hot(maps.section_row(slot, which, pack.tile(FAR).astype(I32)), hot_refs[which])
@@ -594,15 +598,16 @@
     def first_velocities():
         def body(*refs):
             flags = flags_here()
-            mail_refs, own_refs, refs = refs[:slots], refs[slots : 2 * slots], refs[2 * slots :]
+            mail_refs, own_refs, refs = refs[:slots], refs[slots : 3 * slots], refs[3 * slots :]
             spheres = [Spheres(ref, sizes, sizes.section_groups) for ref in mail_refs]
+            owns = [Contacts(*own_refs[2 * slot : 2 * slot + 2]) for slot in range(slots)]
             maps = Maps(spheres, sizes, flags)
             sections = [[ref[:, pl.ds(group * LANES, LANES)] for group in every] for ref in mail_refs]
             sums = [joined(sections, spheres, sizes, flags, slot) for slot in range(slots)]
-            put_velocities(sums, spheres, maps, flags, [Contacts(ref) for ref in own_refs], *refs)
-
-        owns = [contact_arrays[slot][0] for slot in range(slots)]
-        return call(body, [section_shape, sent_shape, sent_shape], [*mails, *owns])
+            put_velocities(sums, spheres, maps, flags, owns, *refs)
+
+        arrays = [array for held in contact_arrays for array in held[:2]]
+        return call(body, [section_shape, sent_shape, sent_shape], [*mails, *arrays])
 
     def gradients(section, sent, got, state):
         def body(section_ref, sent_first, sent_second, got_first, got_second, *refs):

time: 65.5 us -> 63.5 us (0.969)
  waiting for transfers between devices: 12.3 us -> 6.34 us
  blocking collectives: 19.1 us -> 21.3 us
  starting transfers between devices: 17.4 us -> 19.4 us
  Pallas kernels: 13 us -> 11.9 us
  local copies, waits for them, and re-layouts: 1.8 us -> 2.65 us
    ppermute x4, waiting for transfers between devices: 9.41 us -> 4.67 us  [swap(): lax.ppermute(second, 'xy', to_second)]
    all_to_all x2, blocking collectives: 19.1 us -> 21.3 us  [on_device(): parts = lax.all_to_all(parts, 'xy', 0, 0, tiled=True)]
    ppermute x2 -> x3, starting transfers between devices: 2.49 us -> 4.6 us  [turned(): lax.ppermute(array, 'gz', [((i + step) % slots, i) for i in range(slots)])]
    pallas_call x9, Pallas kernels: 13 us -> 11.9 us  [call(): pl.pallas_call(body, out_shape=[jax.ShapeDtypeStruct(*shape) if isinstanc...]
    ppermute x2 -> x3, waiting for transfers between devices: 2.83 us -> 1.66 us  [turned(): lax.ppermute(array, 'gz', [((i + step) % slots, i) for i in range(slots)])]
    unnamed x6 -> x10, local copies, waits for them, and re-layouts: 1.78 us -> 2.65 us
    ppermute x4, starting transfers between devices: 3.45 us -> 2.59 us  [swap(): lax.ppermute(first, 'xy', to_first)]
    ppermute x4, starting transfers between devices: 11.4 us -> 12.2 us  [swap(): lax.ppermute(second, 'xy', to_second)]
  transfers between devices with their start and end apart: 10 -> 11, of which waited for: 4 -> 3; matrix products, arithmetic and copies ran while one was open for 0% -> 0% of each run, Pallas kernels for 4% -> 4%
where the time goes in v4:
time: 63.5 us; the launch traced here: 62.3 us
  blocking collectives  21.3 us (34%)
  starting transfers between devices  19.4 us (31%)
  Pallas kernels  11.9 us (19%)
  waiting for transfers between devices  6.34 us (10%)
  local copies, waits for them, and re-layouts  2.65 us (4%)
  between operations  0.77 us (1%)
    all_to_all x2, blocking collectives, on_device(): parts = lax.all_to_all(parts, 'xy', 0, 0, tiled=True)  21.3 us
    ppermute x4, starting transfers between devices, swap(): lax.ppermute(second, 'xy', to_second)  12.2 us
    pallas_call x9, Pallas kernels, call(): pl.pallas_call(body, out_shape=[jax.ShapeDtypeStruct(*shape) if isinstanc...  11.9 us
    ppermute x4, waiting for transfers between devices, swap(): lax.ppermute(second, 'xy', to_second)  4.67 us
    ppermute x3, starting transfers between devices, turned(): lax.ppermute(array, 'gz', [((i + step) % slots, i) for i in range(slots)])  4.6 us
    unnamed x10, local copies, waits for them, and re-layouts  2.65 us
    ppermute x4, starting transfers between devices, swap(): lax.ppermute(first, 'xy', to_first)  2.59 us
    ppermute x3, waiting for transfers between devices, turned(): lax.ppermute(array, 'gz', [((i + step) % slots, i) for i in range(slots)])  1.66 us
  transfers between devices with their start and end apart: 11, of which 3 were waited for; matrix products, arithmetic and copies ran while one was open for 0% of the time, Pallas kernels for 4%

profile of v4, /device:TPU:1, one launch (start us, length us, event | category | flops | bytes accessed | tf_op | source)
XLA Modules:
  0.0 62.3 jit_solution(7197381946512128570)
XLA Ops:
  0.6 2.0 %shard_map.140 = (f32[28,16,128]{2,1,0:T(8,128)}, f32[20,16,128]{2,1,0:T(8,128)}, f32[8,1408]{1,0:T(8,128)}) custom-call(f32[6,4,128]{2,1,0:T(4,128)} %bitcast.18, f32[2,512]{1,0:T(2,128)} %bitcast.24, f32[36,16,128]{2,1,0:T(8,128)} %bitcast.15, f32[3,16,128]{2,1,0:T(8,128)} %bitcast.16, f32[3,16,128]{2,1,0:T(8,128)} %bitcast.17, f32[1,16,128]{2,1,0:T(8,128)} %bitcast.19, ...), custom_call_target="tpu_custom_call" | custom-call | tf_op jit(solution)/shard_map/pallas_call | solution.py:283
  2.6 0.1 collective-permute-start
  2.8 2.7 %collective-permute-start.1 = (f32[28,16,128]{2,1,0:T(8,128)}, f32[28,16,128]{2,1,0:T(8,128)S(1)}, u32[]{:S(2)}, u32[]{:S(2)}) collective-permute-start(f32[28,16,128]{2,1,0:T(8,128)} %get-tuple-element.31.own_ref.refs_2_.refs_0_), channel_id=1, source_target_pairs={{16,0},{0,16},{17,1},{1,17},{18,2},{2,18},{19,3},{3,19},{20,4},{4,... | collective-permute-start | bytes 688136 | tf_op jit(solution)/shard_map/ppermute | solution.py:435
  5.5 3.3 %collective-permute-start.2 = (f32[28,16,128]{2,1,0:T(8,128)}, f32[28,16,128]{2,1,0:T(8,128)S(1)}, u32[]{:S(2)}, u32[]{:S(2)}) collective-permute-start(f32[28,16,128]{2,1,0:T(8,128)} %get-tuple-element.31.own_ref.refs_2_.refs_0_), channel_id=1, source_target_pairs={{0,0},{1,2},{2,1},{3,4},{4,3},{5,6},{6,5},{7,8},{8,7},{9,10},{10,9... | collective-permute-start | bytes 688136 | tf_op jit(solution)/shard_map/ppermute | solution.py:432
  8.8 0.3 collective-permute-start.4
  9.1 0.0 collective-permute-done.first_ref.refs_2_
  9.1 0.0 copy-start
  9.1 0.9 %copy-done = f32[28,16,128]{2,1,0:T(8,128)S(1)} copy-done((f32[28,16,128]{2,1,0:T(8,128)S(1)}, f32[28,16,128]{2,1,0:T(8,128)}, u32[]{:S(2)}) %copy-start) | copy-done | bytes 229400
  10.0 0.0 copy-start.2
  10.0 0.9 %copy-done.2 = f32[20,16,128]{2,1,0:T(8,128)S(1)} copy-done((f32[20,16,128]{2,1,0:T(8,128)S(1)}, f32[20,16,128]{2,1,0:T(8,128)}, u32[]{:S(2)}) %copy-start.2) | copy-done | bytes 163864
  11.0 0.0 copy-start.4
  11.0 0.8 %copy-done.4 = f32[8,1408]{1,0:T(8,128)S(1)} copy-done((f32[8,1408]{1,0:T(8,128)S(1)}, f32[8,1408]{1,0:T(8,128)}, u32[]{:S(2)}) %copy-start.4) | copy-done | bytes 45080
  11.8 0.0 copy-start.3
  11.8 0.9 %shard_map.141 = (f32[8,640]{1,0:T(8,128)S(1)}, bf16[128,2048]{1,0:T(8,128)(2,1)S(1)}, bf16[128,2048]{1,0:T(8,128)(2,1)S(1)}, bf16[128,2048]{1,0:T(8,128)(2,1)S(1)}) custom-call(f32[28,16,128]{2,1,0:T(8,128)S(1)} %copy-done, f32[20,16,128]{2,1,0:T(8,128)S(1)} %copy-done.2, f32[28,16,128]{2,1,0:T(8,128)S(1)} %collective-permute-done.first_ref.refs_2_, ...), custom_call_target="tpu_custom_call" | custom-call | tf_op jit(solution)/shard_map/pallas_call | solution.py:283
  12.7 0.0 copy-start.1
  12.7 0.0 collective-permute-done.1.refs_4_.own_ref
  12.7 2.9 %collective-permute-start.8 = (f32[28,16,128]{2,1,0:T(8,128)S(1)}, f32[28,16,128]{2,1,0:T(8,128)S(1)}, u32[]{:S(2)}, u32[]{:S(2)}) collective-permute-start(f32[28,16,128]{2,1,0:T(8,128)S(1)} %collective-permute-done.1.refs_4_.own_ref), channel_id=1, source_target_pairs={{0,0},{1,2},{2,1},{3,4},{4,3},{5,6},{6,5},{7,8},{8,7},{9,10},{10,9... | collective-permute-start | bytes 688136 | tf_op jit(solution)/shard_map/ppermute | solution.py:432
  15.6 0.1 collective-permute-start.7
  15.7 0.0 collective-permute-done.2.second_ref.refs_3_
  15.7 0.5 shard_map.142
  16.2 1.6 %collective-permute-start.3 = (f32[8,2048]{1,0:T(8,128)S(1)}, f32[8,2048]{1,0:T(8,128)S(1)}, u32[]{:S(2)}, u32[]{:S(2)}) collective-permute-start(f32[8,2048]{1,0:T(8,128)S(1)} %get-tuple-element.36.refs_0_.refs_8_), channel_id=1, source_target_pairs={{16,0},{0,16},{17,1},{1,17},{18,2},{2,18},{19,3},{3,19},{20,4},{4,... | collective-permute-start | bytes 196616 | tf_op jit(solution)/shard_map/ppermute | solution.py:435
  17.8 0.0 collective-permute-done.4.refs_5_.rest_ref
  17.8 1.7 %collective-permute-done.3.refs_1_.mail_ref.refs_9_ = f32[8,2048]{1,0:T(8,128)S(1)} collective-permute-done((f32[8,2048]{1,0:T(8,128)S(1)}, f32[8,2048]{1,0:T(8,128)S(1)}, u32[]{:S(2)}, u32[]{:S(2)}) %collective-permute-start.3) | collective-permute-done | bytes 65568 | tf_op jit(solution)/shard_map/ppermute | solution.py:435
  19.4 0.0 copy-done.3
  19.4 0.0 copy-done.1
  19.5 0.5 shard_map.143
  19.9 1.6 %collective-permute-start.5 = (f32[2,64,128]{2,1,0:T(8,128)S(1)}, f32[2,64,128]{2,1,0:T(8,128)S(1)}, u32[]{:S(2)}, u32[]{:S(2)}) collective-permute-start(f32[2,64,128]{2,1,0:T(8,128)S(1)} %get-tuple-element.39.sent_first), channel_id=1, source_target_pairs={{0,1},{1,0},{2,3},{3,2},{4,5},{5,4},{6,7},{7,6},{8,9},{9,8},{10,11... | collective-permute-start | bytes 196616 | tf_op jit(solution)/shard_map/ppermute | solution.py:432
  21.5 3.7 %collective-permute-start.6 = (f32[2,64,128]{2,1,0:T(8,128)S(1)}, f32[2,64,128]{2,1,0:T(8,128)S(1)}, u32[]{:S(2)}, u32[]{:S(2)}) collective-permute-start(f32[2,64,128]{2,1,0:T(8,128)S(1)} %get-tuple-element.40.sent_second), channel_id=1, source_target_pairs={{0,0},{1,2},{2,1},{3,4},{4,3},{5,6},{6,5},{7,8},{8,7},{9,10},{10,9... | collective-permute-start | bytes 196616 | tf_op jit(solution)/shard_map/ppermute | solution.py:432
  25.2 0.0 collective-permute-done.8.second_ref.refs_7_
  25.2 0.0 collective-permute-done.7.first_ref.refs_6_
  25.3 0.5 shard_map.144
  25.7 0.0 collective-permute-done.5.got_first
  25.7 1.4 %collective-permute-done.6.got_second = f32[2,64,128]{2,1,0:T(8,128)S(1)} collective-permute-done((f32[2,64,128]{2,1,0:T(8,128)S(1)}, f32[2,64,128]{2,1,0:T(8,128)S(1)}, u32[]{:S(2)}, u32[]{:S(2)}) %collective-permute-start.6) | collective-permute-done | bytes 65568 | tf_op jit(solution)/shard_map/ppermute | solution.py:432
  27.2 1.9 %shard_map.145 = (f32[2,3,3,16,128]{4,3,2,1,0:T(8,128)S(1)}, f32[16,1,128]{2,1,0:T(1,128)S(1)}) custom-call(f32[2,8,640]{2,1,0:T(8,128)S(1)} %get-tuple-element.38.section_ref, f32[2,64,128]{2,1,0:T(8,128)S(1)} %get-tuple-element.39.sent_first, f32[2,64,128]{2,1,0:T(8,128)S(1)} %get-tuple-element.40.sent_second, ...), custom_call_target="tpu_custom_call" | custom-call | tf_op jit(solution)/shard_map/pallas_call | solution.py:283
  29.0 12.3 %all_to_all.10.part_ref = f32[16,1,128]{2,1,0:T(1,128)S(1)} all-to-all(f32[16,1,128]{2,1,0:T(1,128)S(1)} %get-tuple-element.49), channel_id=1, replica_groups=mesh['gz'=2,'xy'=16] {'xy'}, dimensions={0} | all-to-all | bytes 16384 | tf_op jit(solution)/shard_map/all_to_all | solution.py:767
  41.3 1.8 %shard_map.146 = (f32[2,3,3,16,128]{4,3,2,1,0:T(8,128)S(1)}, f32[2,3,3,16,128]{4,3,2,1,0:T(8,128)S(1)}, f32[2,8,640]{2,1,0:T(8,128)S(1)}, f32[2,64,128]{2,1,0:T(8,128)S(1)}, f32[2,64,128]{2,1,0:T(8,128)S(1)}) custom-call(f32[16,1,128]{2,1,0:T(1,128)S(1)} %all_to_all.10.part_ref, f32[2,3,3,16,128]{4,3,2,1,0:T(8,128)S(1)} %get-tuple-element.50.grad_ref, ...), custom_call_target="tpu_custom_call" | custom-call | tf_op jit(solution)/shard_map/pallas_call | solution.py:283
  43.1 0.8 %collective-permute-start.9 = (f32[2,64,128]{2,1,0:T(8,128)S(1)}, f32[2,64,128]{2,1,0:T(8,128)S(1)}, u32[]{:S(2)}, u32[]{:S(2)}) collective-permute-start(f32[2,64,128]{2,1,0:T(8,128)S(1)} %get-tuple-element.52.sent_first), channel_id=1, source_target_pairs={{0,1},{1,0},{2,3},{3,2},{4,5},{5,4},{6,7},{7,6},{8,9},{9,8},{10,11... | collective-permute-start | bytes 196616 | tf_op jit(solution)/shard_map/ppermute | solution.py:432
  43.9 2.3 %collective-permute-start.10 = (f32[2,64,128]{2,1,0:T(8,128)S(1)}, f32[2,64,128]{2,1,0:T(8,128)S(1)}, u32[]{:S(2)}, u32[]{:S(2)}) collective-permute-start(f32[2,64,128]{2,1,0:T(8,128)S(1)} %get-tuple-element.53.sent_second), channel_id=1, source_target_pairs={{0,0},{1,2},{2,1},{3,4},{4,3},{5,6},{6,5},{7,8},{8,7},{9,10},{10,9... | collective-permute-start | bytes 196616 | tf_op jit(solution)/shard_map/ppermute | solution.py:432
  46.3 0.0 collective-permute-done.9.got_first
  46.3 3.2 %collective-permute-done.10.got_second = f32[2,64,128]{2,1,0:T(8,128)S(1)} collective-permute-done((f32[2,64,128]{2,1,0:T(8,128)S(1)}, f32[2,64,128]{2,1,0:T(8,128)S(1)}, u32[]{:S(2)}, u32[]{:S(2)}) %collective-permute-start.10) | collective-permute-done | bytes 65568 | tf_op jit(solution)/shard_map/ppermute | solution.py:432
  49.5 1.9 %shard_map.147 = (f32[2,3,3,16,128]{4,3,2,1,0:T(8,128)S(1)}, f32[16,1,128]{2,1,0:T(1,128)S(1)}) custom-call(f32[2,8,640]{2,1,0:T(8,128)S(1)} %get-tuple-element.51.section_ref, f32[2,64,128]{2,1,0:T(8,128)S(1)} %get-tuple-element.52.sent_first, f32[2,64,128]{2,1,0:T(8,128)S(1)} %get-tuple-element.53.sent_second, ...), custom_call_target="tpu_custom_call" | custom-call | tf_op jit(solution)/shard_map/pallas_call | solution.py:283
  51.4 9.0 %all_to_all.11.part_ref = f32[16,1,128]{2,1,0:T(1,128)S(1)} all-to-all(f32[16,1,128]{2,1,0:T(1,128)S(1)} %get-tuple-element.55), channel_id=1, replica_groups=mesh['gz'=2,'xy'=16] {'xy'}, dimensions={0} | all-to-all | bytes 16384 | tf_op jit(solution)/shard_map/all_to_all | solution.py:767
  60.4 1.9 %shard_map.148 = (f32[3,16,128]{2,1,0:T(8,128)}, f32[6,4,128]{2,1,0:T(4,128)}) custom-call(f32[16,1,128]{2,1,0:T(1,128)S(1)} %all_to_all.11.part_ref, f32[2,3,3,16,128]{4,3,2,1,0:T(8,128)S(1)} %get-tuple-element.56.grad_ref, f32[28,16,128]{2,1,0:T(8,128)S(1)} %copy-done.1, f32[20,16,128]{2,1,0:T(8,128)S(1)} %copy-done.3, ...), custom_call_target="tpu_custom_call" | custom-call | tf_op jit(solution)/shard_map/pallas_call | solution.py:283
Async XLA Ops:
  2.6 6.5 %collective-permute-start = (f32[28,16,128]{2,1,0:T(8,128)}, f32[28,16,128]{2,1,0:T(8,128)S(1)}, u32[]{:S(2)}, u32[]{:S(2)}) collective-permute-start(f32[28,16,128]{2,1,0:T(8,128)} %get-tuple-element.31.own_ref.refs_2_.refs_0_), channel_id=1, source_target_pairs={{0,1},{1,0},{2,3},{3,2},{4,5},{5,4},{6,7},{7,6},{8,9},{9,8},{10,11... | collective-permute-start | bytes 688136 | tf_op jit(solution)/shard_map/ppermute | solution.py:432
  2.8 10.0 %collective-permute-start.1 = (f32[28,16,128]{2,1,0:T(8,128)}, f32[28,16,128]{2,1,0:T(8,128)S(1)}, u32[]{:S(2)}, u32[]{:S(2)}) collective-permute-start(f32[28,16,128]{2,1,0:T(8,128)} %get-tuple-element.31.own_ref.refs_2_.refs_0_), channel_id=1, source_target_pairs={{16,0},{0,16},{17,1},{1,17},{18,2},{2,18},{19,3},{3,19},{20,4},{4,... | collective-permute-start | bytes 688136 | tf_op jit(solution)/shard_map/ppermute | solution.py:435
  5.5 10.2 %collective-permute-start.2 = (f32[28,16,128]{2,1,0:T(8,128)}, f32[28,16,128]{2,1,0:T(8,128)S(1)}, u32[]{:S(2)}, u32[]{:S(2)}) collective-permute-start(f32[28,16,128]{2,1,0:T(8,128)} %get-tuple-element.31.own_ref.refs_2_.refs_0_), channel_id=1, source_target_pairs={{0,0},{1,2},{2,1},{3,4},{4,3},{5,6},{6,5},{7,8},{8,7},{9,10},{10,9... | collective-permute-start | bytes 688136 | tf_op jit(solution)/shard_map/ppermute | solution.py:432
  8.8 9.0 %collective-permute-start.4 = (f32[20,16,128]{2,1,0:T(8,128)}, f32[20,16,128]{2,1,0:T(8,128)S(1)}, u32[]{:S(2)}, u32[]{:S(2)}) collective-permute-start(f32[20,16,128]{2,1,0:T(8,128)} %get-tuple-element.32.rest_ref.refs_3_.refs_1_), channel_id=1, source_target_pairs={{16,0},{0,16},{17,1},{1,17},{18,2},{2,18},{19,3},{3,19},{20,4},{4,... | collective-permute-start | bytes 491528 | tf_op jit(solution)/shard_map/ppermute | solution.py:435
  9.1 0.9 %copy-start = (f32[28,16,128]{2,1,0:T(8,128)S(1)}, f32[28,16,128]{2,1,0:T(8,128)}, u32[]{:S(2)}) copy-start(f32[28,16,128]{2,1,0:T(8,128)} %get-tuple-element.31.own_ref.refs_2_.refs_0_) | copy-start | bytes 688132
  10.0 0.9 %copy-start.2 = (f32[20,16,128]{2,1,0:T(8,128)S(1)}, f32[20,16,128]{2,1,0:T(8,128)}, u32[]{:S(2)}) copy-start(f32[20,16,128]{2,1,0:T(8,128)} %get-tuple-element.32.rest_ref.refs_3_.refs_1_) | copy-start | bytes 491524
  11.0 0.8 %copy-start.4 = (f32[8,1408]{1,0:T(8,128)S(1)}, f32[8,1408]{1,0:T(8,128)}, u32[]{:S(2)}) copy-start(f32[8,1408]{1,0:T(8,128)} %get-tuple-element.33.sphere_ref) | copy-start | bytes 135172
  11.8 7.7 %copy-start.3 = (f32[20,16,128]{2,1,0:T(8,128)S(1)}, f32[20,16,128]{2,1,0:T(8,128)}, u32[]{:S(2)}) copy-start(f32[20,16,128]{2,1,0:T(8,128)} %get-tuple-element.32.rest_ref.refs_3_.refs_1_) | copy-start | bytes 491524
  12.7 6.7 %copy-start.1 = (f32[28,16,128]{2,1,0:T(8,128)S(1)}, f32[28,16,128]{2,1,0:T(8,128)}, u32[]{:S(2)}) copy-start(f32[28,16,128]{2,1,0:T(8,128)} %get-tuple-element.31.own_ref.refs_2_.refs_0_) | copy-start | bytes 688132
  12.7 12.5 %collective-permute-start.8 = (f32[28,16,128]{2,1,0:T(8,128)S(1)}, f32[28,16,128]{2,1,0:T(8,128)S(1)}, u32[]{:S(2)}, u32[]{:S(2)}) collective-permute-start(f32[28,16,128]{2,1,0:T(8,128)S(1)} %collective-permute-done.1.refs_4_.own_ref), channel_id=1, source_target_pairs={{0,0},{1,2},{2,1},{3,4},{4,3},{5,6},{6,5},{7,8},{8,7},{9,10},{10,9... | collective-permute-start | bytes 688136 | tf_op jit(solution)/shard_map/ppermute | solution.py:432
  15.6 9.6 %collective-permute-start.7 = (f32[28,16,128]{2,1,0:T(8,128)S(1)}, f32[28,16,128]{2,1,0:T(8,128)S(1)}, u32[]{:S(2)}, u32[]{:S(2)}) collective-permute-start(f32[28,16,128]{2,1,0:T(8,128)S(1)} %collective-permute-done.1.refs_4_.own_ref), channel_id=1, source_target_pairs={{0,1},{1,0},{2,3},{3,2},{4,5},{5,4},{6,7},{7,6},{8,9},{9,8},{10,11... | collective-permute-start | bytes 688136 | tf_op jit(solution)/shard_map/ppermute | solution.py:432
  16.2 3.3 %collective-permute-start.3 = (f32[8,2048]{1,0:T(8,128)S(1)}, f32[8,2048]{1,0:T(8,128)S(1)}, u32[]{:S(2)}, u32[]{:S(2)}) collective-permute-start(f32[8,2048]{1,0:T(8,128)S(1)} %get-tuple-element.36.refs_0_.refs_8_), channel_id=1, source_target_pairs={{16,0},{0,16},{17,1},{1,17},{18,2},{2,18},{19,3},{3,19},{20,4},{4,... | collective-permute-start | bytes 196616 | tf_op jit(solution)/shard_map/ppermute | solution.py:435
  19.9 5.8 %collective-permute-start.5 = (f32[2,64,128]{2,1,0:T(8,128)S(1)}, f32[2,64,128]{2,1,0:T(8,128)S(1)}, u32[]{:S(2)}, u32[]{:S(2)}) collective-permute-start(f32[2,64,128]{2,1,0:T(8,128)S(1)} %get-tuple-element.39.sent_first), channel_id=1, source_target_pairs={{0,1},{1,0},{2,3},{3,2},{4,5},{5,4},{6,7},{7,6},{8,9},{9,8},{10,11... | collective-permute-start | bytes 196616 | tf_op jit(solution)/shard_map/ppermute | solution.py:432
  21.5 5.6 %collective-permute-start.6 = (f32[2,64,128]{2,1,0:T(8,128)S(1)}, f32[2,64,128]{2,1,0:T(8,128)S(1)}, u32[]{:S(2)}, u32[]{:S(2)}) collective-permute-start(f32[2,64,128]{2,1,0:T(8,128)S(1)} %get-tuple-element.40.sent_second), channel_id=1, source_target_pairs={{0,0},{1,2},{2,1},{3,4},{4,3},{5,6},{6,5},{7,8},{8,7},{9,10},{10,9... | collective-permute-start | bytes 196616 | tf_op jit(solution)/shard_map/ppermute | solution.py:432
  43.1 3.1 %collective-permute-start.9 = (f32[2,64,128]{2,1,0:T(8,128)S(1)}, f32[2,64,128]{2,1,0:T(8,128)S(1)}, u32[]{:S(2)}, u32[]{:S(2)}) collective-permute-start(f32[2,64,128]{2,1,0:T(8,128)S(1)} %get-tuple-element.52.sent_first), channel_id=1, source_target_pairs={{0,1},{1,0},{2,3},{3,2},{4,5},{5,4},{6,7},{7,6},{8,9},{9,8},{10,11... | collective-permute-start | bytes 196616 | tf_op jit(solution)/shard_map/ppermute | solution.py:432
  43.9 5.6 %collective-permute-start.10 = (f32[2,64,128]{2,1,0:T(8,128)S(1)}, f32[2,64,128]{2,1,0:T(8,128)S(1)}, u32[]{:S(2)}, u32[]{:S(2)}) collective-permute-start(f32[2,64,128]{2,1,0:T(8,128)S(1)} %get-tuple-element.53.sent_second), channel_id=1, source_target_pairs={{0,0},{1,2},{2,1},{3,4},{4,3},{5,6},{6,5},{7,8},{8,7},{9,10},{10,9... | collective-permute-start | bytes 196616 | tf_op jit(solution)/shard_map/ppermute | solution.py:432

commit v5 on v4

--- a/solution.py
+++ b/solution.py
@@ -567,14 +567,16 @@
             early, [(8, sizes.section), hot_shape, hot_shape, hot_shape], [own, rest, first, own_spheres], work[:6]
         )
         part, *others = lax.optimization_barrier((part, *above_shared))
-        for held, held_rest in zip(others, above_rest):
-            contact_arrays.append([held, held_rest, *swap(held, held)])
+        seconds = [lax.ppermute(held, "xy", to_second) for held in others]
         mail, second_hot = call(
             late,
             [(8, sizes.mail_groups * LANES), hot_shape],
             [part, second, own_spheres],
             work[4:6],
         )
+        mail, *others = lax.optimization_barrier((mail, *others))
+        for held, held_rest, got in zip(others, above_rest, seconds):
+            contact_arrays.append([held, held_rest, lax.ppermute(held, "xy", to_first), got])
         return mail, [near_hot, far_hot, first_hot, second_hot]
 
     def one_hots(slot, mail):

time: 63.5 us -> 63.4 us (level)
  Pallas kernels: 11.9 us -> 13 us
  blocking collectives: 21.3 us -> 20.4 us
    ppermute x4 -> x3, starting transfers between devices: 12.2 us -> 9.05 us  [swap(): lax.ppermute(second, 'xy', to_second)]
    ppermute x0 -> x2, starting transfers between devices: none -> 2.94 us  [the longest x1 2.86 us: first_terms(): seconds = [lax.ppermute(held, 'xy', to_second) for held in others]]
    pallas_call x9, Pallas kernels: 11.9 us -> 13 us  [call(): pl.pallas_call(body, out_shape=[jax.ShapeDtypeStruct(*shape) if isinstanc...]
    all_to_all x2, blocking collectives: 21.3 us -> 20.4 us  [on_device(): parts = lax.all_to_all(parts, 'xy', 0, 0, tiled=True)]
    ppermute x4 -> x3, waiting for transfers between devices: 4.67 us -> 4.95 us  [swap(): lax.ppermute(second, 'xy', to_second)]
    ppermute x4 -> x3, starting transfers between devices: 2.59 us -> 2.46 us  [swap(): lax.ppermute(first, 'xy', to_first)]
where the time goes in v5:
time: 63.4 us; the launch traced here: 62.5 us
  blocking collectives  20.4 us (32%)
  starting transfers between devices  19 us (30%)
  Pallas kernels  13 us (21%)
  waiting for transfers between devices  6.62 us (10%)
  local copies, waits for them, and re-layouts  2.65 us (4%)
  between operations  0.77 us (1%)
    all_to_all x2, blocking collectives, on_device(): parts = lax.all_to_all(parts, 'xy', 0, 0, tiled=True)  20.4 us
    pallas_call x9, Pallas kernels, call(): pl.pallas_call(body, out_shape=[jax.ShapeDtypeStruct(*shape) if isinstanc...  13 us
    ppermute x3, starting transfers between devices, swap(): lax.ppermute(second, 'xy', to_second)  9.05 us
    ppermute x3, waiting for transfers between devices, swap(): lax.ppermute(second, 'xy', to_second)  4.95 us
    ppermute x3, starting transfers between devices, turned(): lax.ppermute(array, 'gz', [((i + step) % slots, i) for i in range(slots)])  4.61 us
    ppermute x1, starting transfers between devices, first_terms(): seconds = [lax.ppermute(held, 'xy', to_second) for held in others]  2.86 us
    unnamed x10, local copies, waits for them, and re-layouts  2.65 us
    ppermute x3, starting transfers between devices, swap(): lax.ppermute(first, 'xy', to_first)  2.46 us
  transfers between devices with their start and end apart: 11, of which 3 were waited for; matrix products, arithmetic and copies ran while one was open for 0% of the time, Pallas kernels for 4%

profile of v5, /device:TPU:1, one launch (start us, length us, event | category | flops | bytes accessed | tf_op | source)
XLA Modules:
  0.0 62.5 jit_solution(7204038899606428691)
XLA Ops:
  0.6 2.0 %shard_map.140 = (f32[28,16,128]{2,1,0:T(8,128)}, f32[20,16,128]{2,1,0:T(8,128)}, f32[8,1408]{1,0:T(8,128)}) custom-call(f32[6,4,128]{2,1,0:T(4,128)} %bitcast.18, f32[2,512]{1,0:T(2,128)} %bitcast.24, f32[36,16,128]{2,1,0:T(8,128)} %bitcast.15, f32[3,16,128]{2,1,0:T(8,128)} %bitcast.16, f32[3,16,128]{2,1,0:T(8,128)} %bitcast.17, f32[1,16,128]{2,1,0:T(8,128)} %bitcast.19, ...), custom_call_target="tpu_custom_call" | custom-call | tf_op jit(solution)/shard_map/pallas_call | solution.py:283
  2.6 0.1 collective-permute-start
  2.8 2.7 %collective-permute-start.1 = (f32[28,16,128]{2,1,0:T(8,128)}, f32[28,16,128]{2,1,0:T(8,128)S(1)}, u32[]{:S(2)}, u32[]{:S(2)}) collective-permute-start(f32[28,16,128]{2,1,0:T(8,128)} %get-tuple-element.33.own_ref.refs_2_.refs_0_), channel_id=1, source_target_pairs={{16,0},{0,16},{17,1},{1,17},{18,2},{2,18},{19,3},{3,19},{20,4},{4,... | collective-permute-start | bytes 688136 | tf_op jit(solution)/shard_map/ppermute | solution.py:435
  5.5 3.3 %collective-permute-start.2 = (f32[28,16,128]{2,1,0:T(8,128)}, f32[28,16,128]{2,1,0:T(8,128)S(1)}, u32[]{:S(2)}, u32[]{:S(2)}) collective-permute-start(f32[28,16,128]{2,1,0:T(8,128)} %get-tuple-element.33.own_ref.refs_2_.refs_0_), channel_id=1, source_target_pairs={{0,0},{1,2},{2,1},{3,4},{4,3},{5,6},{6,5},{7,8},{8,7},{9,10},{10,9... | collective-permute-start | bytes 688136 | tf_op jit(solution)/shard_map/ppermute | solution.py:432
  8.8 0.3 collective-permute-start.4
  9.1 0.0 collective-permute-done.first_ref.refs_2_
  9.1 0.0 copy-start
  9.1 0.9 %copy-done = f32[28,16,128]{2,1,0:T(8,128)S(1)} copy-done((f32[28,16,128]{2,1,0:T(8,128)S(1)}, f32[28,16,128]{2,1,0:T(8,128)}, u32[]{:S(2)}) %copy-start) | copy-done | bytes 229400
  10.0 0.0 copy-start.2
  10.0 0.9 %copy-done.2 = f32[20,16,128]{2,1,0:T(8,128)S(1)} copy-done((f32[20,16,128]{2,1,0:T(8,128)S(1)}, f32[20,16,128]{2,1,0:T(8,128)}, u32[]{:S(2)}) %copy-start.2) | copy-done | bytes 163864
  11.0 0.0 copy-start.4
  11.0 0.8 %copy-done.4 = f32[8,1408]{1,0:T(8,128)S(1)} copy-done((f32[8,1408]{1,0:T(8,128)S(1)}, f32[8,1408]{1,0:T(8,128)}, u32[]{:S(2)}) %copy-start.4) | copy-done | bytes 45080
  11.8 0.0 copy-start.3
  11.8 0.9 %shard_map.141 = (f32[8,640]{1,0:T(8,128)S(1)}, bf16[128,2048]{1,0:T(8,128)(2,1)S(1)}, bf16[128,2048]{1,0:T(8,128)(2,1)S(1)}, bf16[128,2048]{1,0:T(8,128)(2,1)S(1)}) custom-call(f32[28,16,128]{2,1,0:T(8,128)S(1)} %copy-done, f32[20,16,128]{2,1,0:T(8,128)S(1)} %copy-done.2, f32[28,16,128]{2,1,0:T(8,128)S(1)} %collective-permute-done.first_ref.refs_2_, ...), custom_call_target="tpu_custom_call" | custom-call | tf_op jit(solution)/shard_map/pallas_call | solution.py:283
  12.7 0.0 copy-start.1
  12.7 0.0 collective-permute-done.1.refs_4_.own_ref
  12.7 2.9 %collective-permute-start.8 = (f32[28,16,128]{2,1,0:T(8,128)S(1)}, f32[28,16,128]{2,1,0:T(8,128)S(1)}, u32[]{:S(2)}, u32[]{:S(2)}) collective-permute-start(f32[28,16,128]{2,1,0:T(8,128)S(1)} %collective-permute-done.1.refs_4_.own_ref), channel_id=1, source_target_pairs={{0,0},{1,2},{2,1},{3,4},{4,3},{5,6},{6,5},{7,8},{8,7},{9,10},{10,9... | collective-permute-start | bytes 688136 | tf_op jit(solution)/shard_map/ppermute | solution.py:570
  15.6 0.0 collective-permute-done.2.second_ref.refs_3_
  15.6 0.5 shard_map.142
  16.1 0.1 collective-permute-start.7
  16.2 1.6 %collective-permute-start.3 = (f32[8,2048]{1,0:T(8,128)S(1)}, f32[8,2048]{1,0:T(8,128)S(1)}, u32[]{:S(2)}, u32[]{:S(2)}) collective-permute-start(f32[8,2048]{1,0:T(8,128)S(1)} %get-tuple-element.40.refs_0_.refs_8_), channel_id=1, source_target_pairs={{16,0},{0,16},{17,1},{1,17},{18,2},{2,18},{19,3},{3,19},{20,4},{4,... | collective-permute-start | bytes 196616 | tf_op jit(solution)/shard_map/ppermute | solution.py:435
  17.8 0.0 collective-permute-done.4.refs_5_.rest_ref
  17.8 1.7 %collective-permute-done.3.refs_1_.mail_ref.refs_9_ = f32[8,2048]{1,0:T(8,128)S(1)} collective-permute-done((f32[8,2048]{1,0:T(8,128)S(1)}, f32[8,2048]{1,0:T(8,128)S(1)}, u32[]{:S(2)}, u32[]{:S(2)}) %collective-permute-start.3) | collective-permute-done | bytes 65568 | tf_op jit(solution)/shard_map/ppermute | solution.py:435
  19.4 0.0 copy-done.3
  19.4 0.0 copy-done.1
  19.5 0.5 shard_map.143
  19.9 1.6 %collective-permute-start.5 = (f32[2,64,128]{2,1,0:T(8,128)S(1)}, f32[2,64,128]{2,1,0:T(8,128)S(1)}, u32[]{:S(2)}, u32[]{:S(2)}) collective-permute-start(f32[2,64,128]{2,1,0:T(8,128)S(1)} %get-tuple-element.43.sent_first), channel_id=1, source_target_pairs={{0,1},{1,0},{2,3},{3,2},{4,5},{5,4},{6,7},{7,6},{8,9},{9,8},{10,11... | collective-permute-start | bytes 196616 | tf_op jit(solution)/shard_map/ppermute | solution.py:432
  21.5 3.7 %collective-permute-start.6 = (f32[2,64,128]{2,1,0:T(8,128)S(1)}, f32[2,64,128]{2,1,0:T(8,128)S(1)}, u32[]{:S(2)}, u32[]{:S(2)}) collective-permute-start(f32[2,64,128]{2,1,0:T(8,128)S(1)} %get-tuple-element.44.sent_second), channel_id=1, source_target_pairs={{0,0},{1,2},{2,1},{3,4},{4,3},{5,6},{6,5},{7,8},{8,7},{9,10},{10,9... | collective-permute-start | bytes 196616 | tf_op jit(solution)/shard_map/ppermute | solution.py:432
  25.2 0.0 collective-permute-done.8.second_ref.refs_7_
  25.2 0.0 collective-permute-done.7.first_ref.refs_6_
  25.2 0.5 shard_map.144
  25.7 0.0 collective-permute-done.5.got_first
  25.7 1.4 %collective-permute-done.6.got_second = f32[2,64,128]{2,1,0:T(8,128)S(1)} collective-permute-done((f32[2,64,128]{2,1,0:T(8,128)S(1)}, f32[2,64,128]{2,1,0:T(8,128)S(1)}, u32[]{:S(2)}, u32[]{:S(2)}) %collective-permute-start.6) | collective-permute-done | bytes 65568 | tf_op jit(solution)/shard_map/ppermute | solution.py:432
  27.1 2.2 %shard_map.145 = (f32[2,3,3,16,128]{4,3,2,1,0:T(8,128)S(1)}, f32[16,1,128]{2,1,0:T(1,128)S(1)}) custom-call(f32[2,8,640]{2,1,0:T(8,128)S(1)} %get-tuple-element.42.section_ref, f32[2,64,128]{2,1,0:T(8,128)S(1)} %get-tuple-element.43.sent_first, f32[2,64,128]{2,1,0:T(8,128)S(1)} %get-tuple-element.44.sent_second, ...), custom_call_target="tpu_custom_call" | custom-call | tf_op jit(solution)/shard_map/pallas_call | solution.py:283
  29.3 12.0 %all_to_all.10.part_ref = f32[16,1,128]{2,1,0:T(1,128)S(1)} all-to-all(f32[16,1,128]{2,1,0:T(1,128)S(1)} %get-tuple-element.53), channel_id=1, replica_groups=mesh['gz'=2,'xy'=16] {'xy'}, dimensions={0} | all-to-all | bytes 16384 | tf_op jit(solution)/shard_map/all_to_all | solution.py:769
  41.3 2.1 %shard_map.146 = (f32[2,3,3,16,128]{4,3,2,1,0:T(8,128)S(1)}, f32[2,3,3,16,128]{4,3,2,1,0:T(8,128)S(1)}, f32[2,8,640]{2,1,0:T(8,128)S(1)}, f32[2,64,128]{2,1,0:T(8,128)S(1)}, f32[2,64,128]{2,1,0:T(8,128)S(1)}) custom-call(f32[16,1,128]{2,1,0:T(1,128)S(1)} %all_to_all.10.part_ref, f32[2,3,3,16,128]{4,3,2,1,0:T(8,128)S(1)} %get-tuple-element.54.grad_ref, ...), custom_call_target="tpu_custom_call" | custom-call | tf_op jit(solution)/shard_map/pallas_call | solution.py:283
  43.4 0.8 %collective-permute-start.9 = (f32[2,64,128]{2,1,0:T(8,128)S(1)}, f32[2,64,128]{2,1,0:T(8,128)S(1)}, u32[]{:S(2)}, u32[]{:S(2)}) collective-permute-start(f32[2,64,128]{2,1,0:T(8,128)S(1)} %get-tuple-element.56.sent_first), channel_id=1, source_target_pairs={{0,1},{1,0},{2,3},{3,2},{4,5},{5,4},{6,7},{7,6},{8,9},{9,8},{10,11... | collective-permute-start | bytes 196616 | tf_op jit(solution)/shard_map/ppermute | solution.py:432
  44.2 2.0 %collective-permute-start.10 = (f32[2,64,128]{2,1,0:T(8,128)S(1)}, f32[2,64,128]{2,1,0:T(8,128)S(1)}, u32[]{:S(2)}, u32[]{:S(2)}) collective-permute-start(f32[2,64,128]{2,1,0:T(8,128)S(1)} %get-tuple-element.57.sent_second), channel_id=1, source_target_pairs={{0,0},{1,2},{2,1},{3,4},{4,3},{5,6},{6,5},{7,8},{8,7},{9,10},{10,9... | collective-permute-start | bytes 196616 | tf_op jit(solution)/shard_map/ppermute | solution.py:432
  46.2 0.0 collective-permute-done.9.got_first
  46.2 3.5 %collective-permute-done.10.got_second = f32[2,64,128]{2,1,0:T(8,128)S(1)} collective-permute-done((f32[2,64,128]{2,1,0:T(8,128)S(1)}, f32[2,64,128]{2,1,0:T(8,128)S(1)}, u32[]{:S(2)}, u32[]{:S(2)}) %collective-permute-start.10) | collective-permute-done | bytes 65568 | tf_op jit(solution)/shard_map/ppermute | solution.py:432
  49.7 2.1 %shard_map.147 = (f32[2,3,3,16,128]{4,3,2,1,0:T(8,128)S(1)}, f32[16,1,128]{2,1,0:T(1,128)S(1)}) custom-call(f32[2,8,640]{2,1,0:T(8,128)S(1)} %get-tuple-element.55.section_ref, f32[2,64,128]{2,1,0:T(8,128)S(1)} %get-tuple-element.56.sent_first, f32[2,64,128]{2,1,0:T(8,128)S(1)} %get-tuple-element.57.sent_second, ...), custom_call_target="tpu_custom_call" | custom-call | tf_op jit(solution)/shard_map/pallas_call | solution.py:283
  51.9 8.4 %all_to_all.11.part_ref = f32[16,1,128]{2,1,0:T(1,128)S(1)} all-to-all(f32[16,1,128]{2,1,0:T(1,128)S(1)} %get-tuple-element.59), channel_id=1, replica_groups=mesh['gz'=2,'xy'=16] {'xy'}, dimensions={0} | all-to-all | bytes 16384 | tf_op jit(solution)/shard_map/all_to_all | solution.py:769
  60.3 2.2 %shard_map.148 = (f32[3,16,128]{2,1,0:T(8,128)}, f32[6,4,128]{2,1,0:T(4,128)}) custom-call(f32[16,1,128]{2,1,0:T(1,128)S(1)} %all_to_all.11.part_ref, f32[2,3,3,16,128]{4,3,2,1,0:T(8,128)S(1)} %get-tuple-element.60.grad_ref, f32[28,16,128]{2,1,0:T(8,128)S(1)} %copy-done.1, f32[20,16,128]{2,1,0:T(8,128)S(1)} %copy-done.3, ...), custom_call_target="tpu_custom_call" | custom-call | tf_op jit(solution)/shard_map/pallas_call | solution.py:283
Async XLA Ops:
  2.6 6.5 %collective-permute-start = (f32[28,16,128]{2,1,0:T(8,128)}, f32[28,16,128]{2,1,0:T(8,128)S(1)}, u32[]{:S(2)}, u32[]{:S(2)}) collective-permute-start(f32[28,16,128]{2,1,0:T(8,128)} %get-tuple-element.33.own_ref.refs_2_.refs_0_), channel_id=1, source_target_pairs={{0,1},{1,0},{2,3},{3,2},{4,5},{5,4},{6,7},{7,6},{8,9},{9,8},{10,11... | collective-permute-start | bytes 688136 | tf_op jit(solution)/shard_map/ppermute | solution.py:432
  2.8 10.0 %collective-permute-start.1 = (f32[28,16,128]{2,1,0:T(8,128)}, f32[28,16,128]{2,1,0:T(8,128)S(1)}, u32[]{:S(2)}, u32[]{:S(2)}) collective-permute-start(f32[28,16,128]{2,1,0:T(8,128)} %get-tuple-element.33.own_ref.refs_2_.refs_0_), channel_id=1, source_target_pairs={{16,0},{0,16},{17,1},{1,17},{18,2},{2,18},{19,3},{3,19},{20,4},{4,... | collective-permute-start | bytes 688136 | tf_op jit(solution)/shard_map/ppermute | solution.py:435
  5.5 10.1 %collective-permute-start.2 = (f32[28,16,128]{2,1,0:T(8,128)}, f32[28,16,128]{2,1,0:T(8,128)S(1)}, u32[]{:S(2)}, u32[]{:S(2)}) collective-permute-start(f32[28,16,128]{2,1,0:T(8,128)} %get-tuple-element.33.own_ref.refs_2_.refs_0_), channel_id=1, source_target_pairs={{0,0},{1,2},{2,1},{3,4},{4,3},{5,6},{6,5},{7,8},{8,7},{9,10},{10,9... | collective-permute-start | bytes 688136 | tf_op jit(solution)/shard_map/ppermute | solution.py:432
  8.8 9.0 %collective-permute-start.4 = (f32[20,16,128]{2,1,0:T(8,128)}, f32[20,16,128]{2,1,0:T(8,128)S(1)}, u32[]{:S(2)}, u32[]{:S(2)}) collective-permute-start(f32[20,16,128]{2,1,0:T(8,128)} %get-tuple-element.34.rest_ref.refs_3_.refs_1_), channel_id=1, source_target_pairs={{16,0},{0,16},{17,1},{1,17},{18,2},{2,18},{19,3},{3,19},{20,4},{4,... | collective-permute-start | bytes 491528 | tf_op jit(solution)/shard_map/ppermute | solution.py:435
  9.1 0.9 %copy-start = (f32[28,16,128]{2,1,0:T(8,128)S(1)}, f32[28,16,128]{2,1,0:T(8,128)}, u32[]{:S(2)}) copy-start(f32[28,16,128]{2,1,0:T(8,128)} %get-tuple-element.33.own_ref.refs_2_.refs_0_) | copy-start | bytes 688132
  10.0 0.9 %copy-start.2 = (f32[20,16,128]{2,1,0:T(8,128)S(1)}, f32[20,16,128]{2,1,0:T(8,128)}, u32[]{:S(2)}) copy-start(f32[20,16,128]{2,1,0:T(8,128)} %get-tuple-element.34.rest_ref.refs_3_.refs_1_) | copy-start | bytes 491524
  11.0 0.8 %copy-start.4 = (f32[8,1408]{1,0:T(8,128)S(1)}, f32[8,1408]{1,0:T(8,128)}, u32[]{:S(2)}) copy-start(f32[8,1408]{1,0:T(8,128)} %get-tuple-element.35.sphere_ref) | copy-start | bytes 135172
  11.8 7.7 %copy-start.3 = (f32[20,16,128]{2,1,0:T(8,128)S(1)}, f32[20,16,128]{2,1,0:T(8,128)}, u32[]{:S(2)}) copy-start(f32[20,16,128]{2,1,0:T(8,128)} %get-tuple-element.34.rest_ref.refs_3_.refs_1_) | copy-start | bytes 491524
  12.7 6.7 %copy-start.1 = (f32[28,16,128]{2,1,0:T(8,128)S(1)}, f32[28,16,128]{2,1,0:T(8,128)}, u32[]{:S(2)}) copy-start(f32[28,16,128]{2,1,0:T(8,128)} %get-tuple-element.33.own_ref.refs_2_.refs_0_) | copy-start | bytes 688132
  12.7 12.5 %collective-permute-start.8 = (f32[28,16,128]{2,1,0:T(8,128)S(1)}, f32[28,16,128]{2,1,0:T(8,128)S(1)}, u32[]{:S(2)}, u32[]{:S(2)}) collective-permute-start(f32[28,16,128]{2,1,0:T(8,128)S(1)} %collective-permute-done.1.refs_4_.own_ref), channel_id=1, source_target_pairs={{0,0},{1,2},{2,1},{3,4},{4,3},{5,6},{6,5},{7,8},{8,7},{9,10},{10,9... | collective-permute-start | bytes 688136 | tf_op jit(solution)/shard_map/ppermute | solution.py:570
  16.1 9.1 %collective-permute-start.7 = (f32[28,16,128]{2,1,0:T(8,128)S(1)}, f32[28,16,128]{2,1,0:T(8,128)S(1)}, u32[]{:S(2)}, u32[]{:S(2)}) collective-permute-start(f32[28,16,128]{2,1,0:T(8,128)S(1)} %collective-permute-done.1.refs_4_.own_ref), channel_id=1, source_target_pairs={{0,1},{1,0},{2,3},{3,2},{4,5},{5,4},{6,7},{7,6},{8,9},{9,8},{10,11... | collective-permute-start | bytes 688136 | tf_op jit(solution)/shard_map/ppermute | solution.py:579
  16.2 3.3 %collective-permute-start.3 = (f32[8,2048]{1,0:T(8,128)S(1)}, f32[8,2048]{1,0:T(8,128)S(1)}, u32[]{:S(2)}, u32[]{:S(2)}) collective-permute-start(f32[8,2048]{1,0:T(8,128)S(1)} %get-tuple-element.40.refs_0_.refs_8_), channel_id=1, source_target_pairs={{16,0},{0,16},{17,1},{1,17},{18,2},{2,18},{19,3},{3,19},{20,4},{4,... | collective-permute-start | bytes 196616 | tf_op jit(solution)/shard_map/ppermute | solution.py:435
  19.9 5.7 %collective-permute-start.5 = (f32[2,64,128]{2,1,0:T(8,128)S(1)}, f32[2,64,128]{2,1,0:T(8,128)S(1)}, u32[]{:S(2)}, u32[]{:S(2)}) collective-permute-start(f32[2,64,128]{2,1,0:T(8,128)S(1)} %get-tuple-element.43.sent_first), channel_id=1, source_target_pairs={{0,1},{1,0},{2,3},{3,2},{4,5},{5,4},{6,7},{7,6},{8,9},{9,8},{10,11... | collective-permute-start | bytes 196616 | tf_op jit(solution)/shard_map/ppermute | solution.py:432
  21.5 5.6 %collective-permute-start.6 = (f32[2,64,128]{2,1,0:T(8,128)S(1)}, f32[2,64,128]{2,1,0:T(8,128)S(1)}, u32[]{:S(2)}, u32[]{:S(2)}) collective-permute-start(f32[2,64,128]{2,1,0:T(8,128)S(1)} %get-tuple-element.44.sent_second), channel_id=1, source_target_pairs={{0,0},{1,2},{2,1},{3,4},{4,3},{5,6},{6,5},{7,8},{8,7},{9,10},{10,9... | collective-permute-start | bytes 196616 | tf_op jit(solution)/shard_map/ppermute | solution.py:432
  43.4 2.8 %collective-permute-start.9 = (f32[2,64,128]{2,1,0:T(8,128)S(1)}, f32[2,64,128]{2,1,0:T(8,128)S(1)}, u32[]{:S(2)}, u32[]{:S(2)}) collective-permute-start(f32[2,64,128]{2,1,0:T(8,128)S(1)} %get-tuple-element.56.sent_first), channel_id=1, source_target_pairs={{0,1},{1,0},{2,3},{3,2},{4,5},{5,4},{6,7},{7,6},{8,9},{9,8},{10,11... | collective-permute-start | bytes 196616 | tf_op jit(solution)/shard_map/ppermute | solution.py:432
  44.2 5.6 %collective-permute-start.10 = (f32[2,64,128]{2,1,0:T(8,128)S(1)}, f32[2,64,128]{2,1,0:T(8,128)S(1)}, u32[]{:S(2)}, u32[]{:S(2)}) collective-permute-start(f32[2,64,128]{2,1,0:T(8,128)S(1)} %get-tuple-element.57.sent_second), channel_id=1, source_target_pairs={{0,0},{1,2},{2,1},{3,4},{4,3},{5,6},{6,5},{7,8},{8,7},{9,10},{10,9... | collective-permute-start | bytes 196616 | tf_op jit(solution)/shard_map/ppermute | solution.py:432
